TPU v7x, 32 devices: a whole 2x2x4 slice. The times are simulated.
32 devices in a mesh: dp: 8 (over y, x, core), graph: 4 (over z).
Axes of the slice: x: 2, y: 2, z: 4, core: 2. Of those that a mesh axis runs over, the one named last changes fastest.
Arguments:
- nodes: bfloat16 [8, 64, 6272], P('dp', 'graph'), may hold values from -6 to 6
- sources: int32 [8, 2048], P('dp', 'graph'), may hold values from 0 to 63
- targets: int32 [8, 2048], P('dp', 'graph'), may hold values from 0 to 63
- edge_counts: int32 [8, 4], P('dp', 'graph'), may hold values from 128 to 512, as said below
- wigner: bfloat16 [8, 29, 49, 2048], P('dp', None, None, 'graph'), as said below
- radial: bfloat16 [8, 2048, 128], P('dp', 'graph'), may hold values from 0.5 to 1.5
- cotangent: bfloat16 [8, 64, 6272], P('dp', 'graph'), may hold values from -6 to 6
- w_zero: bfloat16 [896, 896], replicated, may hold values from -0.1875 to 0.1875
- w_one: bfloat16 [2, 768, 768], replicated, may hold values from -0.15625 to 0.15625
- w_two: bfloat16 [2, 640, 640], replicated, may hold values from -0.15625 to 0.15625
- w_gate: bfloat16 [128, 128], replicated, may hold values from -0.5 to 0.5
Outputs:
- aggregated: bfloat16 [8, 64, 6272], P('dp', 'graph')
- grad_nodes: bfloat16 [8, 64, 6272], P('dp', 'graph')
- grad_zero: float32 [896, 896], replicated
- grad_one: float32 [2, 768, 768], replicated
- grad_two: float32 [2, 640, 640], replicated
- grad_gate: float32 [128, 128], replicated
Inputs may be any that keep to these rules, and one draw needn't show every extreme that they name: `edge_counts`: one shard of each batch holds 512 live slots; live slots come first in each shard. `wigner`: for each edge, entry (k, j) is zero unless kept coefficient k and coefficient j have the same degree.
All inputs are finite; a program needn't handle non-finite values.
Results may differ from a plain program's by a relative error of at most 0.013.
Values may be sent and summed in bfloat16 or wider, within the bound.
No kernel may reach another device: no remote copies, remote signals or barrier semaphores. Data moves between devices by JAX's collectives and lax.ppermute only.
A program may use at most 128 MiB of HBM per device.

v0:
```python
import jax
import jax.numpy as jnp
from jax import lax
from jax.sharding import PartitionSpec as P


def product(left, right):
    return jnp.dot(left, right, preferred_element_type=jnp.float32)


def product_left(left, right):
    return lax.dot_general(
        left, right, (((0,), (0,)), ((), ())), preferred_element_type=jnp.float32
    )


def product_right(left, right):
    return lax.dot_general(
        left, right, (((1,), (1,)), ((), ())), preferred_element_type=jnp.float32
    )


def split_kept(values):
    rows = values.shape[0]
    bounds = ((0, 7), (7, 13), (13, 19), (19, 24), (24, 29))
    return tuple((values[:, lower:upper, :].reshape(rows, -1) for lower, upper in bounds))


def edge_forward(gathered, rotation, radial_rows, valid, w_zero, w_one, w_two, w_gate):
    rows = gathered.shape[0]
    width = w_gate.shape[0]
    turned = jnp.einsum("kje,ejc->ekc", rotation, gathered, preferred_element_type=jnp.float32)
    rotated = (turned * radial_rows.astype(jnp.float32)[:, None, :]).astype(jnp.bfloat16)
    zero_part, plus_one, minus_one, plus_two, minus_two = split_kept(rotated)
    mixed = jnp.concatenate(
        [
            product(zero_part, w_zero),
            product(plus_one, w_one[0]) - product(minus_one, w_one[1]),
            product(plus_one, w_one[1]) + product(minus_one, w_one[0]),
            product(plus_two, w_two[0]) - product(minus_two, w_two[1]),
            product(plus_two, w_two[1]) + product(minus_two, w_two[0]),
        ],
        axis=1,
    ).reshape(rows, -1, width)
    scalar = mixed[:, 0, :]
    scalar_low = scalar.astype(jnp.bfloat16)
    gate = jax.nn.sigmoid(product(scalar_low, w_gate))
    message = jnp.concatenate(
        [jax.nn.silu(scalar)[:, None, :], mixed[:, 1:, :] * gate[:, None, :]], axis=1
    )
    message = (message * valid[:, None, None].astype(jnp.float32)).astype(jnp.bfloat16)
    back = jnp.einsum("kje,ekc->ejc", rotation, message, preferred_element_type=jnp.float32).astype(
        jnp.bfloat16
    )
    return (back, (rotated, mixed, scalar_low, gate))


def edge_backward(upstream, rotation, radial_rows, saved, w_zero, w_one, w_two, w_gate):
    rotated, mixed, scalar_low, gate = saved
    rows = upstream.shape[0]
    width = w_gate.shape[0]
    incoming = jnp.einsum("kje,ejc->ekc", rotation, upstream, preferred_element_type=jnp.float32)
    scalar = mixed[:, 0, :]
    sigmoid_value = jax.nn.sigmoid(scalar)
    direct = incoming[:, 0, :] * sigmoid_value * (1.0 + scalar * (1.0 - sigmoid_value))
    gate_low = (jnp.sum(incoming[:, 1:, :] * mixed[:, 1:, :], axis=1) * gate * (1.0 - gate)).astype(
        jnp.bfloat16
    )
    head = direct + product_right(gate_low, w_gate)
    mixed_grad = jnp.concatenate(
        [head[:, None, :], incoming[:, 1:, :] * gate[:, None, :]], axis=1
    ).astype(jnp.bfloat16)
    zero_grad, plus_one_grad, minus_one_grad, plus_two_grad, minus_two_grad = split_kept(mixed_grad)
    zero_part, plus_one, minus_one, plus_two, minus_two = split_kept(rotated)
    grad_zero = product_left(zero_part, zero_grad)
    grad_one = jnp.stack(
        [
            product_left(plus_one, plus_one_grad) + product_left(minus_one, minus_one_grad),
            product_left(plus_one, minus_one_grad) - product_left(minus_one, plus_one_grad),
        ]
    )
    grad_two = jnp.stack(
        [
            product_left(plus_two, plus_two_grad) + product_left(minus_two, minus_two_grad),
            product_left(plus_two, minus_two_grad) - product_left(minus_two, plus_two_grad),
        ]
    )
    grad_gate = product_left(scalar_low, gate_low)
    backward_parts = jnp.concatenate(
        [
            product_right(zero_grad, w_zero),
            product_right(plus_one_grad, w_one[0]) + product_right(minus_one_grad, w_one[1]),
            product_right(minus_one_grad, w_one[0]) - product_right(plus_one_grad, w_one[1]),
            product_right(plus_two_grad, w_two[0]) + product_right(minus_two_grad, w_two[1]),
            product_right(minus_two_grad, w_two[0]) - product_right(plus_two_grad, w_two[1]),
        ],
        axis=1,
    ).reshape(rows, -1, width)
    rotated_grad = (backward_parts * radial_rows.astype(jnp.float32)[:, None, :]).astype(
        jnp.bfloat16
    )
    source_grad = jnp.einsum(
        "kje,ekc->ejc", rotation, rotated_grad, preferred_element_type=jnp.float32
    ).astype(jnp.bfloat16)
    return (source_grad, (grad_zero, grad_one, grad_two, grad_gate))


def selector(index_row, piece):
    columns = jnp.arange(piece.shape[0], dtype=jnp.int32)
    hits = (index_row[:, None] == columns[None, :]).astype(jnp.bfloat16)
    return jnp.dot(hits, piece, preferred_element_type=jnp.float32)


def spreader(index_row, values, count_rows):
    owners = jnp.arange(count_rows, dtype=jnp.int32)
    hits = (owners[:, None] == index_row[None, :]).astype(jnp.bfloat16)
    return jnp.dot(hits, values, preferred_element_type=jnp.float32)


def per_device(
    nodes, sources, targets, edge_counts, wigner, radial, cotangent, w_zero, w_one, w_two, w_gate
):
    node_rows = nodes[0]
    source_ids = sources[0]
    target_ids = targets[0]
    live_edges = edge_counts[0, 0]
    rotation = wigner[0]
    radial_rows = radial[0]
    upstream_rows = cotangent[0]
    edge_rows = source_ids.shape[0]
    width = w_gate.shape[0]
    node_count = node_rows.shape[0]
    valid = jnp.arange(edge_rows, dtype=jnp.int32) < live_edges
    gathered = selector(source_ids, lax.all_gather(node_rows, "graph", axis=0, tiled=True))
    gathered = gathered.astype(jnp.bfloat16).reshape(edge_rows, -1, width)
    back, saved = edge_forward(gathered, rotation, radial_rows, valid, w_zero, w_one, w_two, w_gate)
    summed = lax.psum_scatter(
        spreader(
            target_ids, back.reshape(edge_rows, -1), node_count * lax.axis_size("graph")
        ).astype(jnp.bfloat16),
        "graph",
        scatter_dimension=0,
        tiled=True,
    )
    upstream = selector(target_ids, lax.all_gather(upstream_rows, "graph", axis=0, tiled=True))
    upstream = (
        (upstream * valid[:, None].astype(jnp.float32))
        .astype(jnp.bfloat16)
        .reshape(edge_rows, -1, width)
    )
    source_grad, grads = edge_backward(
        upstream, rotation, radial_rows, saved, w_zero, w_one, w_two, w_gate
    )
    grad_rows = lax.psum_scatter(
        spreader(
            source_ids, source_grad.reshape(edge_rows, -1), node_count * lax.axis_size("graph")
        ).astype(jnp.bfloat16),
        "graph",
        scatter_dimension=0,
        tiled=True,
    )
    grad_zero, grad_one, grad_two, grad_gate = lax.psum(
        (grads[0], grads[1], grads[2], grads[3]), ("dp", "graph")
    )
    return (summed[None], grad_rows[None], grad_zero, grad_one, grad_two, grad_gate)


def solution(mesh):
    in_specs = (
        P("dp", "graph", None),
        P("dp", "graph"),
        P("dp", "graph"),
        P("dp", "graph"),
        P("dp", None, None, "graph"),
        P("dp", "graph", None),
        P("dp", "graph", None),
        P(),
        P(),
        P(),
        P(),
    )
    out_specs = (P("dp", "graph", None), P("dp", "graph", None), P(), P(), P(), P())
    return jax.shard_map(
        per_device, mesh=mesh, in_specs=in_specs, out_specs=out_specs, check_vma=False
    )
```

profile of v0, /device:TPU:0, one launch (start us, length us, event | category | flops | bytes accessed | tf_op | source)
XLA Modules:
  0.0 585.7 jit_solution(10862822458454821019)
XLA Ops:
  8.1 8.5 %copy.28 = bf16[29,49,512]{1,0,2:T(8,128)(2,1)} copy(bf16[29,49,512]{2,0,1:T(8,128)(2,1)} %bitcast.227) | data formatting | bytes 2910208 | tf_op jit(solution)/shard_map/squeeze | solution.py:127
  16.6 21.5 %all-gather = bf16[1,64,6272]{2,1,0:T(8,128)(2,1)S(1)} all-gather(bf16[1,16,6272]{2,1,0:T(8,128)(2,1)S(1)} %copy-done.43), channel_id=2, replica_groups=mesh['dp'=8,'graph'=4] {'graph'}, dimensions={1}, use_global_device_ids=true | all-gather | bytes 1003520 | tf_op jit(solution)/shard_map/all_gather | solution.py:134
  42.7 9.4 %copy.26 = bf16[512,6272]{0,1:T(8,128)(2,1)} copy(bf16[512,6272]{1,0:T(8,128)(2,1)} %convolution_convert_fusion) | data formatting | bytes 12845056 | tf_op jit(solution)/shard_map/convert_element_type | solution.py:135
  52.1 10.8 %copy.27 = bf16[512,49,128]{2,1,0:T(8,128)(2,1)} copy(bf16[512,49,128]{0,2,1:T(8,128)(2,1)} %bitcast.189) | data formatting | bytes 12845056 | tf_op jit(solution)/shard_map/reshape | solution.py:135
  62.8 8.4 %fusion.1 = bf16[512,29,128]{2,1,0:T(8,128)(2,1)} fusion(f32[512,128]{1,0:T(8,128)S(1)} %bitcast_convert_fusion.1, bf16[512,49,128]{2,1,0:T(8,128)(2,1)} %copy.27, bf16[29,49,512]{1,0,2:T(8,128)(2,1)} %copy.28), kind=kOutput, calls=%fused_computation.14 | convolution fusion | flops 190054400 | bytes 11940864 | tf_op jit(solution)/shard_map/kje,ejc->ekc/dot_general | solution.py:32
  107.9 8.8 %copy.34 = f32[512,3712]{0,1:T(8,128)} copy(f32[512,3712]{1,0:T(8,128)} %fusion.5) | data formatting | bytes 15204352 | tf_op jit(solution)/shard_map/concatenate | solution.py:35
  116.7 7.5 %slice.102 = f32[512,28,128]{0,2,1:T(8,128)} slice(f32[512,29,128]{0,2,1:T(8,128)} %bitcast.184), slice={[0:512], [1:29], [0:128]} | slice | bytes 14680064 | tf_op jit(solution)/shard_map/slice | solution.py:49
  125.2 8.4 %copy.57 = f32[512,28,128]{2,0,1:T(8,128)} copy(f32[512,28,128]{0,2,1:T(8,128)} %slice.102) | data formatting | bytes 14680064
  134.3 17.9 %all-gather.1 = bf16[1,64,6272]{2,1,0:T(8,128)(2,1)S(1)} all-gather(bf16[1,16,6272]{2,1,0:T(8,128)(2,1)S(1)} %copy-done.44), channel_id=3, replica_groups=mesh['dp'=8,'graph'=4] {'graph'}, dimensions={1}, use_global_device_ids=true | all-gather | bytes 1003520 | tf_op jit(solution)/shard_map/all_gather | solution.py:145
  156.7 9.5 %copy.40 = bf16[512,6272]{0,1:T(8,128)(2,1)} copy(bf16[512,6272]{1,0:T(8,128)(2,1)} %multiply_convert_fusion) | data formatting | bytes 12845056 | tf_op jit(solution)/shard_map/convert_element_type | solution.py:148
  166.3 10.8 %copy.41 = bf16[512,49,128]{2,1,0:T(8,128)(2,1)} copy(bf16[512,49,128]{0,2,1:T(8,128)(2,1)} %bitcast.190) | data formatting | bytes 12845056 | tf_op jit(solution)/shard_map/reshape | solution.py:149
  177.1 9.8 %fusion.77 = f32[512,128,29]{1,2,0:T(8,128)} fusion(bf16[512,49,128]{2,1,0:T(8,128)(2,1)} %copy.41, bf16[29,49,512]{1,0,2:T(8,128)(2,1)} %copy.28), kind=kOutput, calls=%fused_computation.117 | convolution fusion | flops 186253312 | bytes 15479808 | tf_op jit(solution)/shard_map/kje,ejc->ekc/dot_general | solution.py:62
  186.9 10.8 %copy.61 = f32[512,128,29]{1,0,2:T(8,128)} copy(f32[512,128,29]{1,2,0:T(8,128)} %fusion.77) | data formatting | bytes 15204352 | tf_op jit(solution)/shard_map/kje,ejc->ekc/dot_general | solution.py:62
  198.1 8.7 %multiply_reduce_fusion = (f32[512,128]{1,0:T(8,128)}, bf16[512,28,128]{2,0,1:T(8,128)(2,1)}, f32[512,28,128]{2,0,1:T(8,128)S(1)}) fusion(f32[512,28,128]{2,0,1:T(8,128)} %copy.57, f32[512,29,128]{2,0,1:T(8,128)} %bitcast.187, f32[512,128]{1,0:T(8,128)S(1)} %fusion.21), kind=kLoop, calls=%fused_computation.11 | loop fusion | flops 9109504 | bytes 26214400 | tf_op jit(solution)/shard_map/reduce_sum | solution.py:66
  210.4 9.1 %convert_bitcast_fusion.1 = bf16[512,49,128]{2,1,0:T(8,128)(2,1)} fusion(bf16[29,49,512]{1,0,2:T(8,128)(2,1)S(1)} %copy-done.1, bf16[512,29,128]{2,0,1:T(8,128)(2,1)} %fusion), kind=kOutput, calls=%fused_computation.12 | convolution fusion | flops 189464576 | bytes 11678720 | tf_op jit(solution)/shard_map/kje,ekc->ejc/dot_general | solution.py:52
  219.5 12.2 %copy.39 = bf16[512,49,128]{0,2,1:T(8,128)(2,1)} copy(bf16[512,49,128]{2,1,0:T(8,128)(2,1)} %convert_bitcast_fusion.1) | data formatting | bytes 12845056 | tf_op jit(solution)/shard_map/convert_element_type | solution.py:52
  280.0 8.8 %copy.50 = f32[512,3712]{0,1:T(8,128)} copy(f32[512,3712]{1,0:T(8,128)} %fusion.3) | data formatting | bytes 15204352 | tf_op jit(solution)/shard_map/concatenate | solution.py:89
  288.8 6.2 %multiply_convert_fusion.2 = bf16[512,29,128]{0,2,1:T(8,128)(2,1)} fusion(f32[512,29,128]{0,2,1:T(8,128)} %bitcast.186, f32[512,128]{0,1:T(8,128)S(1)} %copy-done.42), kind=kLoop, calls=%fused_computation.8 | loop fusion | flops 3801088 | bytes 11665408 | tf_op jit(solution)/shard_map/convert_element_type | solution.py:99
  295.0 8.0 %copy.52 = bf16[512,29,128]{2,1,0:T(8,128)(2,1)} copy(bf16[512,29,128]{0,2,1:T(8,128)(2,1)} %multiply_convert_fusion.2) | data formatting | bytes 7602176 | tf_op jit(solution)/shard_map/convert_element_type | solution.py:99
  303.0 10.5 %convert_bitcast_fusion = bf16[512,49,128]{2,1,0:T(8,128)(2,1)} fusion(bf16[512,29,128]{2,1,0:T(8,128)(2,1)} %copy.52, bf16[29,49,512]{1,0,2:T(8,128)(2,1)} %copy.28), kind=kOutput, calls=%fused_computation.9 | convolution fusion | flops 189464576 | bytes 11678720 | tf_op jit(solution)/shard_map/kje,ekc->ejc/dot_general | solution.py:102
  313.5 12.3 %copy.54 = bf16[512,49,128]{0,2,1:T(8,128)(2,1)} copy(bf16[512,49,128]{2,1,0:T(8,128)(2,1)} %convert_bitcast_fusion) | data formatting | bytes 12845056 | tf_op jit(solution)/shard_map/convert_element_type | solution.py:104
  325.7 5.8 convolution_convert_fusion.1
  347.8 7.3 %reduce-scatter.5.cloned.1.call-done = bf16[16,6272]{1,0:T(8,128)(2,1)} async-done(((bf16[64,6272]{1,0:T(8,128)(2,1)}), bf16[16,6272]{1,0:T(8,128)(2,1)}) %reduce-scatter.5.cloned.1.call-update) | async-done | bytes 200720 | tf_op jit(solution)/shard_map/reduce_scatter | solution.py:154
  355.1 213.0 %all-reduce.3.cloned.1.call-done = (f32[896,896]{1,0:T(8,128)}, f32[2,768,768]{2,1,0:T(8,128)}, f32[2,640,640]{2,1,0:T(8,128)}, f32[128,128]{1,0:T(8,128)}) async-done(((f32[896,896]{1,0:T(8,128)}, f32[2,768,768]{2,1,0:T(8,128)}, f32[2,640,640]{2,1,0:T(8,128)}, f32[128,128]{1,0:T(8,128)}), (f32[896,896]{1,0:T(8,128)}, f32[2,768,768]{2,1,0:T(8,128)}, f32[2,640,640]{2,1,0:T(8,128)}, ...) | async-done | bytes 11272208 | tf_op jit(solution)/shard_map/psum | solution.py:162
  (173 shorter events, 124.9 us)
Async XLA Ops:
  8.0 87.9 %copy-start = (bf16[896,896]{1,0:T(8,128)(2,1)S(1)}, bf16[896,896]{1,0:T(8,128)(2,1)}, u32[]{:S(2)}) copy-start(bf16[896,896]{1,0:T(8,128)(2,1)} %param.18) | copy-start | bytes 4816900
  8.0 8.6 %copy-start.45 = (bf16[1,512,128]{2,1,0:T(8,128)(2,1)S(1)}, bf16[1,512,128]{2,1,0:T(8,128)(2,1)}, u32[]{:S(2)}) copy-start(bf16[1,512,128]{2,1,0:T(8,128)(2,1)} %param.16) | copy-start | bytes 393220
  8.0 8.6 %copy-start.43 = (bf16[1,16,6272]{2,1,0:T(8,128)(2,1)S(1)}, bf16[1,16,6272]{2,1,0:T(8,128)(2,1)}, u32[]{:S(2)}) copy-start(bf16[1,16,6272]{2,1,0:T(8,128)(2,1)} %param.11) | copy-start | bytes 602116
  8.0 339.8 %reduce-scatter.3.cloned.1.call-start = ((), (), s32[]{:S(2)}) async-start(), calls=%async_computation.2 | async-start | bytes 1003520 | tf_op jit(solution)/shard_map/reduce_scatter | solution.py:137
  8.1 30.0 %copy-start.47 = (s32[1,512]{1,0:T(1,128)S(1)}, s32[1,512]{1,0:T(1,128)}, u32[]{:S(2)}) copy-start(s32[1,512]{1,0:T(1,128)} %param.12) | copy-start | bytes 6148
  16.6 46.2 %copy-start.28 = (f32[512,128]{1,0:T(8,128)}, f32[512,128]{1,0:T(8,128)S(1)}, u32[]{:S(2)}) copy-start(f32[512,128]{1,0:T(8,128)S(1)} %bitcast_convert_fusion.1) | copy-start | bytes 786436
  75.8 5.5 copy-start.18
  75.8 5.5 copy-start.3
  83.0 7.9 %slice-start = ((bf16[512,29,128]{2,1,0:T(8,128)(2,1)}), bf16[512,7,128]{2,1,0:T(8,128)(2,1)S(1)}, s32[]{:S(2)}) async-start(bf16[512,29,128]{2,1,0:T(8,128)(2,1)} %fusion.1), calls=%async_computation.5 | async-start | bytes 2097152 | tf_op jit(solution)/shard_map/slice | solution.py:26
  84.6 7.7 %copy-start.20 = (bf16[512,5,128]{0,2,1:T(8,128)(2,1)}, bf16[512,5,128]{0,2,1:T(8,128)(2,1)S(1)}, u32[]{:S(2)}) copy-start(bf16[512,5,128]{0,2,1:T(8,128)(2,1)S(1)} %copy.32) | copy-start | bytes 1966084
  95.9 10.1 %copy-start.4 = (bf16[512,5,128]{0,2,1:T(8,128)(2,1)}, bf16[512,5,128]{0,2,1:T(8,128)(2,1)S(1)}, u32[]{:S(2)}) copy-start(bf16[512,5,128]{0,2,1:T(8,128)(2,1)S(1)} %copy.33) | copy-start | bytes 1966084
  125.2 9.1 %copy-start.44 = (bf16[1,16,6272]{2,1,0:T(8,128)(2,1)S(1)}, bf16[1,16,6272]{2,1,0:T(8,128)(2,1)}, u32[]{:S(2)}) copy-start(bf16[1,16,6272]{2,1,0:T(8,128)(2,1)} %param.17) | copy-start | bytes 602116
  125.2 27.0 %copy-start.46 = (s32[1,512]{1,0:T(1,128)S(1)}, s32[1,512]{1,0:T(1,128)}, u32[]{:S(2)}) copy-start(s32[1,512]{1,0:T(1,128)} %param.13) | copy-start | bytes 6148
  186.9 11.0 %copy-start.49 = (bf16[128,128]{1,0:T(8,128)(2,1)S(1)}, bf16[128,128]{1,0:T(8,128)(2,1)}, u32[]{:S(2)}) copy-start(bf16[128,128]{1,0:T(8,128)(2,1)} %param.21) | copy-start | bytes 98308
  197.8 9.0 %copy-start.30 = (f32[512,1,128]{2,0,1:T(8,128)}, f32[512,1,128]{2,0,1:T(8,128)S(1)}, u32[]{:S(2)}) copy-start(f32[512,1,128]{2,0,1:T(8,128)S(1)} %copy.56) | copy-start | bytes 786436
  198.1 8.7 %copy-start.39 = (f32[512,128]{1,0:T(8,128)}, f32[512,128]{1,0:T(8,128)S(1)}, u32[]{:S(2)}) copy-start(f32[512,128]{1,0:T(8,128)S(1)} %fusion.21) | copy-start | bytes 786436
  237.5 117.6 %reduce-scatter.5.cloned.1.call-start = ((), (), s32[]{:S(2)}) async-start(), calls=%async_computation.3 | async-start | bytes 1003520 | tf_op jit(solution)/shard_map/reduce_scatter | solution.py:154
  237.6 6.5 %copy-start.2 = (bf16[512,28,128]{2,0,1:T(8,128)(2,1)S(1)}, bf16[512,28,128]{2,0,1:T(8,128)(2,1)}, u32[]{:S(2)}) copy-start(bf16[512,28,128]{2,0,1:T(8,128)(2,1)} %get-tuple-element.11) | copy-start | bytes 11010052
  250.9 9.3 %copy-start.10 = (bf16[512,6,128]{0,2,1:T(8,128)(2,1)}, bf16[512,6,128]{0,2,1:T(8,128)(2,1)S(1)}, u32[]{:S(2)}) copy-start(bf16[512,6,128]{0,2,1:T(8,128)(2,1)S(1)} %copy.46) | copy-start | bytes 2359300
  266.8 5.9 %copy-start.11 = (bf16[512,6,128]{0,2,1:T(8,128)(2,1)S(1)}, bf16[512,6,128]{0,2,1:T(8,128)(2,1)}, u32[]{:S(2)}) copy-start(bf16[512,6,128]{0,2,1:T(8,128)(2,1)} %copy-done.10) | copy-start | bytes 2359300
  266.8 5.9 %copy-start.17 = (bf16[2,768,768]{2,1,0:T(8,128)(2,1)S(1)}, bf16[2,768,768]{2,1,0:T(8,128)(2,1)}, u32[]{:S(2)}) copy-start(bf16[2,768,768]{2,1,0:T(8,128)(2,1)} %param.19) | copy-start | bytes 7077892
  266.8 5.9 %copy-start.36 = (f32[512,768]{1,0:T(8,128)S(1)}, f32[512,768]{1,0:T(8,128)}, u32[]{:S(2)}) copy-start(f32[512,768]{1,0:T(8,128)} %fusion.12) | copy-start | bytes 4718596
  280.0 8.8 %copy-start.42 = (f32[512,128]{0,1:T(8,128)S(1)}, f32[512,128]{0,1:T(8,128)}, u32[]{:S(2)}) copy-start(f32[512,128]{0,1:T(8,128)} %copy.51) | copy-start | bytes 786436
  331.5 236.6 %all-reduce.3.cloned.1.call-start = ((), (), s32[]{:S(2)}) async-start(), calls=%async_computation.4 | async-start | bytes 22544384 | tf_op jit(solution)/shard_map/psum | solution.py:162
  (31 other events, 94.8 us)
Sparse Core Ops, SparseCore 0:
  237.6 23.4 reduce-scatter.2
  331.7 23.4 reduce-scatter.4
Sparse Core Ops, SparseCore 1:
  347.9 220.2 all-reduce.2
where the time goes:
time: 597 us; the launch traced here: 586 us
  waiting for transfers between devices  220 us (37%)
  local copies, waits for them, and re-layouts  166 us (28%)
  matrix products  119 us (20%)
  blocking collectives  39.4 us (7%)
  other arithmetic  23.2 us (4%)
  between operations  16.9 us (3%)
    psum x1, waiting for transfers between devices, per_device(): lax.psum((grads[0], grads[1], grads[2], grads[3]), ('dp', 'graph'))  213 us
    slice x16, local copies, waits for them, and re-layouts, split_kept(): values[:, lower:upper, :].reshape(rows, -1)  27.1 us
    dot_general x10, matrix products, product_right(): lax.dot_general(left, right, (((1,), (1,)), ((), ())), preferred_element_...  25.6 us
    dot_general x10, matrix products, product(): return jnp.dot(left, right, preferred_element_type=jnp.float32)  23.9 us
    all_gather x1, blocking collectives, per_device(): lax.all_gather(node_rows, 'graph', axis=0, tiled=True)  21.5 us
    unnamed x108, local copies, waits for them, and re-layouts  20.2 us
    all_gather x1, blocking collectives, per_device(): lax.all_gather(upstream_rows, 'graph', axis=0, tiled=True)  17.9 us
    convert_element_type x1, local copies, waits for them, and re-layouts, edge_backward(): source_grad = jnp.einsum('kje,ekc->ejc', rotation, rotated_grad, preferre...  12.3 us
  transfers between devices with their start and end apart: 3, of which 2 were waited for; matrix products, arithmetic and copies ran while one was open for 19% of the time, Pallas kernels for 0%

commit v1 on v0

v1 whole, which is shorter than its diff:
```python
import functools
import math

import jax
import jax.numpy as jnp
from jax import lax
from jax.experimental import pallas as pl
from jax.experimental.pallas import tpu as pltpu
from jax.sharding import PartitionSpec as P

F32 = jnp.float32
BF16 = jnp.bfloat16
VMEM_LIMIT = 48 * 1024 * 1024


def dot_nn(left, right):
    return jnp.dot(left, right, preferred_element_type=F32)


def dot_nt(left, right):
    return lax.dot_general(left, right, (((1,), (1,)), ((), ())), preferred_element_type=F32)


def dot_tn(left, right):
    return lax.dot_general(left, right, (((0,), (0,)), ((), ())), preferred_element_type=F32)


def kept_rows(degree, sizes):
    zero, one, two = sizes
    rows = [degree]
    if degree >= 1:
        rows += [zero + degree - 1, zero + one + degree - 1]
    if degree >= 2:
        rows += [zero + 2 * one + degree - 2, zero + 2 * one + two + degree - 2]
    return rows


def group_of(row, sizes):
    zero, one, two = sizes
    if row < zero:
        return 0, row
    if row < zero + 2 * one:
        return 1, row - zero
    return 2, row - zero - 2 * one


def widen(wigner_ref, wide_ref):
    for j in range(wigner_ref.shape[0]):
        wide_ref[j] = wigner_ref[j].astype(F32)


def fill_spread(degree, sizes, hits, wide_ref, spread_ref):
    nodes, edges = hits.shape
    for j in range(2 * degree + 1):
        for place, k in enumerate(kept_rows(degree, sizes)):
            row = wide_ref[degree * degree + j, k : k + 1, :]
            row = jnp.broadcast_to(row, (16, edges)).astype(BF16)
            for part in range(nodes // 16):
                at = j * nodes + part * 16
                spread_ref[at : at + 16, place * edges : (place + 1) * edges] = (
                    hits[part * 16 : (part + 1) * 16] * row
                )


def turn(pieces, sizes, hits, wide_ref, spreads, stacked, degree, width):
    nodes, edges = hits.shape
    orders = 2 * degree + 1
    spread_ref = spreads[degree % 2]
    fill_spread(degree, sizes, hits, wide_ref, spread_ref)
    for j in range(orders):
        column = (degree * degree + j) * width
        at = j * nodes
        for piece in pieces:
            stacked[at : at + piece.shape[0], :] = piece[:, column : column + width]
            at += piece.shape[0]
    count = len(kept_rows(degree, sizes))
    return dot_tn(stacked[0 : orders * nodes, :], spread_ref[0 : orders * nodes, 0 : count * edges])


def nodes_kernel(
    sizes, ids, sources, wigner, radial, first, gating, *refs
):
    pieces, (x_zero, x_one, x_two, scalar, gate), (wide, even, odd, stacked) = (
        refs[:-9],
        refs[-9:-4],
        refs[-4:],
    )
    width = gating.shape[0]
    edges = sources.shape[1]
    widen(wigner, wide)
    hits = (ids[...] == sources[...]).astype(F32).astype(BF16)
    scale = radial[...].astype(F32).T
    outs = (x_zero, x_one, x_two)
    for degree in range(sizes[0]):
        turned = turn(pieces, sizes, hits, wide, (even, odd), stacked, degree, width)
        for place, k in enumerate(kept_rows(degree, sizes)):
            group, row = group_of(k, sizes)
            outs[group][row * width : (row + 1) * width, :] = (
                turned[:, place * edges : (place + 1) * edges] * scale
            ).astype(BF16)
    low = dot_tn(first[...], x_zero[...])
    scalar[...] = low
    gate[...] = jax.nn.sigmoid(dot_tn(gating[...], low.astype(BF16)))


def cotangent_kernel(sizes, live, ids, targets, wigner, gate, *refs):
    pieces, (g_zero, g_one, g_two, head), (wide, even, odd, stacked) = (
        refs[:-8],
        refs[-8:-4],
        refs[-4:],
    )
    width, edges = gate.shape
    widen(wigner, wide)
    slots = lax.broadcasted_iota(jnp.int32, (1, edges), 1)
    wanted = jnp.where(slots < live[0], targets[...], -1)
    hits = (ids[...] == wanted).astype(F32).astype(BF16)
    outs = (g_zero, g_one, g_two)
    for degree in range(sizes[0]):
        turned = turn(pieces, sizes, hits, wide, (even, odd), stacked, degree, width)
        for place, k in enumerate(kept_rows(degree, sizes)):
            group, row = group_of(k, sizes)
            value = turned[:, place * edges : (place + 1) * edges]
            if k == 0:
                head[...] = value
                g_zero[0:width, :] = jnp.zeros((width, edges), BF16)
            else:
                outs[group][row * width : (row + 1) * width, :] = (value * gate[...]).astype(BF16)


def place_rows(shift, out, block, flat, values):
    rows = values.shape[0]
    step = math.gcd(math.gcd(block, flat), rows) if flat else math.gcd(block, rows)
    for at in range(0, rows, step):
        start = pl.multiple_of(flat + at + shift[(flat + at) // block], 16)
        out[pl.ds(start, step), :] = values[at : at + step]


def take_rows(shift, source, block, flat, rows, store):
    step = math.gcd(math.gcd(block, flat), rows) if flat else math.gcd(block, rows)
    for at in range(0, rows, step):
        start = pl.multiple_of(flat + at + shift[(flat + at) // block], 16)
        store(at, step, source[pl.ds(start, step), :])


def pair_grad_kernel(width, block, shift, x, g, out, total):
    half = x.shape[0] // 2
    flat = 0
    for part in range(2):
        if part == 0:
            total[...] = dot_nt(x[:half], g[:half]) + dot_nt(x[half:], g[half:])
        else:
            total[...] = dot_nt(x[:half], g[half:]) - dot_nt(x[half:], g[:half])
        for column in range(0, half, width):
            place_rows(shift, out, block, flat, total[:, column : column + width].astype(BF16))
            flat += half
    if flat < out.shape[0]:
        place_rows(shift, out, block, flat, jnp.zeros((out.shape[0] - flat, width), BF16))


def zero_grad_kernel(width, block, shift, x, g, out, total):
    rows = x.shape[0]
    total[...] = dot_nt(x[...], g[width:])
    flat = 0
    for column in range(0, rows - width, width):
        place_rows(shift, out, block, flat, total[:, column : column + width].astype(BF16))
        flat += rows
    if flat < out.shape[0]:
        place_rows(shift, out, block, flat, jnp.zeros((out.shape[0] - flat, width), BF16))


def message_kernel(
    sizes, live, targets, wigner, x_zero, x_one, x_two, g_zero, g_one, g_two, scalar, gate, head,
    w_zero, w_one, w_two, gating, partial, g_first, late, wide, even, odd, message, mixed
):
    width, edges = gate.shape
    zero, one, two = sizes
    nodes = partial.shape[0]
    widen(wigner, wide)

    def settle(group, first_row, count, total):
        inputs = (g_zero, g_one, g_two)[group]
        base = (0, zero, zero + 2 * one)[group]
        for row in range(count):
            k = base + first_row + row
            if k == 0:
                v = scalar[...]
                value = v * jax.nn.sigmoid(v)
            else:
                raw = mixed[row * width : (row + 1) * width, :]
                at = (first_row + row) * width
                total = total + raw * inputs[at : at + width, :].astype(F32)
                value = raw * gate[...]
            for degree in range(zero):
                rows = kept_rows(degree, sizes)
                if k in rows:
                    place = rows.index(k)
                    message[degree, :, place * edges : (place + 1) * edges] = value.astype(BF16)
        return total

    total = jnp.zeros((width, edges), F32)
    mixed[0 : zero * width, :] = dot_nn(w_zero[...], x_zero[...])
    total = settle(0, 0, zero, total)
    for group, size, x, w in ((1, one, x_one, w_one), (2, two, x_two, w_two)):
        half = size * width
        mixed[0:half, :] = dot_nn(w[0], x[:half]) - dot_nn(w[1], x[half:])
        total = settle(group, 0, size, total)
        mixed[0:half, :] = dot_nn(w[1], x[:half]) + dot_nn(w[0], x[half:])
        total = settle(group, size, size, total)

    gates = gate[...]
    gate_low = (total * (1.0 - gates)).astype(BF16)
    v = scalar[...]
    s = jax.nn.sigmoid(v)
    first = (head[...] * s * (1.0 + v * (1.0 - s)) + dot_nn(gating[...], gate_low)).astype(BF16)
    g_first[...] = first
    late[0 : zero * width, :] = dot_nt(x_zero[...], first)
    late[zero * width : (zero + 1) * width, :] = dot_nt(v.astype(BF16), gate_low)

    slots = lax.broadcasted_iota(jnp.int32, (1, edges), 1)
    wanted = jnp.where(slots < live[0], targets[...], -1)
    hits = lax.broadcasted_iota(jnp.int32, (nodes, edges), 0) == wanted
    scatter(sizes, hits, wide, (even, odd), message, partial, width)


def scatter(sizes, hits, wide, spreads, values, partial, width):
    hits = hits.astype(F32).astype(BF16)
    nodes, edges = hits.shape
    for degree in range(sizes[0]):
        spread_ref = spreads[degree % 2]
        fill_spread(degree, sizes, hits, wide, spread_ref)
        lanes = len(kept_rows(degree, sizes)) * edges
        orders = 2 * degree + 1
        summed = dot_nt(
            spread_ref[0 : orders * nodes, 0:lanes], values[degree, :, 0:lanes]
        ).astype(BF16)
        for j in range(orders):
            column = (degree * degree + j) * width
            partial[:, column : column + width] = summed[j * nodes : (j + 1) * nodes]


def source_kernel(
    sizes, sources, wigner, radial, g_first, g_zero, g_one, g_two, w_zero, w_one, w_two,
    partial, wide, even, odd, values, moved
):
    zero, one, two = sizes
    width, edges = g_first.shape
    nodes = partial.shape[0]
    widen(wigner, wide)
    scale = radial[...].astype(F32).T

    def settle(base, count):
        for row in range(count):
            k = base + row
            value = moved[row * width : (row + 1) * width, :] * scale
            for degree in range(zero):
                rows = kept_rows(degree, sizes)
                if k in rows:
                    place = rows.index(k)
                    values[degree, :, place * edges : (place + 1) * edges] = value.astype(BF16)

    moved[0 : zero * width, :] = dot_nn(w_zero[:, :width], g_first[...]) + dot_nn(
        w_zero[:, width:], g_zero[width:]
    )
    settle(0, zero)
    base = zero
    for size, g, w in ((one, g_one, w_one), (two, g_two, w_two)):
        half = size * width
        moved[0:half, :] = dot_nn(w[0], g[:half]) + dot_nn(w[1], g[half:])
        settle(base, size)
        moved[0:half, :] = dot_nn(w[0], g[half:]) - dot_nn(w[1], g[:half])
        settle(base + size, size)
        base += 2 * size
    hits = lax.broadcasted_iota(jnp.int32, (nodes, edges), 0) == sources[...]
    scatter(sizes, hits, wide, (even, odd), values, partial, width)


def pair_finish_kernel(width, block, shift, source, out):
    half = out.shape[1]
    flat = 0
    for part in range(2):
        for column in range(0, half, width):

            def store(at, step, rows, part=part, column=column):
                out[part, at : at + step, column : column + width] = rows.astype(F32)

            take_rows(shift, source, block, flat, half, store)
            flat += half


def zero_finish_kernel(width, block, shift, source, first, out):
    rows = out.shape[0]
    out[:, 0:width] = first[0:rows, :]
    flat = 0
    for column in range(width, rows, width):

        def store(at, step, values, column=column):
            out[at : at + step, column : column + width] = values.astype(F32)

        take_rows(shift, source, block, flat, rows, store)
        flat += rows


SMEM = pl.BlockSpec(memory_space=pltpu.SMEM)
VMEM = pl.BlockSpec(memory_space=pltpu.VMEM)


def call(kernel, out_shape, args, scratch=(), smem=0, flops=0, moved=0):
    return pl.pallas_call(
        kernel,
        out_shape=out_shape,
        in_specs=[SMEM] * smem + [VMEM] * (len(args) - smem),
        out_specs=jax.tree.map(lambda _: VMEM, out_shape),
        scratch_shapes=list(scratch),
        compiler_params=pltpu.CompilerParams(vmem_limit_bytes=VMEM_LIMIT),
        cost_estimate=pl.CostEstimate(
            flops=int(flops), bytes_accessed=int(moved), transcendentals=0
        ),
    )(*args)


def shaped(shape, dtype):
    return jax.ShapeDtypeStruct(shape, dtype)


def exchange(value, axis, bit):
    count = lax.axis_size(axis)
    return lax.ppermute(value, axis, [(i, i ^ bit) for i in range(count)])


def bits_of(axis):
    count = lax.axis_size(axis)
    return [(axis, 1 << b) for b in range(count.bit_length() - 1)]


def relative_gather(shard):
    order = [0]
    held = [shard]
    for axis, bit in bits_of("graph")[::-1]:
        block = held[0] if len(held) == 1 else jnp.concatenate(held, axis=0)
        held = [block, exchange(block, axis, bit)]
        order = order + [o ^ bit for o in order]
    return held, order


def block_shift(stages, blocks, block):
    mine = jnp.int32(0)
    for axis, bit in stages:
        mine = 2 * mine + ((lax.axis_index(axis) & bit) != 0).astype(jnp.int32)
    at = jnp.arange(blocks, dtype=jnp.int32)
    return ((at ^ mine) - at) * block


def sum_rows(value, stages):
    for axis, bit in stages:
        half = value.shape[0] // 2
        other = exchange(value[half:], axis, bit)
        value = (value[:half].astype(F32) + other.astype(F32)).astype(BF16)
    for axis, bit in stages[::-1]:
        value = jnp.concatenate([value, exchange(value, axis, bit)], axis=0)
    return value


def per_device(
    nodes, sources, targets, edge_counts, wigner, radial, cotangent, w_zero, w_one, w_two, w_gate
):
    width = w_gate.shape[0]
    zero, one, two = w_zero.shape[0] // width, w_one.shape[1] // width, w_two.shape[1] // width
    sizes = (zero, one, two)
    shard = nodes.shape[1]
    node_count = shard * lax.axis_size("graph")
    edges = sources.shape[1]
    coefficients = wigner.shape[2]
    kept = wigner.shape[1]
    features = nodes.shape[2]
    live = edge_counts[0]
    rotation = jnp.transpose(wigner[0], (1, 0, 2))
    radial_rows = radial[0]

    node_blocks, order = relative_gather(nodes[0])
    upstream_blocks, _ = relative_gather(cotangent[0])
    ids = (jnp.array(order, jnp.int32) ^ lax.axis_index("graph"))[:, None] * shard
    ids = (ids + jnp.arange(shard, dtype=jnp.int32)[None, :]).reshape(node_count, 1)

    pairs = 2 * zero - 1
    spread = [
        pltpu.VMEM(((2 * d + 1) * node_count, 5 * edges), BF16) for d in (zero - 1, zero - 2)
    ]
    if zero % 2 == 0:
        spread = spread[::-1]
    wide = pltpu.VMEM((coefficients, kept, edges), F32)
    turning = [wide, *spread, pltpu.VMEM((pairs * node_count, width), BF16)]
    turn_cost = 2 * coefficients * 5 * node_count * width * edges
    edge_flops = 2 * edges * width * width * (zero * zero + 4 * one * one + 4 * two * two)
    rows = [zero * width, 2 * one * width, 2 * two * width]
    wide_rows = [shaped((r, edges), BF16) for r in rows]
    one_row = shaped((width, edges), F32)
    wigner_bytes = rotation.size * 2

    x_zero, x_one, x_two, scalar, gate = call(
        functools.partial(nodes_kernel, sizes),
        (*wide_rows, one_row, one_row),
        [ids, sources, rotation, radial_rows, w_zero[:, :width], w_gate, *node_blocks],
        turning,
        flops=turn_cost,
        moved=wigner_bytes + 2 * sum(rows) * edges,
    )
    g_zero, g_one, g_two, head = call(
        functools.partial(cotangent_kernel, sizes),
        (*wide_rows, one_row),
        [live, ids, targets, rotation, gate, *upstream_blocks],
        turning,
        smem=1,
        flops=turn_cost,
        moved=wigner_bytes + 2 * sum(rows) * edges,
    )

    dp_bits = bits_of("dp")
    forward = dp_bits + bits_of("graph")
    other_way = dp_bits[:1] + dp_bits[1:][::-1] + bits_of("graph")
    blocks = lax.axis_size("dp") * lax.axis_size("graph")

    def padded(count):
        return -(-count // (16 * blocks)) * 16

    def summed_pair(x, g, stages, size):
        side = size * width
        block = padded(2 * size * side)
        shift = block_shift(stages, blocks, block)
        partial = call(
            functools.partial(pair_grad_kernel, width, block),
            shaped((blocks * block, width), BF16),
            [shift, x, g],
            [pltpu.VMEM((side, side), F32)],
            smem=1,
            flops=8 * side * side * edges,
            moved=8 * side * side,
        )
        total = sum_rows(partial, stages)
        return call(
            functools.partial(pair_finish_kernel, width, block),
            shaped((2, side, side), F32),
            [shift, total],
            smem=1,
            moved=12 * side * side,
        )

    grad_two = summed_pair(x_two, g_two, forward, two)
    grad_one = summed_pair(x_one, g_one, other_way, one)

    side = zero * width
    zero_block = padded(side * (zero - 1))
    zero_shift = block_shift(forward, blocks, zero_block)
    zero_partial = call(
        functools.partial(zero_grad_kernel, width, zero_block),
        shaped((blocks * zero_block, width), BF16),
        [zero_shift, x_zero, g_zero],
        [pltpu.VMEM((side, side - width), F32)],
        smem=1,
        flops=2 * side * side * edges,
        moved=4 * side * side,
    )
    zero_total = sum_rows(zero_partial, forward)

    messages = pltpu.VMEM((zero, width, 5 * edges), BF16)
    products = pltpu.VMEM((zero * width, edges), F32)
    partial_shape = shaped((node_count, features), BF16)
    partial, g_first, late = call(
        functools.partial(message_kernel, sizes),
        (partial_shape, shaped((width, edges), BF16), shaped((side + width, width), F32)),
        [
            live, targets, rotation, x_zero, x_one, x_two, g_zero, g_one, g_two, scalar, gate, head,
            w_zero.T, jnp.swapaxes(w_one, 1, 2), jnp.swapaxes(w_two, 1, 2), w_gate,
        ],
        [wide, *spread, messages, products],
        smem=1,
        flops=edge_flops + turn_cost,
        moved=wigner_bytes + 4 * sum(rows) * edges,
    )
    summed = lax.psum_scatter(partial, "graph", scatter_dimension=0, tiled=True)
    late = lax.psum(late, ("dp", "graph"))
    grad_partial = call(
        functools.partial(source_kernel, sizes),
        partial_shape,
        [sources, rotation, radial_rows, g_first, g_zero, g_one, g_two, w_zero, w_one, w_two],
        [wide, *spread, messages, products],
        flops=edge_flops + turn_cost,
        moved=wigner_bytes + 2 * sum(rows) * edges,
    )
    grad_rows = lax.psum_scatter(grad_partial, "graph", scatter_dimension=0, tiled=True)
    grad_zero = call(
        functools.partial(zero_finish_kernel, width, zero_block),
        shaped((side, side), F32),
        [zero_shift, zero_total, late],
        smem=1,
        moved=6 * side * side,
    )
    return (summed[None], grad_rows[None], grad_zero, grad_one, grad_two, late[side:])


def solution(mesh):
    in_specs = (
        P("dp", "graph", None),
        P("dp", "graph"),
        P("dp", "graph"),
        P("dp", "graph"),
        P("dp", None, None, "graph"),
        P("dp", "graph", None),
        P("dp", "graph", None),
        P(),
        P(),
        P(),
        P(),
    )
    out_specs = (P("dp", "graph", None), P("dp", "graph", None), P(), P(), P(), P())
    return jax.shard_map(
        per_device, mesh=mesh, in_specs=in_specs, out_specs=out_specs, check_vma=False
    )
```

time: 597 us -> 264 us (0.44); the launches traced: 586 us -> 264 us
  waiting for transfers between devices: 220 us -> 97.3 us
  local copies, waits for them, and re-layouts: 166 us -> 43.7 us
  matrix products: 119 us -> 0 us
  Pallas kernels: 0 us -> 54 us
  starting transfers between devices: 0.12 us -> 40.8 us
  blocking collectives: 39.4 us -> 0 us
  other arithmetic: 23.2 us -> 11.1 us
    psum x1, waiting for transfers between devices: 213 us -> 25.9 us  [per_device(): late = lax.psum(late, ('dp', 'graph'))]
    dot_general x38 -> x0, matrix products: 119 us -> none  [the longest x10 25.6 us: product_right(): lax.dot_general(left, right, (((1,), (1,)), ((), ())), preferred_element_...]
    ppermute x0 -> x34, waiting for transfers between devices: none -> 71.4 us  [exchange(): return lax.ppermute(value, axis, [(i, i ^ bit) for i in range(count)])]
    pallas_call x0 -> x10, Pallas kernels: none -> 54 us  [call(): pl.pallas_call(kernel, out_shape=out_shape, in_specs=[SMEM] * smem + [VME...]
    convert_element_type x6 -> x0, local copies, waits for them, and re-layouts: 52.2 us -> none  [the longest x1 12.3 us: edge_backward(): source_grad = jnp.einsum('kje,ekc->ejc', rotation, rotated_grad, preferre...]
    ppermute x0 -> x34, starting transfers between devices: none -> 40.5 us  [exchange(): return lax.ppermute(value, axis, [(i, i ^ bit) for i in range(count)])]
    all_gather x2 -> x0, blocking collectives: 39.4 us -> none  [the longest x1 21.5 us: per_device(): lax.all_gather(node_rows, 'graph', axis=0, tiled=True)]
    slice x18 -> x17, local copies, waits for them, and re-layouts: 35.6 us -> 6.58 us  [the longest x15 4.08 us: sum_rows(): other = exchange(value[half:], axis, bit)]
  transfers between devices with their start and end apart: 3 -> 37, of which waited for: 2 -> 19; matrix products, arithmetic and copies ran while one was open for 19% -> 16% of each run, Pallas kernels for 0% -> 18%
where the time goes in v1:
time: 264 us
  waiting for transfers between devices  97.3 us (37%)
  Pallas kernels  54 us (20%)
  local copies, waits for them, and re-layouts  43.7 us (17%)
  starting transfers between devices  40.8 us (15%)
  between operations  16.7 us (6%)
  other arithmetic  11.1 us (4%)
    ppermute x34, waiting for transfers between devices, exchange(): return lax.ppermute(value, axis, [(i, i ^ bit) for i in range(count)])  71.4 us
    pallas_call x10, Pallas kernels, call(): pl.pallas_call(kernel, out_shape=out_shape, in_specs=[SMEM] * smem + [VME...  54 us
    ppermute x34, starting transfers between devices, exchange(): return lax.ppermute(value, axis, [(i, i ^ bit) for i in range(count)])  40.5 us
    unnamed x79, local copies, waits for them, and re-layouts  29.8 us
    psum x1, waiting for transfers between devices, per_device(): late = lax.psum(late, ('dp', 'graph'))  25.9 us
    concatenate x6, local copies, waits for them, and re-layouts, sum_rows(): value = jnp.concatenate([value, exchange(value, axis, bit)], axis=0)  7.21 us
    convert_element_type x12, other arithmetic, sum_rows(): value = (value[:half].astype(F32) + other.astype(F32)).astype(BF16)  6.31 us
  transfers between devices with their start and end apart: 37, of which 19 were waited for; matrix products, arithmetic and copies ran while one was open for 16% of the time, Pallas kernels for 18%

profile of v1, /device:TPU:0, one launch (start us, length us, event | category | flops | bytes accessed | tf_op | source)
XLA Modules:
  0.0 263.5 jit_solution(799367416435930992)
XLA Ops:
  8.1 4.1 %collective-permute-start = (bf16[16,6272]{1,0:T(8,128)(2,1)}, bf16[16,6272]{1,0:T(8,128)(2,1)S(1)}, u32[]{:S(2)}, u32[]{:S(2)}) collective-permute-start(bf16[16,6272]{1,0:T(8,128)(2,1)} %bitcast.19), channel_id=1, source_target_pairs={{0,2},{1,3},{2,0},{3,1},{4,6},{5,7},{6,4},{7,5},{8,10},{9,11},{10,... | collective-permute-start | bytes 602120 | tf_op jit(solution)/shard_map/ppermute | solution.py:327
  12.9 13.9 %collective-permute-done = bf16[16,6272]{1,0:T(8,128)(2,1)S(1)} collective-permute-done((bf16[16,6272]{1,0:T(8,128)(2,1)}, bf16[16,6272]{1,0:T(8,128)(2,1)S(1)}, u32[]{:S(2)}, u32[]{:S(2)}) %collective-permute-start) | collective-permute-done | bytes 200736 | tf_op jit(solution)/shard_map/ppermute | solution.py:327
  33.9 6.1 %collective-permute-done.1.refs_1_ = bf16[32,6272]{1,0:T(8,128)(2,1)S(1)} collective-permute-done((bf16[32,6272]{1,0:T(8,128)(2,1)S(1)}, bf16[32,6272]{1,0:T(8,128)(2,1)S(1)}, u32[]{:S(2)}, u32[]{:S(2)}) %collective-permute-start.1) | collective-permute-done | bytes 401440 | tf_op jit(solution)/shard_map/ppermute | solution.py:327
  40.1 4.6 %shard_map.163 = (bf16[896,512]{1,0:T(8,128)(2,1)S(1)}, bf16[1536,512]{1,0:T(8,128)(2,1)S(1)}, bf16[1280,512]{1,0:T(8,128)(2,1)S(1)}, f32[128,512]{1,0:T(8,128)S(1)}, f32[128,512]{1,0:T(8,128)S(1)}) custom-call(s32[64,1]{1,0:T(8,128)S(1)} %add.129.ids, s32[1,512]{1,0:T(1,128)S(1)} %copy-done.11, bf16[49,29,512]{2,1,0:T(8,128)(2,1)} %bitcast.23, ...), custom_call_target="tpu_custom_call" | custom-call | flops 2055208960 | bytes 5256192 | tf_op jit(solution)/shard_map/pallas_call | solution.py:308
  47.5 4.2 %shard_map.164 = (bf16[896,512]{1,0:T(8,128)(2,1)S(1)}, bf16[1536,512]{1,0:T(8,128)(2,1)S(1)}, bf16[1280,512]{1,0:T(8,128)(2,1)S(1)}, f32[128,512]{1,0:T(8,128)S(1)}) custom-call(s32[1]{0:T(128)} %bitcast.12.live, s32[64,1]{1,0:T(8,128)S(1)} %add.129.ids, s32[1,512]{1,0:T(1,128)S(1)} %copy-done.10, bf16[49,29,512]{2,1,0:T(8,128)(2,1)} %bitcast.24, ...), custom_call_target="tpu_custom_call" | custom-call | flops 2055208960 | bytes 5256192 | tf_op jit(solution)/shard_map/pallas_call | solution.py:308
  55.0 3.6 %copy.20 = bf16[896,896]{0,1:T(8,128)(2,1)} copy(bf16[896,896]{1,0:T(8,128)(2,1)} %w_zero.1) | data formatting | bytes 3211264 | tf_op args[7]
  58.5 4.3 %copy.21 = bf16[2,768,768]{1,2,0:T(8,128)(2,1)} copy(bf16[2,768,768]{2,1,0:T(8,128)(2,1)} %w_one.1) | data formatting | bytes 4718592 | tf_op args[8]
  62.8 3.5 %copy.22 = bf16[2,640,640]{1,2,0:T(8,128)(2,1)} copy(bf16[2,640,640]{2,1,0:T(8,128)(2,1)} %w_two.1) | data formatting | bytes 3276800 | tf_op args[9]
  69.0 2.9 %shard_map.171 = bf16[6656,128]{1,0:T(8,128)(2,1)S(1)} custom-call(s32[32]{0:T(128)S(1)} %fusion.shift, bf16[1280,512]{1,0:T(8,128)(2,1)S(1)} %copy-done.16, bf16[1280,512]{1,0:T(8,128)(2,1)S(1)} %copy-done.13), custom_call_target="tpu_custom_call" | custom-call | flops 1677721600 | bytes 3276800 | tf_op jit(solution)/shard_map/pallas_call | solution.py:308
  77.3 16.0 %shard_map.165 = (bf16[64,6272]{1,0:T(8,128)(2,1)S(1)}, bf16[128,512]{1,0:T(8,128)(2,1)S(1)}, f32[1024,128]{1,0:T(8,128)}) custom-call(s32[1]{0:T(128)} %bitcast.13.live, s32[1,512]{1,0:T(1,128)S(1)} %copy-done.10, bf16[49,29,512]{2,1,0:T(8,128)(2,1)} %bitcast.25, bf16[896,512]{1,0:T(8,128)(2,1)S(1)} %get-tuple-element.18.x_zero.x, ...), custom_call_target="tpu_custom_call" | custom-call | flops 6970933248 | bytes 9057280 | tf_op jit(solution)/shard_map/pallas_call | solution.py:308
  97.8 3.3 %shard_map.169 = bf16[9216,128]{1,0:T(8,128)(2,1)S(1)} custom-call(s32[32]{0:T(128)S(1)} %subtract_multiply_fusion.shift, bf16[1536,512]{1,0:T(8,128)(2,1)S(1)} %copy-done.22, bf16[1536,512]{1,0:T(8,128)(2,1)S(1)} %copy-done.19), custom_call_target="tpu_custom_call" | custom-call | flops 2415919104 | bytes 4718592 | tf_op jit(solution)/shard_map/pallas_call | solution.py:308
  107.5 3.3 %collective-permute-done.6 = bf16[704,128]{1,0:T(8,128)(2,1)S(1)} collective-permute-done((bf16[704,128]{1,0:T(8,128)(2,1)S(1)}, bf16[704,128]{1,0:T(8,128)(2,1)S(1)}, u32[]{:S(2)}, u32[]{:S(2)}) %collective-permute-start.6) | collective-permute-done | bytes 180256 | tf_op jit(solution)/shard_map/ppermute | solution.py:327
  114.4 5.2 %collective-permute-done.7 = bf16[352,128]{1,0:T(8,128)(2,1)S(1)} collective-permute-done((bf16[352,128]{1,0:T(8,128)(2,1)S(1)}, bf16[352,128]{1,0:T(8,128)(2,1)S(1)}, u32[]{:S(2)}, u32[]{:S(2)}) %collective-permute-start.7) | collective-permute-done | bytes 90144 | tf_op jit(solution)/shard_map/ppermute | solution.py:327
  122.9 5.3 %collective-permute-done.8 = bf16[176,128]{1,0:T(8,128)(2,1)S(1)} collective-permute-done((bf16[176,128]{1,0:T(8,128)(2,1)S(1)}, bf16[176,128]{1,0:T(8,128)(2,1)S(1)}, u32[]{:S(2)}, u32[]{:S(2)}) %collective-permute-start.8) | collective-permute-done | bytes 45088 | tf_op jit(solution)/shard_map/ppermute | solution.py:327
  128.8 4.9 %collective-permute-done.9 = bf16[176,128]{1,0:T(8,128)(2,1)S(1)} collective-permute-done((bf16[176,128]{1,0:T(8,128)(2,1)S(1)}, bf16[176,128]{1,0:T(8,128)(2,1)S(1)}, u32[]{:S(2)}, u32[]{:S(2)}) %collective-permute-start.9) | collective-permute-done | bytes 45088 | tf_op jit(solution)/shard_map/ppermute | solution.py:327
  153.5 3.1 %collective-permute-done.16 = bf16[1152,128]{1,0:T(8,128)(2,1)S(1)} collective-permute-done((bf16[1152,128]{1,0:T(8,128)(2,1)S(1)}, bf16[1152,128]{1,0:T(8,128)(2,1)S(1)}, u32[]{:S(2)}, u32[]{:S(2)}) %collective-permute-start.16) | collective-permute-done | bytes 294944 | tf_op jit(solution)/shard_map/ppermute | solution.py:327
  159.3 2.7 %collective-permute-done.17 = bf16[576,128]{1,0:T(8,128)(2,1)S(1)} collective-permute-done((bf16[576,128]{1,0:T(8,128)(2,1)S(1)}, bf16[576,128]{1,0:T(8,128)(2,1)S(1)}, u32[]{:S(2)}, u32[]{:S(2)}) %collective-permute-start.17) | collective-permute-done | bytes 147488 | tf_op jit(solution)/shard_map/ppermute | solution.py:327
  178.7 2.9 %collective-permute-start.21 = (bf16[1152,128]{1,0:T(8,128)(2,1)S(1)}, bf16[1152,128]{1,0:T(8,128)(2,1)S(1)}, u32[]{:S(2)}, u32[]{:S(2)}) collective-permute-start(bf16[1152,128]{1,0:T(8,128)(2,1)S(1)} %pad_maximum_fusion.5), channel_id=1, source_target_pairs={{0,8},{4,12},{8,0},{12,4},{16,24},{20,28},{24,16},{28,20},{1,9},{5... | collective-permute-start | bytes 884744 | tf_op jit(solution)/shard_map/ppermute | solution.py:327
  183.1 3.7 %collective-permute-done.21 = bf16[1152,128]{1,0:T(8,128)(2,1)S(1)} collective-permute-done((bf16[1152,128]{1,0:T(8,128)(2,1)S(1)}, bf16[1152,128]{1,0:T(8,128)(2,1)S(1)}, u32[]{:S(2)}, u32[]{:S(2)}) %collective-permute-start.21) | collective-permute-done | bytes 294944 | tf_op jit(solution)/shard_map/ppermute | solution.py:327
  190.7 8.5 %collective-permute-done.22 = bf16[2304,128]{1,0:T(8,128)(2,1)S(1)} collective-permute-done((bf16[2304,128]{1,0:T(8,128)(2,1)S(1)}, bf16[2304,128]{1,0:T(8,128)(2,1)S(1)}, u32[]{:S(2)}, u32[]{:S(2)}) %collective-permute-start.22) | collective-permute-done | bytes 589856 | tf_op jit(solution)/shard_map/ppermute | solution.py:327
  200.2 13.1 %shard_map.166 = bf16[64,6272]{1,0:T(8,128)(2,1)S(1)} custom-call(s32[1,512]{1,0:T(1,128)S(1)} %copy-done.11, bf16[49,29,512]{2,1,0:T(8,128)(2,1)} %bitcast.26, bf16[512,128]{1,0:T(8,128)(2,1)S(1)} %bitcast.15, bf16[128,512]{1,0:T(8,128)(2,1)S(1)} %copy-done.30, bf16[896,512]{1,0:T(8,128)(2,1)S(1)} %get-tuple-element.22.g_zero.g, ...), custom_call_target="tpu_custom_call" | custom-call | flops 6970933248 | bytes 5256192 | tf_op jit(solution)/shard_map/pallas_call | solution.py:308
  214.3 25.9 %all-reduce.2.cloned.1.call-done.first = f32[1024,128]{1,0:T(8,128)} async-done(((f32[1024,128]{1,0:T(8,128)}), f32[1024,128]{1,0:T(8,128)}) %all-reduce.2.cloned.1.call-update) | async-done | bytes 524304 | tf_op jit(solution)/shard_map/psum | solution.py:480
  248.9 2.7 %shard_map.172 = f32[2,640,640]{2,1,0:T(8,128)} custom-call(s32[32]{0:T(128)S(1)} %fusion.shift, bf16[6656,128]{1,0:T(8,128)(2,1)S(1)} %constant_dynamic-update-slice_fusion.27.source), custom_call_target="tpu_custom_call" | custom-call | bytes 4915200 | tf_op jit(solution)/shard_map/pallas_call | solution.py:308
  253.0 3.1 %shard_map.170 = f32[2,768,768]{2,1,0:T(8,128)} custom-call(s32[32]{0:T(128)S(1)} %subtract_multiply_fusion.shift, bf16[9216,128]{1,0:T(8,128)(2,1)S(1)} %constant_dynamic-update-slice_fusion.16.source), custom_call_target="tpu_custom_call" | custom-call | bytes 7077888 | tf_op jit(solution)/shard_map/pallas_call | solution.py:308
  (197 shorter events, 96.1 us)
Async XLA Ops:
  8.0 232.1 %all-reduce.2.cloned.1.call-start = ((), (), s32[]{:S(2)}) async-start(), calls=%async_computation.4 | async-start | bytes 1048576 | tf_op jit(solution)/shard_map/psum | solution.py:480
  8.1 18.7 %collective-permute-start = (bf16[16,6272]{1,0:T(8,128)(2,1)}, bf16[16,6272]{1,0:T(8,128)(2,1)S(1)}, u32[]{:S(2)}, u32[]{:S(2)}) collective-permute-start(bf16[16,6272]{1,0:T(8,128)(2,1)} %bitcast.19), channel_id=1, source_target_pairs={{0,2},{1,3},{2,0},{3,1},{4,6},{5,7},{6,4},{7,5},{8,10},{9,11},{10,... | collective-permute-start | bytes 602120 | tf_op jit(solution)/shard_map/ppermute | solution.py:327
  12.2 18.2 %collective-permute-start.2 = (bf16[16,6272]{1,0:T(8,128)(2,1)}, bf16[16,6272]{1,0:T(8,128)(2,1)S(1)}, u32[]{:S(2)}, u32[]{:S(2)}) collective-permute-start(bf16[16,6272]{1,0:T(8,128)(2,1)} %bitcast.21), channel_id=1, source_target_pairs={{0,2},{1,3},{2,0},{3,1},{4,6},{5,7},{6,4},{7,5},{8,10},{9,11},{10,... | collective-permute-start | bytes 602120 | tf_op jit(solution)/shard_map/ppermute | solution.py:327
  27.8 12.3 %collective-permute-start.1 = (bf16[32,6272]{1,0:T(8,128)(2,1)S(1)}, bf16[32,6272]{1,0:T(8,128)(2,1)S(1)}, u32[]{:S(2)}, u32[]{:S(2)}) collective-permute-start(bf16[32,6272]{1,0:T(8,128)(2,1)S(1)} %pad_maximum_fusion.2.refs_0_), channel_id=1, source_target_pairs={{0,1},{1,0},{2,3},{3,2},{4,5},{5,4},{6,7},{7,6},{8,9},{9,8},{10,11... | collective-permute-start | bytes 1204232 | tf_op jit(solution)/shard_map/ppermute | solution.py:327
  31.3 16.1 %collective-permute-start.3 = (bf16[32,6272]{1,0:T(8,128)(2,1)S(1)}, bf16[32,6272]{1,0:T(8,128)(2,1)S(1)}, u32[]{:S(2)}, u32[]{:S(2)}) collective-permute-start(bf16[32,6272]{1,0:T(8,128)(2,1)S(1)} %pad_maximum_fusion.3.refs_0_), channel_id=1, source_target_pairs={{0,1},{1,0},{2,3},{3,2},{4,5},{5,4},{6,7},{7,6},{8,9},{9,8},{10,11... | collective-permute-start | bytes 1204232 | tf_op jit(solution)/shard_map/ppermute | solution.py:327
  55.0 18.6 %collective-permute-start.4 = (bf16[2816,128]{1,0:T(8,128)(2,1)}, bf16[2816,128]{1,0:T(8,128)(2,1)}, u32[]{:S(2)}, u32[]{:S(2)}) collective-permute-start(bf16[2816,128]{1,0:T(8,128)(2,1)} %slice.129), channel_id=1, source_target_pairs={{0,4},{4,0},{8,12},{12,8},{16,20},{20,16},{24,28},{28,24},{1,5},{5... | collective-permute-start | bytes 2162696 | tf_op jit(solution)/shard_map/ppermute | solution.py:327
  73.0 32.3 %collective-permute-start.24 = (bf16[3328,128]{1,0:T(8,128)(2,1)}, bf16[3328,128]{1,0:T(8,128)(2,1)}, u32[]{:S(2)}, u32[]{:S(2)}) collective-permute-start(bf16[3328,128]{1,0:T(8,128)(2,1)} %slice.149), channel_id=1, source_target_pairs={{0,4},{4,0},{8,12},{12,8},{16,20},{20,16},{24,28},{28,24},{1,5},{5... | collective-permute-start | bytes 2555912 | tf_op jit(solution)/shard_map/ppermute | solution.py:327
  75.8 26.7 %collective-permute-start.5 = (bf16[1408,128]{1,0:T(8,128)(2,1)}, bf16[1408,128]{1,0:T(8,128)(2,1)}, u32[]{:S(2)}, u32[]{:S(2)}) collective-permute-start(bf16[1408,128]{1,0:T(8,128)(2,1)} %slice.131), channel_id=1, source_target_pairs={{0,8},{4,12},{8,0},{12,4},{16,24},{20,28},{24,16},{28,20},{1,9},{5... | collective-permute-start | bytes 1081352 | tf_op jit(solution)/shard_map/ppermute | solution.py:327
  94.9 161.2 %reduce-scatter.3.cloned.1.call-start = ((), (), s32[]{:S(2)}) async-start(), calls=%async_computation.2 | async-start | bytes 1003520 | tf_op jit(solution)/shard_map/reduce_scatter | solution.py:479
  102.1 9.1 %collective-permute-start.14 = (bf16[4608,128]{1,0:T(8,128)(2,1)}, bf16[4608,128]{1,0:T(8,128)(2,1)}, u32[]{:S(2)}, u32[]{:S(2)}) collective-permute-start(bf16[4608,128]{1,0:T(8,128)(2,1)} %slice.139), channel_id=1, source_target_pairs={{0,4},{4,0},{8,12},{12,8},{16,20},{20,16},{24,28},{28,24},{1,5},{5... | collective-permute-start | bytes 3538952 | tf_op jit(solution)/shard_map/ppermute | solution.py:327
  102.2 153.9 %reduce-scatter.5.cloned.1.call-start = ((), (), s32[]{:S(2)}) async-start(), calls=%async_computation.3 | async-start | bytes 1003520 | tf_op jit(solution)/shard_map/reduce_scatter | solution.py:489
  106.9 14.1 %collective-permute-start.25 = (bf16[1664,128]{1,0:T(8,128)(2,1)S(1)}, bf16[1664,128]{1,0:T(8,128)(2,1)S(1)}, u32[]{:S(2)}, u32[]{:S(2)}) collective-permute-start(bf16[1664,128]{1,0:T(8,128)(2,1)S(1)} %slice.151), channel_id=1, source_target_pairs={{0,8},{4,12},{8,0},{12,4},{16,24},{20,28},{24,16},{28,20},{1,9},{5... | collective-permute-start | bytes 1277960 | tf_op jit(solution)/shard_map/ppermute | solution.py:327
  112.9 34.9 %collective-permute-start.15 = (bf16[2304,128]{1,0:T(8,128)(2,1)S(1)}, bf16[2304,128]{1,0:T(8,128)(2,1)S(1)}, u32[]{:S(2)}, u32[]{:S(2)}) collective-permute-start(bf16[2304,128]{1,0:T(8,128)(2,1)S(1)} %slice.141), channel_id=1, source_target_pairs={{0,16},{4,20},{8,24},{12,28},{16,0},{20,4},{24,8},{28,12},{1,17},{... | collective-permute-start | bytes 1769480 | tf_op jit(solution)/shard_map/ppermute | solution.py:327
  121.2 13.3 %collective-permute-start.26 = (bf16[832,128]{1,0:T(8,128)(2,1)S(1)}, bf16[832,128]{1,0:T(8,128)(2,1)S(1)}, u32[]{:S(2)}, u32[]{:S(2)}) collective-permute-start(bf16[832,128]{1,0:T(8,128)(2,1)S(1)} %slice.153), channel_id=1, source_target_pairs={{0,16},{4,20},{8,24},{12,28},{16,0},{20,4},{24,8},{28,12},{1,17},{... | collective-permute-start | bytes 638984 | tf_op jit(solution)/shard_map/ppermute | solution.py:327
  138.4 18.4 %collective-permute-start.11 = (bf16[704,128]{1,0:T(8,128)(2,1)S(1)}, bf16[704,128]{1,0:T(8,128)(2,1)S(1)}, u32[]{:S(2)}, u32[]{:S(2)}) collective-permute-start(bf16[704,128]{1,0:T(8,128)(2,1)S(1)} %pad_maximum_fusion.7), channel_id=1, source_target_pairs={{0,16},{4,20},{8,24},{12,28},{16,0},{20,4},{24,8},{28,12},{1,17},{... | collective-permute-start | bytes 540680 | tf_op jit(solution)/shard_map/ppermute | solution.py:327
  147.9 8.7 %collective-permute-start.16 = (bf16[1152,128]{1,0:T(8,128)(2,1)S(1)}, bf16[1152,128]{1,0:T(8,128)(2,1)S(1)}, u32[]{:S(2)}, u32[]{:S(2)}) collective-permute-start(bf16[1152,128]{1,0:T(8,128)(2,1)S(1)} %slice.143), channel_id=1, source_target_pairs={{0,8},{4,12},{8,0},{12,4},{16,24},{20,28},{24,16},{28,20},{1,9},{5... | collective-permute-start | bytes 884744 | tf_op jit(solution)/shard_map/ppermute | solution.py:327
  150.9 13.0 %collective-permute-start.30 = (bf16[416,128]{1,0:T(8,128)(2,1)S(1)}, bf16[416,128]{1,0:T(8,128)(2,1)S(1)}, u32[]{:S(2)}, u32[]{:S(2)}) collective-permute-start(bf16[416,128]{1,0:T(8,128)(2,1)S(1)} %pad_maximum_fusion.9), channel_id=1, source_target_pairs={{0,1},{1,0},{2,3},{3,2},{4,5},{5,4},{6,7},{7,6},{8,9},{9,8},{10,11... | collective-permute-start | bytes 319496 | tf_op jit(solution)/shard_map/ppermute | solution.py:327
  156.8 24.8 %collective-permute-start.12 = (bf16[1408,128]{1,0:T(8,128)(2,1)S(1)}, bf16[1408,128]{1,0:T(8,128)(2,1)S(1)}, u32[]{:S(2)}, u32[]{:S(2)}) collective-permute-start(bf16[1408,128]{1,0:T(8,128)(2,1)S(1)} %pad_maximum_fusion.4), channel_id=1, source_target_pairs={{0,8},{4,12},{8,0},{12,4},{16,24},{20,28},{24,16},{28,20},{1,9},{5... | collective-permute-start | bytes 1081352 | tf_op jit(solution)/shard_map/ppermute | solution.py:327
  163.9 11.5 %collective-permute-start.31 = (bf16[832,128]{1,0:T(8,128)(2,1)S(1)}, bf16[832,128]{1,0:T(8,128)(2,1)S(1)}, u32[]{:S(2)}, u32[]{:S(2)}) collective-permute-start(bf16[832,128]{1,0:T(8,128)(2,1)S(1)} %pad_maximum_fusion.6), channel_id=1, source_target_pairs={{0,16},{4,20},{8,24},{12,28},{16,0},{20,4},{24,8},{28,12},{1,17},{... | collective-permute-start | bytes 638984 | tf_op jit(solution)/shard_map/ppermute | solution.py:327
  175.5 13.0 %collective-permute-start.32 = (bf16[1664,128]{1,0:T(8,128)(2,1)S(1)}, bf16[1664,128]{1,0:T(8,128)(2,1)S(1)}, u32[]{:S(2)}, u32[]{:S(2)}) collective-permute-start(bf16[1664,128]{1,0:T(8,128)(2,1)S(1)} %pad_maximum_fusion.1), channel_id=1, source_target_pairs={{0,8},{4,12},{8,0},{12,4},{16,24},{20,28},{24,16},{28,20},{1,9},{5... | collective-permute-start | bytes 1277960 | tf_op jit(solution)/shard_map/ppermute | solution.py:327
  182.4 59.3 %collective-permute-start.13 = (bf16[2816,128]{1,0:T(8,128)(2,1)}, bf16[2816,128]{1,0:T(8,128)(2,1)}, u32[]{:S(2)}, u32[]{:S(2)}) collective-permute-start(bf16[2816,128]{1,0:T(8,128)(2,1)} %get-tuple-element.40), channel_id=1, source_target_pairs={{0,4},{4,0},{8,12},{12,8},{16,20},{20,16},{24,28},{28,24},{1,5},{5... | collective-permute-start | bytes 2162696 | tf_op jit(solution)/shard_map/ppermute | solution.py:327
  186.9 12.4 %collective-permute-start.22 = (bf16[2304,128]{1,0:T(8,128)(2,1)S(1)}, bf16[2304,128]{1,0:T(8,128)(2,1)S(1)}, u32[]{:S(2)}, u32[]{:S(2)}) collective-permute-start(bf16[2304,128]{1,0:T(8,128)(2,1)S(1)} %pad_maximum_fusion), channel_id=1, source_target_pairs={{0,16},{4,20},{8,24},{12,28},{16,0},{20,4},{24,8},{28,12},{1,17},{... | collective-permute-start | bytes 1769480 | tf_op jit(solution)/shard_map/ppermute | solution.py:327
  189.3 58.4 %collective-permute-start.33 = (bf16[3328,128]{1,0:T(8,128)(2,1)}, bf16[3328,128]{1,0:T(8,128)(2,1)}, u32[]{:S(2)}, u32[]{:S(2)}) collective-permute-start(bf16[3328,128]{1,0:T(8,128)(2,1)} %get-tuple-element.38), channel_id=1, source_target_pairs={{0,4},{4,0},{8,12},{12,8},{16,20},{20,16},{24,28},{28,24},{1,5},{5... | collective-permute-start | bytes 2555912 | tf_op jit(solution)/shard_map/ppermute | solution.py:327
  200.1 51.5 %collective-permute-start.23 = (bf16[4608,128]{1,0:T(8,128)(2,1)}, bf16[4608,128]{1,0:T(8,128)(2,1)}, u32[]{:S(2)}, u32[]{:S(2)}) collective-permute-start(bf16[4608,128]{1,0:T(8,128)(2,1)} %get-tuple-element.36), channel_id=1, source_target_pairs={{0,4},{4,0},{8,12},{12,8},{16,20},{20,16},{24,28},{28,24},{1,5},{5... | collective-permute-start | bytes 3538952 | tf_op jit(solution)/shard_map/ppermute | solution.py:327
  (45 other events, 286.2 us)
Sparse Core Ops, SparseCore 0:
  95.0 145.0 all-reduce.1
Sparse Core Ops, SparseCore 1:
  102.2 27.5 reduce-scatter.2
  214.3 24.0 reduce-scatter.4

commit v2 on v1

v2 whole, which is shorter than its diff:
```python
import functools
import math

import jax
import jax.numpy as jnp
from jax import lax
from jax.experimental import pallas as pl
from jax.experimental.pallas import tpu as pltpu
from jax.sharding import PartitionSpec as P

F32 = jnp.float32
BF16 = jnp.bfloat16
SPARE_VMEM = 8 * 1024 * 1024


def dot_nn(left, right):
    return jnp.dot(left, right, preferred_element_type=F32)


def dot_nt(left, right):
    return lax.dot_general(left, right, (((1,), (1,)), ((), ())), preferred_element_type=F32)


def dot_tn(left, right):
    return lax.dot_general(left, right, (((0,), (0,)), ((), ())), preferred_element_type=F32)


def kept_rows(degree, sizes):
    zero, one, two = sizes
    rows = [degree]
    if degree >= 1:
        rows += [zero + degree - 1, zero + one + degree - 1]
    if degree >= 2:
        rows += [zero + 2 * one + degree - 2, zero + 2 * one + two + degree - 2]
    return rows


def group_of(row, sizes):
    zero, one, two = sizes
    if row < zero:
        return 0, row
    if row < zero + 2 * one:
        return 1, row - zero
    return 2, row - zero - 2 * one


class Copies:
    def __init__(self, semaphores):
        self.semaphores = semaphores
        self.count = 0

    def start(self, sources, targets):
        started = []
        for source, target in zip(sources, targets):
            copy = pltpu.make_async_copy(source, target, self.semaphores.at[self.count])
            copy.start()
            self.count += 1
            started.append(copy)
        return started


def wait(started):
    for copy in started:
        copy.wait()


def prepare_kernel(
    wigner_hbm, w_zero_hbm, w_one_hbm, w_two_hbm, radial, wide, scale, t_zero, t_one, t_two,
    wigner, w_zero, w_one, w_two, semaphores
):
    copies = Copies(semaphores)
    first = copies.start((wigner_hbm, w_zero_hbm), (wigner, w_zero))
    rest = copies.start((w_one_hbm, w_two_hbm), (w_one, w_two))
    scale[...] = radial[...].astype(F32).T
    wait(first)
    for j in range(wigner.shape[0]):
        wide[j] = wigner[j].astype(F32)
    t_zero[...] = w_zero[...].T
    wait(rest)
    for part in range(2):
        t_one[part] = w_one[part].T
        t_two[part] = w_two[part].T


def fill_spread(degree, sizes, hits, wide_ref, spread_ref):
    nodes, edges = hits.shape
    for j in range(2 * degree + 1):
        for place, k in enumerate(kept_rows(degree, sizes)):
            row = wide_ref[degree * degree + j, k : k + 1, :]
            row = jnp.broadcast_to(row, (16, edges)).astype(BF16)
            for part in range(nodes // 16):
                at = j * nodes + part * 16
                spread_ref[at : at + 16, place * edges : (place + 1) * edges] = (
                    hits[part * 16 : (part + 1) * 16] * row
                )


def turn(pieces, sizes, hits, wide_ref, spreads, stacked, degree, width):
    nodes, edges = hits.shape
    orders = 2 * degree + 1
    spread_ref = spreads[degree % 2]
    fill_spread(degree, sizes, hits, wide_ref, spread_ref)
    for j in range(orders):
        column = (degree * degree + j) * width
        at = j * nodes
        for piece in pieces:
            stacked[at : at + piece.shape[0], :] = piece[:, column : column + width]
            at += piece.shape[0]
    count = len(kept_rows(degree, sizes))
    return dot_tn(stacked[0 : orders * nodes, :], spread_ref[0 : orders * nodes, 0 : count * edges])


def nodes_kernel(sizes, order, sources, wide, scale, first, gating, *refs):
    pieces, (x_zero, x_one, x_two, scalar, gate), (even, odd, stacked) = (
        refs[:-8],
        refs[-8:-3],
        refs[-3:],
    )
    width = gating.shape[0]
    edges = sources.shape[1]
    hits = shard_hits(order, pieces[0].shape[0], sources[...])
    outs = (x_zero, x_one, x_two)
    for degree in range(sizes[0]):
        turned = turn(pieces, sizes, hits, wide, (even, odd), stacked, degree, width)
        for place, k in enumerate(kept_rows(degree, sizes)):
            group, row = group_of(k, sizes)
            outs[group][row * width : (row + 1) * width, :] = (
                turned[:, place * edges : (place + 1) * edges] * scale[...]
            ).astype(BF16)
    low = dot_nn(first[...], x_zero[...])
    scalar[...] = low
    gate[...] = jax.nn.sigmoid(dot_tn(gating[...], low.astype(BF16)))


def products_kernel(
    sizes, x_zero, x_one, x_two, scalar, gate, w_zero, w_one, w_two,
    m_zero, m_one, m_two, messages, mixed
):
    width, edges = gate.shape
    zero, one, two = sizes

    def settle(out, first_row, base, count):
        for row in range(count):
            k = base + row
            at = (first_row + row) * width
            raw = mixed[row * width : (row + 1) * width, :]
            out[at : at + width, :] = raw.astype(BF16)
            if k == 0:
                v = scalar[...]
                value = v * jax.nn.sigmoid(v)
            else:
                value = raw * gate[...]
            store_row(messages, sizes, k, value)

    mixed[0 : zero * width, :] = dot_nn(w_zero[...], x_zero[...])
    settle(m_zero, 0, 0, zero)
    base = zero
    for size, x, w, out in ((one, x_one, w_one, m_one), (two, x_two, w_two, m_two)):
        half = size * width
        mixed[0:half, :] = dot_nn(w[0], x[:half]) - dot_nn(w[1], x[half:])
        settle(out, 0, base, size)
        mixed[0:half, :] = dot_nn(w[1], x[:half]) + dot_nn(w[0], x[half:])
        settle(out, size, base + size, size)
        base += 2 * size


def store_row(values, sizes, k, value):
    edges = value.shape[1]
    for degree in range(sizes[0]):
        rows = kept_rows(degree, sizes)
        if k in rows:
            place = rows.index(k)
            values[degree, :, place * edges : (place + 1) * edges] = value.astype(BF16)


def shard_hits(order, shard, index):
    mine = lax.axis_index("graph")
    rows = lax.broadcasted_iota(jnp.int32, (shard, index.shape[1]), 0)
    hits = [(rows + (other ^ mine) * shard == index).astype(F32).astype(BF16) for other in order]
    return jnp.concatenate(hits, axis=0)


def only_live(live, index):
    slots = lax.broadcasted_iota(jnp.int32, index.shape, 1)
    return jnp.where(slots < live[0], index[...], -1)


def place_of(stages):
    mine = jnp.int32(0)
    for axis, bit in stages:
        mine = 2 * mine + jnp.where((lax.axis_index(axis) & bit) != 0, 1, 0)
    return mine


def cotangent_kernel(
    sizes, order, live, targets, wide, scalar, gate, gating, m_zero, m_one, m_two, *refs
):
    pieces, (g_zero, g_one, g_two, gate_low), (even, odd, stacked, total, head) = (
        refs[:-9],
        refs[-9:-5],
        refs[-5:],
    )
    width, edges = gate.shape
    hits = shard_hits(order, pieces[0].shape[0], only_live(live, targets))
    outs = (g_zero, g_one, g_two)
    mixed = (m_zero, m_one, m_two)
    total[...] = jnp.zeros((width, edges), F32)
    for degree in range(sizes[0]):
        turned = turn(pieces, sizes, hits, wide, (even, odd), stacked, degree, width)
        for place, k in enumerate(kept_rows(degree, sizes)):
            group, row = group_of(k, sizes)
            value = turned[:, place * edges : (place + 1) * edges]
            if k == 0:
                head[...] = value
            else:
                at = row * width
                value = value * gate[...]
                outs[group][at : at + width, :] = value.astype(BF16)
                total[...] += value * mixed[group][at : at + width, :].astype(F32)
    low = (total[...] * (1.0 - gate[...])).astype(BF16)
    gate_low[...] = low
    v = scalar[...]
    s = jax.nn.sigmoid(v)
    first = head[...] * s * (1.0 + v * (1.0 - s)) + dot_nn(gating[...], low)
    g_zero[0:width, :] = first.astype(BF16)


def runs(block, flat, rows):
    at = 0
    while at < rows:
        step = min(rows - at, block - (flat + at) % block)
        yield at, step, (flat + at) // block
        at += step


def place_rows(mine, out, block, flat, values):
    for at, step, index in runs(block, flat, values.shape[0]):
        start = pl.multiple_of(flat + at + ((index ^ mine) - index) * block, 16)
        out[pl.ds(start, step), :] = values[at : at + step]


def place_matrix(mine, out, block, flat, total, rows, columns, width):
    for column in range(0, columns, width):
        place_rows(mine, out, block, flat, total[0:rows, column : column + width].astype(BF16))
        flat += rows
    return flat


def finish_rows(mine, out, block, flat, kept, sent):
    rows, width = out.shape
    if flat < rows:
        place_rows(mine, out, block, flat, jnp.zeros((rows - flat, width), BF16))
    kept[...] = out[: rows // 2]
    sent[...] = out[rows // 2 :]


def grad_a_kernel(block, stages, x_two, g_two, x_one, g_one, kept, sent, out, total):
    mine = place_of(stages)
    width = out.shape[1]
    half = x_two.shape[0] // 2
    total[0:half, 0:half] = dot_nt(x_two[:half], g_two[:half]) + dot_nt(x_two[half:], g_two[half:])
    flat = place_matrix(mine, out, block, 0, total, half, half, width)
    total[0:half, 0:half] = dot_nt(x_two[:half], g_two[half:]) - dot_nt(x_two[half:], g_two[:half])
    flat = place_matrix(mine, out, block, flat, total, half, half, width)
    half = x_one.shape[0] // 2
    total[0:half, 0:half] = dot_nt(x_one[:half], g_one[:half]) + dot_nt(x_one[half:], g_one[half:])
    flat = place_matrix(mine, out, block, flat, total, half, half, width)
    finish_rows(mine, out, block, flat, kept, sent)


def grad_b_kernel(
    block, stages, x_one, g_one, x_zero, g_zero, scalar, gate_low, kept, sent, out, total
):
    mine = place_of(stages)
    width = out.shape[1]
    half = x_one.shape[0] // 2
    total[0:half, 0:half] = dot_nt(x_one[:half], g_one[half:]) - dot_nt(x_one[half:], g_one[:half])
    flat = place_matrix(mine, out, block, 0, total, half, half, width)
    rows = x_zero.shape[0]
    total[...] = dot_nt(x_zero[...], g_zero[...])
    flat = place_matrix(mine, out, block, flat, total, rows, rows, width)
    gate_grad = dot_nt(scalar[...].astype(BF16), gate_low[...]).astype(BF16)
    place_rows(mine, out, block, flat, gate_grad)
    finish_rows(mine, out, block, flat + width, kept, sent)


def spread_back(sizes, hits, wide, spreads, values, kept, sent):
    width = values.shape[1]
    half = kept.shape[0]
    nodes, edges = hits.shape
    for degree in range(sizes[0]):
        spread_ref = spreads[degree % 2]
        fill_spread(degree, sizes, hits, wide, spread_ref)
        lanes = len(kept_rows(degree, sizes)) * edges
        orders = 2 * degree + 1
        summed = dot_nt(
            spread_ref[0 : orders * nodes, 0:lanes], values[degree, :, 0:lanes]
        ).astype(BF16)
        for j in range(orders):
            column = (degree * degree + j) * width
            kept[:, column : column + width] = summed[j * nodes : j * nodes + half]
            sent[:, column : column + width] = summed[j * nodes + half : (j + 1) * nodes]


def back_kernel(
    sizes, order, live, w_zero_hbm, w_one_hbm, w_two_hbm, sources, targets, wide, scale, messages,
    g_zero, g_one, g_two, sum_kept, sum_sent, grad_kept, grad_sent,
    w_zero, w_one, w_two, even, odd, values, moved, semaphores
):
    copies = Copies(semaphores)
    given = copies.start((w_zero_hbm, w_one_hbm, w_two_hbm), (w_zero, w_one, w_two))
    shard = 2 * sum_kept.shape[0] // len(order)
    hits = shard_hits(order, shard, only_live(live, targets))
    spread_back(sizes, hits, wide, (even, odd), messages, sum_kept, sum_sent)

    zero, one, two = sizes
    width = scale.shape[0]

    def settle(base, count):
        for row in range(count):
            value = moved[row * width : (row + 1) * width, :] * scale[...]
            store_row(values, sizes, base + row, value)

    wait(given)
    moved[0 : zero * width, :] = dot_nn(w_zero[...], g_zero[...])
    settle(0, zero)
    base = zero
    for size, g, w in ((one, g_one, w_one), (two, g_two, w_two)):
        half = size * width
        moved[0:half, :] = dot_nn(w[0], g[:half]) + dot_nn(w[1], g[half:])
        settle(base, size)
        moved[0:half, :] = dot_nn(w[0], g[half:]) - dot_nn(w[1], g[:half])
        settle(base + size, size)
        base += 2 * size
    hits = shard_hits(order, shard, sources[...])
    spread_back(sizes, hits, wide, (even, odd), values, grad_kept, grad_sent)


def take_matrix(mine, joined, block, flat, rows, columns, out):
    width = joined.shape[1]
    for column in range(0, columns, width):
        for at, step, index in runs(block, flat, rows):
            start = pl.multiple_of(flat + at + ((index ^ mine) - index) * block, 16)
            out[at : at + step, column : column + width] = joined[pl.ds(start, step), :].astype(F32)
        flat += rows
    return flat


def join(low, high, joined):
    rows = low.shape[0]
    joined[0:rows, :] = low[...]
    joined[rows:, :] = high[...]


def finish_two_kernel(block, stages, low, high, result, out, joined, semaphores):
    half = out.shape[1]
    copies = Copies(semaphores)
    join(low, high, joined)
    flat, started = 0, []
    for part in range(2):
        flat = take_matrix(place_of(stages), joined, block, flat, half, half, out.at[part])
        started += copies.start((out.at[part],), (result.at[part],))
    wait(started)


def finish_kernel(
    block, skip_a, skip_b, stages_a, stages_b, low_a, high_a, low_b, high_b,
    one_result, zero_result, gate_result, one, zero, gate, joined, semaphores
):
    half = one.shape[1]
    copies = Copies(semaphores)
    join(low_a, high_a, joined)
    take_matrix(place_of(stages_a), joined, block, skip_a, half, half, one.at[0])
    started = copies.start((one.at[0],), (one_result.at[0],))
    join(low_b, high_b, joined)
    mine = place_of(stages_b)
    take_matrix(mine, joined, block, 0, half, half, one.at[1])
    started += copies.start((one.at[1],), (one_result.at[1],))
    side = zero.shape[0]
    flat = take_matrix(mine, joined, block, skip_b, side, side, zero)
    started += copies.start((zero,), (zero_result,))
    take_matrix(mine, joined, block, flat, gate.shape[0], gate.shape[1], gate)
    started += copies.start((gate,), (gate_result,))
    wait(started)


SMEM = pl.BlockSpec(memory_space=pltpu.SMEM)
VMEM = pl.BlockSpec(memory_space=pltpu.VMEM)
ANY = pl.BlockSpec(memory_space=pl.ANY)


def call(kernel, out_shape, args, scratch=(), smem=0, hbm=0, copies=0, flops=0, moved=0):
    vmem = [pltpu.with_memory_space_constraint(a, pltpu.VMEM) for a in args[smem + hbm :]]
    held = sum(math.prod(a.shape) * jnp.dtype(a.dtype).itemsize for a in scratch)
    held += held // 8
    if copies:
        scratch = [*scratch, pltpu.SemaphoreType.DMA((copies,))]
    return pl.pallas_call(
        kernel,
        out_shape=out_shape,
        in_specs=[SMEM] * smem + [ANY] * hbm + [VMEM] * len(vmem),
        out_specs=tuple(ANY if isinstance(o, jax.ShapeDtypeStruct) else VMEM for o in out_shape),
        scratch_shapes=list(scratch),
        compiler_params=pltpu.CompilerParams(vmem_limit_bytes=held + SPARE_VMEM),
        cost_estimate=pl.CostEstimate(
            flops=int(flops), bytes_accessed=int(moved), transcendentals=0
        ),
    )(*args[: smem + hbm], *vmem)


def shaped(shape, dtype):
    return jax.ShapeDtypeStruct(shape, dtype)


def exchange(value, axis, bit):
    count = lax.axis_size(axis)
    return lax.ppermute(value, axis, [(i, i ^ bit) for i in range(count)])


def bits_of(axis):
    count = lax.axis_size(axis)
    return [(axis, 1 << b) for b in range(count.bit_length() - 1)]


def relative_gather(shards, beside):
    order, held = [0], [[shard] for shard in shards]
    for axis, bit in bits_of("graph")[::-1]:
        held = [blocks + [exchange(block, axis, bit) for block in blocks] for blocks in held]
        order = order + [o ^ bit for o in order]
        if len(order) == 2:
            held[0][1], *beside = tied(held[0][1], *beside)
    return held, order, beside


def relative_sum(arrays, stages):
    for axis, bit in stages:
        half = arrays[0].shape[0] // 2
        sent = jnp.concatenate([rows[half:] for rows in arrays], axis=0)
        other = exchange(sent, axis, bit)
        arrays = [
            add_low(rows[:half], other[at * half : (at + 1) * half])
            for at, rows in enumerate(arrays)
        ]
    return arrays


def tied(*values):
    return lax.optimization_barrier(values)


def add_low(kept, other):
    return (kept.astype(F32) + other.astype(F32)).astype(BF16)


def per_device(
    nodes, sources, targets, edge_counts, wigner, radial, cotangent, w_zero, w_one, w_two, w_gate
):
    width = w_gate.shape[0]
    zero, one, two = w_zero.shape[0] // width, w_one.shape[1] // width, w_two.shape[1] // width
    sizes = (zero, one, two)
    shard = nodes.shape[1]
    node_count = shard * lax.axis_size("graph")
    edges = sources.shape[1]
    coefficients = wigner.shape[2]
    kept = wigner.shape[1]
    features = nodes.shape[2]
    live = edge_counts[0]
    rotation = jnp.transpose(wigner[0], (1, 0, 2))
    radial_rows = radial[0]

    pairs = 2 * zero - 1
    spread = [
        pltpu.VMEM(((2 * d + 1) * node_count, 5 * edges), BF16) for d in (zero - 1, zero - 2)
    ]
    if zero % 2 == 0:
        spread = spread[::-1]
    stacked = pltpu.VMEM((pairs * node_count, width), BF16)
    edge_block = pltpu.VMEM((width, edges), F32)
    turn_cost = 2 * coefficients * 5 * node_count * width * edges
    edge_flops = 2 * edges * width * width * (zero * zero + 4 * one * one + 4 * two * two)
    rows = [zero * width, 2 * one * width, 2 * two * width]
    wide_rows = [pltpu.VMEM((r, edges), BF16) for r in rows]
    values_shape = pltpu.VMEM((zero, width, 5 * edges), BF16)
    products = pltpu.VMEM((zero * width, edges), F32)
    partial_shape = pltpu.VMEM((node_count // 2, features), BF16)
    weights = [pltpu.VMEM(w.shape, BF16) for w in (w_zero, w_one, w_two)]

    prepared = call(
        prepare_kernel,
        (pltpu.VMEM(rotation.shape, F32), edge_block, *weights),
        [rotation, w_zero, w_one, w_two, radial_rows],
        [pltpu.VMEM(rotation.shape, BF16), *weights],
        hbm=4,
        copies=4,
        moved=rotation.size * 8 + edge_flops / edges,
    )
    (node_blocks, upstream_blocks), order, prepared = relative_gather(
        (nodes[0], cotangent[0]), prepared
    )
    wide, scale, *turned = prepared
    node_blocks[0], *upstream_blocks[:2] = tied(node_blocks[0], *upstream_blocks[:2])
    x_zero, x_one, x_two, scalar, gate = call(
        functools.partial(nodes_kernel, sizes, order),
        (*wide_rows, edge_block, edge_block),
        [sources, wide, scale, turned[0][:width], w_gate, *node_blocks],
        [*spread, stacked],
        flops=turn_cost,
        moved=4 * sum(rows) * edges,
    )
    m_zero, m_one, m_two, messages = call(
        functools.partial(products_kernel, sizes),
        (*wide_rows, values_shape),
        [x_zero, x_one, x_two, scalar, gate, *turned],
        [products],
        flops=edge_flops,
        moved=6 * sum(rows) * edges,
    )
    g_zero, g_one, g_two, gate_low = call(
        functools.partial(cotangent_kernel, sizes, order),
        (*wide_rows, pltpu.VMEM((width, edges), BF16)),
        [live, targets, wide, scalar, gate, w_gate, m_zero, m_one, m_two]
        + upstream_blocks,
        [*spread, stacked, edge_block, edge_block],
        smem=1,
        flops=turn_cost,
        moved=4 * sum(rows) * edges,
    )

    dp_bits = bits_of("dp")
    stages_a = dp_bits + bits_of("graph")
    stages_b = dp_bits[:1] + dp_bits[1:][::-1] + bits_of("graph")
    blocks = lax.axis_size("dp") * lax.axis_size("graph")
    rows_two = 2 * two * two * width
    rows_one = one * one * width
    rows_zero = zero * zero * width
    most = max(rows_two + rows_one, rows_one + rows_zero + width)
    block = -(-most // (16 * blocks)) * 16
    half_list = pltpu.VMEM((blocks * block // 2, width), BF16)
    whole_list = pltpu.VMEM((blocks * block, width), BF16)
    side = zero * width
    square = pltpu.VMEM((side, side), F32)
    a, sent_a = call(
        functools.partial(grad_a_kernel, block, stages_a),
        (half_list, half_list),
        [x_two, g_two, x_one, g_one],
        [whole_list, square],
        flops=edge_flops / 2,
        moved=4 * blocks * block * width,
    )
    b, sent_b = call(
        functools.partial(grad_b_kernel, block, stages_b),
        (half_list, half_list),
        [x_one, g_one, x_zero, g_zero, scalar, gate_low],
        [whole_list, square],
        flops=edge_flops / 2,
        moved=4 * blocks * block * width,
    )

    graph_bits = bits_of("graph")
    last = len(dp_bits) - 1
    for place, (stage_a, stage_b) in enumerate(zip(stages_a, stages_b)):
        if place > 0:
            half = a.shape[0] // 2
            a, sent_a, b, sent_b = a[:half], a[half:], b[:half], b[half:]
        if place <= last:
            other_a, other_b = exchange(sent_a, *stage_a), exchange(sent_b, *stage_b)
        else:
            other = exchange(jnp.concatenate([sent_a, sent_b], axis=0), *stage_a)
            other_a, other_b = other[:half], other[half:]
        if place == 0:
            a, b = add_low(a, other_a), add_low(b, other_b)
            a, b, messages = tied(a, b, messages)
            sum_kept, sum_sent, grad_kept, grad_sent = call(
                functools.partial(back_kernel, sizes, order),
                (partial_shape,) * 4,
                [
                    live, w_zero, w_one, w_two, sources, targets, wide, scale, messages,
                    g_zero, g_one, g_two,
                ],
                [*weights, *spread, pltpu.VMEM(values_shape.shape, BF16), products],
                smem=1,
                hbm=3,
                copies=3,
                flops=edge_flops + 2 * turn_cost,
                moved=8 * sum(rows) * edges,
            )
            continue
        if place == 1:
            other_a, other_b, sum_kept, sum_sent, grad_kept, grad_sent = tied(
                other_a, other_b, sum_kept, sum_sent, grad_kept, grad_sent
            )
            sum_half = add_low(sum_kept, exchange(sum_sent, *graph_bits[0]))
        if place == last:
            other_a, other_b, sum_half = tied(other_a, other_b, sum_half)
        a, b = add_low(a, other_a), add_low(b, other_b)
    ab = jnp.concatenate([a, b], axis=0)
    for stage in stages_a[:last:-1]:
        half = ab.shape[0] // 2
        other = exchange(ab, *stage)
        ab = jnp.concatenate([ab[:half], other[:half], ab[half:], other[half:]], axis=0)
    ab, grad_kept, grad_sent, sum_half = tied(ab, grad_kept, grad_sent, sum_half)
    grad_half = add_low(grad_kept, exchange(grad_sent, *graph_bits[0]))
    half = ab.shape[0] // 2
    a, b = ab[:half], ab[half:]
    for place in range(len(dp_bits))[::-1]:
        half_a = (a, exchange(a, *stages_a[place]))
        half_b = (b, exchange(b, *stages_b[place]))
        if place == last:
            (low_a, high_a), (low_b, high_b) = half_a, half_b
            high_a, high_b, grad_half = tied(high_a, high_b, grad_half)
            half_a, half_b = (low_a, high_a), (low_b, high_b)
            both = relative_sum([sum_half, grad_half], graph_bits[1:])
        if place > 0:
            a, b = jnp.concatenate(half_a, axis=0), jnp.concatenate(half_b, axis=0)
    summed, grad_rows = both

    two_shape = (2, two * width, two * width)
    one_shape = (2, one * width, one * width)
    (grad_two,) = call(
        functools.partial(finish_two_kernel, block, stages_a),
        (shaped(two_shape, F32),),
        [*half_a],
        [pltpu.VMEM(two_shape, F32), whole_list],
        copies=2,
        moved=6 * rows_two * width,
    )
    grad_one, grad_zero, grad_gate = call(
        functools.partial(finish_kernel, block, rows_two, rows_one, stages_a, stages_b),
        (shaped(one_shape, F32), shaped((side, side), F32), shaped((width, width), F32)),
        [*half_a, *half_b],
        [pltpu.VMEM(one_shape, F32), square, pltpu.VMEM((width, width), F32), whole_list],
        copies=4,
        moved=12 * rows_one * width,
    )
    return (summed[None], grad_rows[None], grad_zero, grad_one, grad_two, grad_gate)


def solution(mesh):
    in_specs = (
        P("dp", "graph", None),
        P("dp", "graph"),
        P("dp", "graph"),
        P("dp", "graph"),
        P("dp", None, None, "graph"),
        P("dp", "graph", None),
        P("dp", "graph", None),
        P(),
        P(),
        P(),
        P(),
    )
    out_specs = (P("dp", "graph", None), P("dp", "graph", None), P(), P(), P(), P())
    return jax.shard_map(
        per_device, mesh=mesh, in_specs=in_specs, out_specs=out_specs, check_vma=False
    )
```

time: 264 us -> 155 us (0.59)
  local copies, waits for them, and re-layouts: 43.7 us -> 7.28 us
  waiting for transfers between devices: 97.3 us -> 66.1 us
  between operations: 16.7 us -> 1.88 us
  Pallas kernels: 54 us -> 42.3 us
  other arithmetic: 11.1 us -> 2.91 us
  starting transfers between devices: 40.8 us -> 34.2 us
    psum x1 -> x0, waiting for transfers between devices: 25.9 us -> none  [per_device(): late = lax.psum(late, ('dp', 'graph'))]
    unnamed x79 -> x33, local copies, waits for them, and re-layouts: 29.8 us -> 6.94 us
    pallas_call x10 -> x9, Pallas kernels: 54 us -> 42.3 us  [call(): pl.pallas_call(kernel, out_shape=out_shape, in_specs=[SMEM] * smem + [ANY...]
    concatenate x6 -> x1, local copies, waits for them, and re-layouts: 7.21 us -> 0.03 us  [per_device(): jnp.concatenate([ab[:half], other[:half], ab[half:], other[half:]], axis=0)]
    ppermute x34 -> x25, starting transfers between devices: 40.5 us -> 34.2 us  [exchange(): return lax.ppermute(value, axis, [(i, i ^ bit) for i in range(count)])]
    slice x17 -> x14, local copies, waits for them, and re-layouts: 6.58 us -> 0.32 us  [the longest x8 0.19 us: per_device(): a, sent_a, b, sent_b = (a[:half], a[half:], b[:half], b[half:])]
    ppermute x34 -> x25, waiting for transfers between devices: 71.4 us -> 66.1 us  [exchange(): return lax.ppermute(value, axis, [(i, i ^ bit) for i in range(count)])]
    convert_element_type x12 -> x9, other arithmetic: 6.31 us -> 1.63 us  [add_low(): return (kept.astype(F32) + other.astype(F32)).astype(BF16)]
  transfers between devices with their start and end apart: 37 -> 25, of which waited for: 19 -> 15; matrix products, arithmetic and copies ran while one was open for 16% -> 1% of each run, Pallas kernels for 18% -> 21%
where the time goes in v2:
time: 155 us
  waiting for transfers between devices  66.1 us (43%)
  Pallas kernels  42.3 us (27%)
  starting transfers between devices  34.2 us (22%)
  local copies, waits for them, and re-layouts  7.28 us (5%)
  other arithmetic  2.91 us (2%)
  between operations  1.88 us (1%)
    ppermute x25, waiting for transfers between devices, exchange(): return lax.ppermute(value, axis, [(i, i ^ bit) for i in range(count)])  66.1 us
    pallas_call x9, Pallas kernels, call(): pl.pallas_call(kernel, out_shape=out_shape, in_specs=[SMEM] * smem + [ANY...  42.3 us
    ppermute x25, starting transfers between devices, exchange(): return lax.ppermute(value, axis, [(i, i ^ bit) for i in range(count)])  34.2 us
    unnamed x33, local copies, waits for them, and re-layouts  6.94 us
  transfers between devices with their start and end apart: 25, of which 15 were waited for; matrix products, arithmetic and copies ran while one was open for 1% of the time, Pallas kernels for 21%

profile of v2, /device:TPU:0, one launch (start us, length us, event | category | flops | bytes accessed | tf_op | source)
XLA Modules:
  0.0 154.6 jit_solution(12204140593941859408)
XLA Ops:
  0.6 4.1 %collective-permute-start = (bf16[16,6272]{1,0:T(8,128)(2,1)}, bf16[16,6272]{1,0:T(8,128)(2,1)S(1)}, u32[]{:S(2)}, u32[]{:S(2)}) collective-permute-start(bf16[16,6272]{1,0:T(8,128)(2,1)} %bitcast.18), channel_id=1, source_target_pairs={{0,2},{1,3},{2,0},{3,1},{4,6},{5,7},{6,4},{7,5},{8,10},{9,11},{10,... | collective-permute-start | bytes 602120 | tf_op jit(solution)/shard_map/ppermute | solution.py:417
  13.5 2.5 %shard_map.154 = (f32[49,29,512]{2,1,0:T(8,128)S(1)}, f32[128,512]{1,0:T(8,128)S(1)}, bf16[896,896]{1,0:T(8,128)(2,1)S(1)}, bf16[2,768,768]{2,1,0:T(8,128)(2,1)S(1)}, bf16[2,640,640]{2,1,0:T(8,128)(2,1)S(1)}) custom-call(bf16[49,29,512]{2,1,0:T(8,128)(2,1)S(1)} %bitcast.13, bf16[896,896]{1,0:T(8,128)(2,1)S(1)} %copy-done.5, ...), custom_call_target="tpu_custom_call" | custom-call | bytes 15421440 | tf_op jit(solution)/shard_map/pallas_call | solution.py:398
  18.8 4.2 %collective-permute-done.1.refs_1_ = bf16[16,6272]{1,0:T(8,128)(2,1)S(1)} collective-permute-done((bf16[16,6272]{1,0:T(8,128)(2,1)}, bf16[16,6272]{1,0:T(8,128)(2,1)S(1)}, u32[]{:S(2)}, u32[]{:S(2)}) %collective-permute-start.1) | collective-permute-done | bytes 200736 | tf_op jit(solution)/shard_map/ppermute | solution.py:417
  23.7 3.4 %collective-permute-done.3.refs_3_ = bf16[16,6272]{1,0:T(8,128)(2,1)S(1)} collective-permute-done((bf16[16,6272]{1,0:T(8,128)(2,1)S(1)}, bf16[16,6272]{1,0:T(8,128)(2,1)S(1)}, u32[]{:S(2)}, u32[]{:S(2)}) %collective-permute-start.3) | collective-permute-done | bytes 200736 | tf_op jit(solution)/shard_map/ppermute | solution.py:417
  27.2 3.1 %shard_map.155 = (bf16[896,512]{1,0:T(8,128)(2,1)S(1)}, bf16[1536,512]{1,0:T(8,128)(2,1)S(1)}, bf16[1280,512]{1,0:T(8,128)(2,1)S(1)}, f32[128,512]{1,0:T(8,128)S(1)}, f32[128,512]{1,0:T(8,128)S(1)}) custom-call(s32[1,512]{1,0:T(1,128)S(1)} %copy-done.12, f32[49,29,512]{2,1,0:T(8,128)S(1)} %get-tuple-element.68.wide, f32[128,512]{1,0:T(8,128)S(1)} %get-tuple-element.69.scale, ...), custom_call_target="tpu_custom_call" | custom-call | flops 2055208960 | bytes 7602176 | tf_op jit(solution)/shard_map/pallas_call | solution.py:398
  30.3 5.6 %shard_map.156 = (bf16[896,512]{1,0:T(8,128)(2,1)S(1)}, bf16[1536,512]{1,0:T(8,128)(2,1)S(1)}, bf16[1280,512]{1,0:T(8,128)(2,1)S(1)}, bf16[7,128,2560]{2,1,0:T(8,128)(2,1)S(1)}) custom-call(bf16[896,512]{1,0:T(8,128)(2,1)S(1)} %get-tuple-element.76.x_zero, bf16[1536,512]{1,0:T(8,128)(2,1)S(1)} %get-tuple-element.77.x_one, ...), custom_call_target="tpu_custom_call" | custom-call | flops 4915724288 | bytes 11403264 | tf_op jit(solution)/shard_map/pallas_call | solution.py:398
  35.9 3.5 %shard_map.157 = (bf16[896,512]{1,0:T(8,128)(2,1)S(1)}, bf16[1536,512]{1,0:T(8,128)(2,1)S(1)}, bf16[1280,512]{1,0:T(8,128)(2,1)S(1)}, bf16[128,512]{1,0:T(8,128)(2,1)S(1)}) custom-call(s32[1]{0:T(128)} %bitcast.11.live, s32[1,512]{1,0:T(1,128)S(1)} %copy-done.10, f32[49,29,512]{2,1,0:T(8,128)S(1)} %get-tuple-element.68.wide, ...), custom_call_target="tpu_custom_call" | custom-call | flops 2055208960 | bytes 7602176 | tf_op jit(solution)/shard_map/pallas_call | solution.py:398
  39.5 2.9 %shard_map.159 = (bf16[5632,128]{1,0:T(8,128)(2,1)S(1)}, bf16[5632,128]{1,0:T(8,128)(2,1)S(1)}) custom-call(bf16[1536,512]{1,0:T(8,128)(2,1)S(1)} %get-tuple-element.77.x_one, bf16[1536,512]{1,0:T(8,128)(2,1)S(1)} %get-tuple-element.86.g_one, bf16[896,512]{1,0:T(8,128)(2,1)S(1)} %get-tuple-element.76.x_zero, bf16[896,512]{1,0:T(8,128)(2,1)S(1)} %get-tuple-element.89.g_zero, ...), custom_call_target="tpu_custom_call" | custom-call | flops 2457862144 | bytes 5767168 | tf_op jit(solution)/shard_map/pallas_call | solution.py:398
  42.5 3.8 %shard_map.158 = (bf16[5632,128]{1,0:T(8,128)(2,1)S(1)}, bf16[5632,128]{1,0:T(8,128)(2,1)S(1)}) custom-call(bf16[1280,512]{1,0:T(8,128)(2,1)S(1)} %get-tuple-element.73.x_two, bf16[1280,512]{1,0:T(8,128)(2,1)S(1)} %get-tuple-element.85.g_two, bf16[1536,512]{1,0:T(8,128)(2,1)S(1)} %get-tuple-element.77.x_one, bf16[1536,512]{1,0:T(8,128)(2,1)S(1)} %get-tuple-element.86.g_one), custom_call_target="tpu_custom_call" | custom-call | flops 2457862144 | bytes 5767168 | tf_op jit(solution)/shard_map/pallas_call | solution.py:398
  47.2 2.5 %collective-permute-done.6 = bf16[5632,128]{1,0:T(8,128)(2,1)S(1)} collective-permute-done((bf16[5632,128]{1,0:T(8,128)(2,1)S(1)}, bf16[5632,128]{1,0:T(8,128)(2,1)S(1)}, u32[]{:S(2)}, u32[]{:S(2)}) %collective-permute-start.6) | collective-permute-done | bytes 1441824 | tf_op jit(solution)/shard_map/ppermute | solution.py:417
  53.8 15.2 %shard_map.160 = (bf16[32,6272]{1,0:T(8,128)(2,1)S(1)}, bf16[32,6272]{1,0:T(8,128)(2,1)S(1)}, bf16[32,6272]{1,0:T(8,128)(2,1)S(1)}, bf16[32,6272]{1,0:T(8,128)(2,1)S(1)}) custom-call(s32[1]{0:T(128)} %bitcast.12.live, bf16[896,896]{1,0:T(8,128)(2,1)S(1)} %copy-done.6, bf16[2,768,768]{2,1,0:T(8,128)(2,1)S(1)} %copy-done.1, ...), custom_call_target="tpu_custom_call" | custom-call | flops 9026142208 | bytes 15204352 | tf_op jit(solution)/shard_map/pallas_call | solution.py:398
  73.1 7.8 %collective-permute-done.12 = bf16[32,6272]{1,0:T(8,128)(2,1)S(1)} collective-permute-done((bf16[32,6272]{1,0:T(8,128)(2,1)S(1)}, bf16[32,6272]{1,0:T(8,128)(2,1)S(1)}, u32[]{:S(2)}, u32[]{:S(2)}) %collective-permute-start.12) | collective-permute-done | bytes 401440 | tf_op jit(solution)/shard_map/ppermute | solution.py:417
  83.0 7.0 %collective-permute-done.13 = bf16[1408,128]{1,0:T(8,128)(2,1)S(1)} collective-permute-done((bf16[1408,128]{1,0:T(8,128)(2,1)S(1)}, bf16[1408,128]{1,0:T(8,128)(2,1)S(1)}, u32[]{:S(2)}, u32[]{:S(2)}) %collective-permute-start.13) | collective-permute-done | bytes 360480 | tf_op jit(solution)/shard_map/ppermute | solution.py:417
  92.4 6.4 %collective-permute-done.14 = bf16[704,128]{1,0:T(8,128)(2,1)S(1)} collective-permute-done((bf16[704,128]{1,0:T(8,128)(2,1)S(1)}, bf16[704,128]{1,0:T(8,128)(2,1)S(1)}, u32[]{:S(2)}, u32[]{:S(2)}) %collective-permute-start.14) | collective-permute-done | bytes 180256 | tf_op jit(solution)/shard_map/ppermute | solution.py:417
  99.0 6.3 %collective-permute-done.15 = bf16[704,128]{1,0:T(8,128)(2,1)S(1)} collective-permute-done((bf16[704,128]{1,0:T(8,128)(2,1)S(1)}, bf16[704,128]{1,0:T(8,128)(2,1)S(1)}, u32[]{:S(2)}, u32[]{:S(2)}) %collective-permute-start.15) | collective-permute-done | bytes 180256 | tf_op jit(solution)/shard_map/ppermute | solution.py:417
  105.4 3.4 %collective-permute-start.16 = (bf16[1408,128]{1,0:T(8,128)(2,1)S(1)}, bf16[1408,128]{1,0:T(8,128)(2,1)S(1)}, u32[]{:S(2)}, u32[]{:S(2)}) collective-permute-start(bf16[1408,128]{1,0:T(8,128)(2,1)S(1)} %pad_maximum_fusion.6), channel_id=1, source_target_pairs={{0,1},{1,0},{2,3},{3,2},{4,5},{5,4},{6,7},{7,6},{8,9},{9,8},{10,11... | collective-permute-start | bytes 1081352 | tf_op jit(solution)/shard_map/ppermute | solution.py:417
  108.8 7.7 %collective-permute-done.16 = bf16[1408,128]{1,0:T(8,128)(2,1)S(1)} collective-permute-done((bf16[1408,128]{1,0:T(8,128)(2,1)S(1)}, bf16[1408,128]{1,0:T(8,128)(2,1)S(1)}, u32[]{:S(2)}, u32[]{:S(2)}) %collective-permute-start.16) | collective-permute-done | bytes 360480 | tf_op jit(solution)/shard_map/ppermute | solution.py:417
  116.7 2.4 %collective-permute-start.19 = (bf16[32,6272]{1,0:T(8,128)(2,1)S(1)}, bf16[32,6272]{1,0:T(8,128)(2,1)S(1)}, u32[]{:S(2)}, u32[]{:S(2)}) collective-permute-start(bf16[32,6272]{1,0:T(8,128)(2,1)S(1)} %get-tuple-element.113), channel_id=1, source_target_pairs={{0,1},{1,0},{2,3},{3,2},{4,5},{5,4},{6,7},{7,6},{8,9},{9,8},{10,11... | collective-permute-start | bytes 1204232 | tf_op jit(solution)/shard_map/ppermute | solution.py:417
  120.3 2.4 %collective-permute-start.18 = (bf16[1408,128]{1,0:T(8,128)(2,1)S(1)}, bf16[1408,128]{1,0:T(8,128)(2,1)S(1)}, u32[]{:S(2)}, u32[]{:S(2)}) collective-permute-start(bf16[1408,128]{1,0:T(8,128)(2,1)S(1)} %get-tuple-element.122), channel_id=1, source_target_pairs={{0,8},{4,12},{8,0},{12,4},{16,24},{20,28},{24,16},{28,20},{1,9},{5... | collective-permute-start | bytes 1081352 | tf_op jit(solution)/shard_map/ppermute | solution.py:417
  125.0 3.6 %collective-permute-done.17 = bf16[1408,128]{1,0:T(8,128)(2,1)S(1)} collective-permute-done((bf16[1408,128]{1,0:T(8,128)(2,1)S(1)}, bf16[1408,128]{1,0:T(8,128)(2,1)S(1)}, u32[]{:S(2)}, u32[]{:S(2)}) %collective-permute-start.17) | collective-permute-done | bytes 360480 | tf_op jit(solution)/shard_map/ppermute | solution.py:417
  128.6 3.4 %collective-permute-done.18 = bf16[1408,128]{1,0:T(8,128)(2,1)S(1)} collective-permute-done((bf16[1408,128]{1,0:T(8,128)(2,1)S(1)}, bf16[1408,128]{1,0:T(8,128)(2,1)S(1)}, u32[]{:S(2)}, u32[]{:S(2)}) %collective-permute-start.18) | collective-permute-done | bytes 360480 | tf_op jit(solution)/shard_map/ppermute | solution.py:417
  134.8 2.6 %collective-permute-start.20 = (bf16[32,6272]{1,0:T(8,128)(2,1)S(1)}, bf16[32,6272]{1,0:T(8,128)(2,1)S(1)}, u32[]{:S(2)}, u32[]{:S(2)}) collective-permute-start(bf16[32,6272]{1,0:T(8,128)(2,1)S(1)} %pad_maximum_fusion.4), channel_id=1, source_target_pairs={{0,2},{1,3},{2,0},{3,1},{4,6},{5,7},{6,4},{7,5},{8,10},{9,11},{10,... | collective-permute-start | bytes 1204232 | tf_op jit(solution)/shard_map/ppermute | solution.py:417
  137.3 6.1 %collective-permute-done.21 = bf16[2816,128]{1,0:T(8,128)(2,1)S(1)} collective-permute-done((bf16[2816,128]{1,0:T(8,128)(2,1)S(1)}, bf16[2816,128]{1,0:T(8,128)(2,1)S(1)}, u32[]{:S(2)}, u32[]{:S(2)}) %collective-permute-start.21) | collective-permute-done | bytes 720928 | tf_op jit(solution)/shard_map/ppermute | solution.py:417
  150.8 3.7 %shard_map.161 = (f32[2,768,768]{2,1,0:T(8,128)}, f32[896,896]{1,0:T(8,128)}, f32[128,128]{1,0:T(8,128)}) custom-call(bf16[5632,128]{1,0:T(8,128)(2,1)S(1)} %pad_maximum_fusion.low_a.low, bf16[5632,128]{1,0:T(8,128)(2,1)S(1)} %collective-permute-done.22.high_a.high, bf16[5632,128]{1,0:T(8,128)(2,1)S(1)} %pad_maximum_fusion.1.low_b, ...), custom_call_target="tpu_custom_call" | custom-call | bytes 7077888 | tf_op jit(solution)/shard_map/pallas_call | solution.py:398
  (103 shorter events, 39.0 us)
Async XLA Ops:
  0.6 15.4 %collective-permute-start = (bf16[16,6272]{1,0:T(8,128)(2,1)}, bf16[16,6272]{1,0:T(8,128)(2,1)S(1)}, u32[]{:S(2)}, u32[]{:S(2)}) collective-permute-start(bf16[16,6272]{1,0:T(8,128)(2,1)} %bitcast.18), channel_id=1, source_target_pairs={{0,2},{1,3},{2,0},{3,1},{4,6},{5,7},{6,4},{7,5},{8,10},{9,11},{10,... | collective-permute-start | bytes 602120 | tf_op jit(solution)/shard_map/ppermute | solution.py:417
  4.7 19.0 %collective-permute-start.2 = (bf16[16,6272]{1,0:T(8,128)(2,1)}, bf16[16,6272]{1,0:T(8,128)(2,1)S(1)}, u32[]{:S(2)}, u32[]{:S(2)}) collective-permute-start(bf16[16,6272]{1,0:T(8,128)(2,1)} %bitcast.19), channel_id=1, source_target_pairs={{0,1},{1,0},{2,3},{3,2},{4,5},{5,4},{6,7},{7,6},{8,9},{9,8},{10,11... | collective-permute-start | bytes 602120 | tf_op jit(solution)/shard_map/ppermute | solution.py:417
  6.3 16.7 %collective-permute-start.1 = (bf16[16,6272]{1,0:T(8,128)(2,1)}, bf16[16,6272]{1,0:T(8,128)(2,1)S(1)}, u32[]{:S(2)}, u32[]{:S(2)}) collective-permute-start(bf16[16,6272]{1,0:T(8,128)(2,1)} %bitcast.14), channel_id=1, source_target_pairs={{0,2},{1,3},{2,0},{3,1},{4,6},{5,7},{6,4},{7,5},{8,10},{9,11},{10,... | collective-permute-start | bytes 602120 | tf_op jit(solution)/shard_map/ppermute | solution.py:417
  16.0 11.1 %collective-permute-start.3 = (bf16[16,6272]{1,0:T(8,128)(2,1)S(1)}, bf16[16,6272]{1,0:T(8,128)(2,1)S(1)}, u32[]{:S(2)}, u32[]{:S(2)}) collective-permute-start(bf16[16,6272]{1,0:T(8,128)(2,1)S(1)} %collective-permute-done.refs_1_), channel_id=1, source_target_pairs={{0,1},{1,0},{2,3},{3,2},{4,5},{5,4},{6,7},{7,6},{8,9},{9,8},{10,11... | collective-permute-start | bytes 602120 | tf_op jit(solution)/shard_map/ppermute | solution.py:417
  16.3 19.6 %collective-permute-start.4 = (bf16[16,6272]{1,0:T(8,128)(2,1)S(1)}, bf16[16,6272]{1,0:T(8,128)(2,1)S(1)}, u32[]{:S(2)}, u32[]{:S(2)}) collective-permute-start(bf16[16,6272]{1,0:T(8,128)(2,1)S(1)} %bitcast.15), channel_id=1, source_target_pairs={{0,1},{1,0},{2,3},{3,2},{4,5},{5,4},{6,7},{7,6},{8,9},{9,8},{10,11... | collective-permute-start | bytes 602120 | tf_op jit(solution)/shard_map/ppermute | solution.py:417
  23.0 12.9 %collective-permute-start.5 = (bf16[16,6272]{1,0:T(8,128)(2,1)S(1)}, bf16[16,6272]{1,0:T(8,128)(2,1)S(1)}, u32[]{:S(2)}, u32[]{:S(2)}) collective-permute-start(bf16[16,6272]{1,0:T(8,128)(2,1)S(1)} %collective-permute-done.1.refs_1_), channel_id=1, source_target_pairs={{0,1},{1,0},{2,3},{3,2},{4,5},{5,4},{6,7},{7,6},{8,9},{9,8},{10,11... | collective-permute-start | bytes 602120 | tf_op jit(solution)/shard_map/ppermute | solution.py:417
  42.4 4.4 %collective-permute-start.7 = (bf16[5632,128]{1,0:T(8,128)(2,1)S(1)}, bf16[5632,128]{1,0:T(8,128)(2,1)S(1)}, u32[]{:S(2)}, u32[]{:S(2)}) collective-permute-start(bf16[5632,128]{1,0:T(8,128)(2,1)S(1)} %get-tuple-element.92), channel_id=1, source_target_pairs={{0,4},{4,0},{8,12},{12,8},{16,20},{20,16},{24,28},{28,24},{1,5},{5... | collective-permute-start | bytes 4325384 | tf_op jit(solution)/shard_map/ppermute | solution.py:417
  50.1 19.0 %collective-permute-start.8 = (bf16[2816,128]{1,0:T(8,128)(2,1)S(1)}, bf16[2816,128]{1,0:T(8,128)(2,1)S(1)}, u32[]{:S(2)}, u32[]{:S(2)}) collective-permute-start(bf16[2816,128]{1,0:T(8,128)(2,1)S(1)} %slice.105), channel_id=1, source_target_pairs={{0,8},{4,12},{8,0},{12,4},{16,24},{20,28},{24,16},{28,20},{1,9},{5... | collective-permute-start | bytes 2162696 | tf_op jit(solution)/shard_map/ppermute | solution.py:417
  52.2 18.2 %collective-permute-start.9 = (bf16[2816,128]{1,0:T(8,128)(2,1)S(1)}, bf16[2816,128]{1,0:T(8,128)(2,1)S(1)}, u32[]{:S(2)}, u32[]{:S(2)}) collective-permute-start(bf16[2816,128]{1,0:T(8,128)(2,1)S(1)} %slice.106), channel_id=1, source_target_pairs={{0,16},{4,20},{8,24},{12,28},{16,0},{20,4},{24,8},{28,12},{1,17},{... | collective-permute-start | bytes 2162696 | tf_op jit(solution)/shard_map/ppermute | solution.py:417
  70.4 10.4 %collective-permute-start.12 = (bf16[32,6272]{1,0:T(8,128)(2,1)S(1)}, bf16[32,6272]{1,0:T(8,128)(2,1)S(1)}, u32[]{:S(2)}, u32[]{:S(2)}) collective-permute-start(bf16[32,6272]{1,0:T(8,128)(2,1)S(1)} %get-tuple-element.104), channel_id=1, source_target_pairs={{0,1},{1,0},{2,3},{3,2},{4,5},{5,4},{6,7},{7,6},{8,9},{9,8},{10,11... | collective-permute-start | bytes 1204232 | tf_op jit(solution)/shard_map/ppermute | solution.py:417
  70.7 10.3 %collective-permute-start.11 = (bf16[1408,128]{1,0:T(8,128)(2,1)S(1)}, bf16[1408,128]{1,0:T(8,128)(2,1)S(1)}, u32[]{:S(2)}, u32[]{:S(2)}) collective-permute-start(bf16[1408,128]{1,0:T(8,128)(2,1)S(1)} %slice.138), channel_id=1, source_target_pairs={{0,8},{4,12},{8,0},{12,4},{16,24},{20,28},{24,16},{28,20},{1,9},{5... | collective-permute-start | bytes 1081352 | tf_op jit(solution)/shard_map/ppermute | solution.py:417
  71.3 9.7 %collective-permute-start.10 = (bf16[1408,128]{1,0:T(8,128)(2,1)S(1)}, bf16[1408,128]{1,0:T(8,128)(2,1)S(1)}, u32[]{:S(2)}, u32[]{:S(2)}) collective-permute-start(bf16[1408,128]{1,0:T(8,128)(2,1)S(1)} %slice.137), channel_id=1, source_target_pairs={{0,16},{4,20},{8,24},{12,28},{16,0},{20,4},{24,8},{28,12},{1,17},{... | collective-permute-start | bytes 1081352 | tf_op jit(solution)/shard_map/ppermute | solution.py:417
  81.3 8.7 %collective-permute-start.13 = (bf16[1408,128]{1,0:T(8,128)(2,1)S(1)}, bf16[1408,128]{1,0:T(8,128)(2,1)S(1)}, u32[]{:S(2)}, u32[]{:S(2)}) collective-permute-start(bf16[1408,128]{1,0:T(8,128)(2,1)S(1)} %pad_maximum_fusion.5), channel_id=1, source_target_pairs={{0,1},{1,0},{2,3},{3,2},{4,5},{5,4},{6,7},{7,6},{8,9},{9,8},{10,11... | collective-permute-start | bytes 1081352 | tf_op jit(solution)/shard_map/ppermute | solution.py:417
  90.1 8.7 %collective-permute-start.14 = (bf16[704,128]{1,0:T(8,128)(2,1)S(1)}, bf16[704,128]{1,0:T(8,128)(2,1)S(1)}, u32[]{:S(2)}, u32[]{:S(2)}) collective-permute-start(bf16[704,128]{1,0:T(8,128)(2,1)S(1)} %pad_maximum_fusion.7), channel_id=1, source_target_pairs={{0,2},{1,3},{2,0},{3,1},{4,6},{5,7},{6,4},{7,5},{8,10},{9,11},{10,... | collective-permute-start | bytes 540680 | tf_op jit(solution)/shard_map/ppermute | solution.py:417
  98.9 6.5 %collective-permute-start.15 = (bf16[704,128]{1,0:T(8,128)(2,1)S(1)}, bf16[704,128]{1,0:T(8,128)(2,1)S(1)}, u32[]{:S(2)}, u32[]{:S(2)}) collective-permute-start(bf16[704,128]{1,0:T(8,128)(2,1)S(1)} %pad_maximum_fusion.8), channel_id=1, source_target_pairs={{0,2},{1,3},{2,0},{3,1},{4,6},{5,7},{6,4},{7,5},{8,10},{9,11},{10,... | collective-permute-start | bytes 540680 | tf_op jit(solution)/shard_map/ppermute | solution.py:417
  105.4 11.1 %collective-permute-start.16 = (bf16[1408,128]{1,0:T(8,128)(2,1)S(1)}, bf16[1408,128]{1,0:T(8,128)(2,1)S(1)}, u32[]{:S(2)}, u32[]{:S(2)}) collective-permute-start(bf16[1408,128]{1,0:T(8,128)(2,1)S(1)} %pad_maximum_fusion.6), channel_id=1, source_target_pairs={{0,1},{1,0},{2,3},{3,2},{4,5},{5,4},{6,7},{7,6},{8,9},{9,8},{10,11... | collective-permute-start | bytes 1081352 | tf_op jit(solution)/shard_map/ppermute | solution.py:417
  116.7 8.2 %collective-permute-start.19 = (bf16[32,6272]{1,0:T(8,128)(2,1)S(1)}, bf16[32,6272]{1,0:T(8,128)(2,1)S(1)}, u32[]{:S(2)}, u32[]{:S(2)}) collective-permute-start(bf16[32,6272]{1,0:T(8,128)(2,1)S(1)} %get-tuple-element.113), channel_id=1, source_target_pairs={{0,1},{1,0},{2,3},{3,2},{4,5},{5,4},{6,7},{7,6},{8,9},{9,8},{10,11... | collective-permute-start | bytes 1204232 | tf_op jit(solution)/shard_map/ppermute | solution.py:417
  119.1 9.5 %collective-permute-start.17 = (bf16[1408,128]{1,0:T(8,128)(2,1)S(1)}, bf16[1408,128]{1,0:T(8,128)(2,1)S(1)}, u32[]{:S(2)}, u32[]{:S(2)}) collective-permute-start(bf16[1408,128]{1,0:T(8,128)(2,1)S(1)} %get-tuple-element.123), channel_id=1, source_target_pairs={{0,16},{4,20},{8,24},{12,28},{16,0},{20,4},{24,8},{28,12},{1,17},{... | collective-permute-start | bytes 1081352 | tf_op jit(solution)/shard_map/ppermute | solution.py:417
  120.3 11.7 %collective-permute-start.18 = (bf16[1408,128]{1,0:T(8,128)(2,1)S(1)}, bf16[1408,128]{1,0:T(8,128)(2,1)S(1)}, u32[]{:S(2)}, u32[]{:S(2)}) collective-permute-start(bf16[1408,128]{1,0:T(8,128)(2,1)S(1)} %get-tuple-element.122), channel_id=1, source_target_pairs={{0,8},{4,12},{8,0},{12,4},{16,24},{20,28},{24,16},{28,20},{1,9},{5... | collective-permute-start | bytes 1081352 | tf_op jit(solution)/shard_map/ppermute | solution.py:417
  132.1 11.4 %collective-permute-start.21 = (bf16[2816,128]{1,0:T(8,128)(2,1)S(1)}, bf16[2816,128]{1,0:T(8,128)(2,1)S(1)}, u32[]{:S(2)}, u32[]{:S(2)}) collective-permute-start(bf16[2816,128]{1,0:T(8,128)(2,1)S(1)} %pad_maximum_fusion.2), channel_id=1, source_target_pairs={{0,8},{4,12},{8,0},{12,4},{16,24},{20,28},{24,16},{28,20},{1,9},{5... | collective-permute-start | bytes 2162696 | tf_op jit(solution)/shard_map/ppermute | solution.py:417
  134.3 11.4 %collective-permute-start.23 = (bf16[2816,128]{1,0:T(8,128)(2,1)S(1)}, bf16[2816,128]{1,0:T(8,128)(2,1)S(1)}, u32[]{:S(2)}, u32[]{:S(2)}) collective-permute-start(bf16[2816,128]{1,0:T(8,128)(2,1)S(1)} %pad_maximum_fusion.3), channel_id=1, source_target_pairs={{0,16},{4,20},{8,24},{12,28},{16,0},{20,4},{24,8},{28,12},{1,17},{... | collective-permute-start | bytes 2162696 | tf_op jit(solution)/shard_map/ppermute | solution.py:417
  134.8 13.1 %collective-permute-start.20 = (bf16[32,6272]{1,0:T(8,128)(2,1)S(1)}, bf16[32,6272]{1,0:T(8,128)(2,1)S(1)}, u32[]{:S(2)}, u32[]{:S(2)}) collective-permute-start(bf16[32,6272]{1,0:T(8,128)(2,1)S(1)} %pad_maximum_fusion.4), channel_id=1, source_target_pairs={{0,2},{1,3},{2,0},{3,1},{4,6},{5,7},{6,4},{7,5},{8,10},{9,11},{10,... | collective-permute-start | bytes 1204232 | tf_op jit(solution)/shard_map/ppermute | solution.py:417
  143.6 5.2 %collective-permute-start.22 = (bf16[5632,128]{1,0:T(8,128)(2,1)S(1)}, bf16[5632,128]{1,0:T(8,128)(2,1)S(1)}, u32[]{:S(2)}, u32[]{:S(2)}) collective-permute-start(bf16[5632,128]{1,0:T(8,128)(2,1)S(1)} %pad_maximum_fusion.low_a.low), channel_id=1, source_target_pairs={{0,4},{4,0},{8,12},{12,8},{16,20},{20,16},{24,28},{28,24},{1,5},{5... | collective-permute-start | bytes 4325384 | tf_op jit(solution)/shard_map/ppermute | solution.py:417
  145.7 5.1 %collective-permute-start.24 = (bf16[5632,128]{1,0:T(8,128)(2,1)S(1)}, bf16[5632,128]{1,0:T(8,128)(2,1)S(1)}, u32[]{:S(2)}, u32[]{:S(2)}) collective-permute-start(bf16[5632,128]{1,0:T(8,128)(2,1)S(1)} %pad_maximum_fusion.1.low_b), channel_id=1, source_target_pairs={{0,4},{4,0},{8,12},{12,8},{16,20},{20,16},{24,28},{28,24},{1,5},{5... | collective-permute-start | bytes 4325384 | tf_op jit(solution)/shard_map/ppermute | solution.py:417
  (17 other events, 127.7 us)

commit v3 on v2

--- a/solution.py
+++ b/solution.py
@@ -336,52 +336,50 @@
     spread_back(sizes, hits, wide, (even, odd), values, grad_kept, grad_sent)
 
 
-def take_matrix(mine, joined, block, flat, rows, columns, out):
-    width = joined.shape[1]
-    for column in range(0, columns, width):
-        for at, step, index in runs(block, flat, rows):
-            start = pl.multiple_of(flat + at + ((index ^ mine) - index) * block, 16)
-            out[at : at + step, column : column + width] = joined[pl.ds(start, step), :].astype(F32)
-        flat += rows
-    return flat
-
-
-def join(low, high, joined):
-    rows = low.shape[0]
-    joined[0:rows, :] = low[...]
-    joined[rows:, :] = high[...]
-
-
-def finish_two_kernel(block, stages, low, high, result, out, joined, semaphores):
-    half = out.shape[1]
-    copies = Copies(semaphores)
-    join(low, high, joined)
-    flat, started = 0, []
-    for part in range(2):
-        flat = take_matrix(place_of(stages), joined, block, flat, half, half, out.at[part])
-        started += copies.start((out.at[part],), (result.at[part],))
-    wait(started)
-
-
-def finish_kernel(
-    block, skip_a, skip_b, stages_a, stages_b, low_a, high_a, low_b, high_b,
-    one_result, zero_result, gate_result, one, zero, gate, joined, semaphores
-):
-    half = one.shape[1]
-    copies = Copies(semaphores)
-    join(low_a, high_a, joined)
-    take_matrix(place_of(stages_a), joined, block, skip_a, half, half, one.at[0])
-    started = copies.start((one.at[0],), (one_result.at[0],))
-    join(low_b, high_b, joined)
-    mine = place_of(stages_b)
-    take_matrix(mine, joined, block, 0, half, half, one.at[1])
-    started += copies.start((one.at[1],), (one_result.at[1],))
-    side = zero.shape[0]
-    flat = take_matrix(mine, joined, block, skip_b, side, side, zero)
-    started += copies.start((zero,), (zero_result,))
-    take_matrix(mine, joined, block, flat, gate.shape[0], gate.shape[1], gate)
-    started += copies.start((gate,), (gate_result,))
-    wait(started)
+def finish_kernel(sizes, block_count, block, stages_a, stages_b, high, *refs):
+    if high:
+        refs = refs[4:]
+    rows_a, rows_b, grad_two, grad_one, grad_zero, grad_gate, wide_a, wide_b, semaphores = refs
+    width = rows_a.shape[1]
+    zero, one, two = sizes
+    list_a = [(grad_two.at[part], two, column) for part in range(2) for column in range(two)]
+    list_a += [(grad_one.at[0], one, column) for column in range(one)]
+    list_b = [(grad_one.at[1], one, column) for column in range(one)]
+    list_b += [(grad_zero, zero, column) for column in range(zero)] + [(grad_gate, 1, 0)]
+    axis, bit = stages_a[0]
+    first = jnp.where((lax.axis_index(axis) & bit) != 0, 1, 0)
+    half = block_count // 2
+
+    def write(copies, pieces, mine, rows, wide, low, high_end):
+        started, flat = [], 0
+        for target, size, column in pieces:
+            begin, end = max(flat, low), min(flat + size * width, high_end)
+            if begin < end:
+                for at, step, index in runs(block, begin, end - begin):
+                    place = (index ^ mine) - (half if high else 0)
+                    start = pl.multiple_of(place * block + (begin + at) % block, 16)
+                    to = begin + at - low
+                    wide[to : to + step, :] = rows[pl.ds(start, step), :].astype(F32)
+                started += copies.start(
+                    (wide.at[begin - low : end - low],),
+                    (
+                        target.at[
+                            begin - flat : end - flat, column * width : (column + 1) * width
+                        ],
+                    ),
+                )
+            flat += size * width
+        return started
+
+    for side in range(2):
+
+        @pl.when(first == (1 - side if high else side))
+        def _(side=side):
+            copies = Copies(semaphores)
+            low, end = side * half * block, (side + 1) * half * block
+            started = write(copies, list_a, place_of(stages_a), rows_a, wide_a, low, end)
+            started += write(copies, list_b, place_of(stages_b), rows_b, wide_b, low, end)
+            wait(started)
 
 
 SMEM = pl.BlockSpec(memory_space=pltpu.SMEM)
@@ -389,7 +387,9 @@
 ANY = pl.BlockSpec(memory_space=pl.ANY)
 
 
-def call(kernel, out_shape, args, scratch=(), smem=0, hbm=0, copies=0, flops=0, moved=0):
+def call(
+    kernel, out_shape, args, scratch=(), smem=0, hbm=0, copies=0, flops=0, moved=0, aliased=0
+):
     vmem = [pltpu.with_memory_space_constraint(a, pltpu.VMEM) for a in args[smem + hbm :]]
     held = sum(math.prod(a.shape) * jnp.dtype(a.dtype).itemsize for a in scratch)
     held += held // 8
@@ -401,6 +401,7 @@
         in_specs=[SMEM] * smem + [ANY] * hbm + [VMEM] * len(vmem),
         out_specs=tuple(ANY if isinstance(o, jax.ShapeDtypeStruct) else VMEM for o in out_shape),
         scratch_shapes=list(scratch),
+        input_output_aliases={i: i for i in range(aliased)},
         compiler_params=pltpu.CompilerParams(vmem_limit_bytes=held + SPARE_VMEM),
         cost_estimate=pl.CostEstimate(
             flops=int(flops), bytes_accessed=int(moved), transcendentals=0
@@ -422,14 +423,15 @@
     return [(axis, 1 << b) for b in range(count.bit_length() - 1)]
 
 
-def relative_gather(shards, beside):
-    order, held = [0], [[shard] for shard in shards]
-    for axis, bit in bits_of("graph")[::-1]:
-        held = [blocks + [exchange(block, axis, bit) for block in blocks] for blocks in held]
+def relative_gather(first, second, beside):
+    order, held, also = [0], [first], [second]
+    for place, (axis, bit) in enumerate(bits_of("graph")[::-1]):
+        if place == 1:
+            held[1], also[0], *beside = tied(held[1], also[0], *beside)
+        held = held + [exchange(block, axis, bit) for block in (first, *held[1:])]
+        also = also + [exchange(block, axis, bit) for block in also]
         order = order + [o ^ bit for o in order]
-        if len(order) == 2:
-            held[0][1], *beside = tied(held[0][1], *beside)
-    return held, order, beside
+    return held, also, order, beside
 
 
 def relative_sum(arrays, stages):
@@ -494,11 +496,10 @@
         copies=4,
         moved=rotation.size * 8 + edge_flops / edges,
     )
-    (node_blocks, upstream_blocks), order, prepared = relative_gather(
-        (nodes[0], cotangent[0]), prepared
+    node_blocks, upstream_blocks, order, prepared = relative_gather(
+        nodes[0], cotangent[0], prepared
     )
     wide, scale, *turned = prepared
-    node_blocks[0], *upstream_blocks[:2] = tied(node_blocks[0], *upstream_blocks[:2])
     x_zero, x_one, x_two, scalar, gate = call(
         functools.partial(nodes_kernel, sizes, order),
         (*wide_rows, edge_block, edge_block),
@@ -507,6 +508,7 @@
         flops=turn_cost,
         moved=4 * sum(rows) * edges,
     )
+    gate, *upstream_blocks[:2] = tied(gate, *upstream_blocks[:2])
     m_zero, m_one, m_two, messages = call(
         functools.partial(products_kernel, sizes),
         (*wide_rows, values_shape),
@@ -562,11 +564,7 @@
         if place > 0:
             half = a.shape[0] // 2
             a, sent_a, b, sent_b = a[:half], a[half:], b[:half], b[half:]
-        if place <= last:
-            other_a, other_b = exchange(sent_a, *stage_a), exchange(sent_b, *stage_b)
-        else:
-            other = exchange(jnp.concatenate([sent_a, sent_b], axis=0), *stage_a)
-            other_a, other_b = other[:half], other[half:]
+        other_a, other_b = exchange(sent_a, *stage_a), exchange(sent_b, *stage_b)
         if place == 0:
             a, b = add_low(a, other_a), add_low(b, other_b)
             a, b, messages = tied(a, b, messages)
@@ -593,45 +591,42 @@
         if place == last:
             other_a, other_b, sum_half = tied(other_a, other_b, sum_half)
         a, b = add_low(a, other_a), add_low(b, other_b)
-    ab = jnp.concatenate([a, b], axis=0)
-    for stage in stages_a[:last:-1]:
-        half = ab.shape[0] // 2
-        other = exchange(ab, *stage)
-        ab = jnp.concatenate([ab[:half], other[:half], ab[half:], other[half:]], axis=0)
-    ab, grad_kept, grad_sent, sum_half = tied(ab, grad_kept, grad_sent, sum_half)
-    grad_half = add_low(grad_kept, exchange(grad_sent, *graph_bits[0]))
-    half = ab.shape[0] // 2
-    a, b = ab[:half], ab[half:]
-    for place in range(len(dp_bits))[::-1]:
+    for place in range(len(stages_a))[::-1]:
         half_a = (a, exchange(a, *stages_a[place]))
         half_b = (b, exchange(b, *stages_b[place]))
+        if place == last + 2:
+            (low_a, high_a), (low_b, high_b) = half_a, half_b
+            high_a, high_b, grad_kept, grad_sent = tied(high_a, high_b, grad_kept, grad_sent)
+            half_a, half_b = (low_a, high_a), (low_b, high_b)
+            grad_half = add_low(grad_kept, exchange(grad_sent, *graph_bits[0]))
         if place == last:
             (low_a, high_a), (low_b, high_b) = half_a, half_b
-            high_a, high_b, grad_half = tied(high_a, high_b, grad_half)
+            high_a, high_b, sum_half, grad_half = tied(high_a, high_b, sum_half, grad_half)
             half_a, half_b = (low_a, high_a), (low_b, high_b)
-            both = relative_sum([sum_half, grad_half], graph_bits[1:])
+            summed, grad_rows = relative_sum([sum_half, grad_half], graph_bits[1:])
         if place > 0:
             a, b = jnp.concatenate(half_a, axis=0), jnp.concatenate(half_b, axis=0)
-    summed, grad_rows = both
-
-    two_shape = (2, two * width, two * width)
-    one_shape = (2, one * width, one * width)
-    (grad_two,) = call(
-        functools.partial(finish_two_kernel, block, stages_a),
-        (shaped(two_shape, F32),),
-        [*half_a],
-        [pltpu.VMEM(two_shape, F32), whole_list],
-        copies=2,
-        moved=6 * rows_two * width,
-    )
-    grad_one, grad_zero, grad_gate = call(
-        functools.partial(finish_kernel, block, rows_two, rows_one, stages_a, stages_b),
-        (shaped(one_shape, F32), shaped((side, side), F32), shaped((width, width), F32)),
-        [*half_a, *half_b],
-        [pltpu.VMEM(one_shape, F32), square, pltpu.VMEM((width, width), F32), whole_list],
-        copies=4,
-        moved=12 * rows_one * width,
-    )
+
+    shapes = (
+        shaped((2, two * width, two * width), F32),
+        shaped((2, one * width, one * width), F32),
+        shaped((side, side), F32),
+        shaped((width, width), F32),
+    )
+    half_wide = pltpu.VMEM((blocks * block // 2, width), F32)
+    grads = ()
+    for high, halves in ((False, (half_a[0], half_b[0])), (True, (half_a[1], half_b[1]))):
+        grads = call(
+            functools.partial(finish_kernel, sizes, blocks, block, stages_a, stages_b, high),
+            shapes,
+            [*grads, *halves],
+            [half_wide, half_wide],
+            hbm=len(grads),
+            aliased=len(grads),
+            copies=2 * two + 2 * one + zero + 3,
+            moved=6 * blocks * block * width,
+        )
+    grad_two, grad_one, grad_zero, grad_gate = grads
     return (summed[None], grad_rows[None], grad_zero, grad_one, grad_two, grad_gate)
 
 

time: 155 us -> 149 us (0.961)
  waiting for transfers between devices: 66.1 us -> 61.4 us
    ppermute x25 -> x29, waiting for transfers between devices: 66.1 us -> 61.4 us  [exchange(): return lax.ppermute(value, axis, [(i, i ^ bit) for i in range(count)])]
    ppermute x25 -> x29, starting transfers between devices: 34.2 us -> 33 us  [exchange(): return lax.ppermute(value, axis, [(i, i ^ bit) for i in range(count)])]
    unnamed x33 -> x31, local copies, waits for them, and re-layouts: 6.94 us -> 7.04 us
  transfers between devices with their start and end apart: 25 -> 29, of which waited for: 15 -> 19; matrix products, arithmetic and copies ran while one was open for 1% -> 2% of each run, Pallas kernels for 21% -> 21%
where the time goes in v3:
time: 149 us
  waiting for transfers between devices  61.4 us (41%)
  Pallas kernels  42.1 us (28%)
  starting transfers between devices  33 us (22%)
  local copies, waits for them, and re-layouts  7.47 us (5%)
  other arithmetic  2.94 us (2%)
  between operations  1.89 us (1%)
    ppermute x29, waiting for transfers between devices, exchange(): return lax.ppermute(value, axis, [(i, i ^ bit) for i in range(count)])  61.4 us
    pallas_call x9, Pallas kernels, call(): pl.pallas_call(kernel, out_shape=out_shape, in_specs=[SMEM] * smem + [ANY...  42.1 us
    ppermute x29, starting transfers between devices, exchange(): return lax.ppermute(value, axis, [(i, i ^ bit) for i in range(count)])  33 us
    unnamed x31, local copies, waits for them, and re-layouts  7.04 us
  transfers between devices with their start and end apart: 29, of which 19 were waited for; matrix products, arithmetic and copies ran while one was open for 2% of the time, Pallas kernels for 21%

profile of v3, /device:TPU:0, one launch (start us, length us, event | category | flops | bytes accessed | tf_op | source)
XLA Modules:
  0.0 148.9 jit_solution(17795345048931615650)
XLA Ops:
  0.6 4.1 %collective-permute-start = (bf16[16,6272]{1,0:T(8,128)(2,1)}, bf16[16,6272]{1,0:T(8,128)(2,1)S(1)}, u32[]{:S(2)}, u32[]{:S(2)}) collective-permute-start(bf16[16,6272]{1,0:T(8,128)(2,1)} %bitcast.18), channel_id=1, source_target_pairs={{0,2},{1,3},{2,0},{3,1},{4,6},{5,7},{6,4},{7,5},{8,10},{9,11},{10,... | collective-permute-start | bytes 602120 | tf_op jit(solution)/shard_map/ppermute | solution.py:418
  13.5 2.5 %shard_map.154 = (f32[49,29,512]{2,1,0:T(8,128)S(1)}, f32[128,512]{1,0:T(8,128)S(1)}, bf16[896,896]{1,0:T(8,128)(2,1)S(1)}, bf16[2,768,768]{2,1,0:T(8,128)(2,1)S(1)}, bf16[2,640,640]{2,1,0:T(8,128)(2,1)S(1)}) custom-call(bf16[49,29,512]{2,1,0:T(8,128)(2,1)S(1)} %bitcast.13, bf16[896,896]{1,0:T(8,128)(2,1)S(1)} %copy-done.5, ...), custom_call_target="tpu_custom_call" | custom-call | bytes 15421440 | tf_op jit(solution)/shard_map/pallas_call | solution.py:398
  18.9 4.1 %collective-permute-done.3.refs_1_ = bf16[16,6272]{1,0:T(8,128)(2,1)S(1)} collective-permute-done((bf16[16,6272]{1,0:T(8,128)(2,1)}, bf16[16,6272]{1,0:T(8,128)(2,1)S(1)}, u32[]{:S(2)}, u32[]{:S(2)}) %collective-permute-start.3) | collective-permute-done | bytes 200736 | tf_op jit(solution)/shard_map/ppermute | solution.py:418
  23.7 3.4 %collective-permute-done.2.refs_3_ = bf16[16,6272]{1,0:T(8,128)(2,1)S(1)} collective-permute-done((bf16[16,6272]{1,0:T(8,128)(2,1)S(1)}, bf16[16,6272]{1,0:T(8,128)(2,1)S(1)}, u32[]{:S(2)}, u32[]{:S(2)}) %collective-permute-start.2) | collective-permute-done | bytes 200736 | tf_op jit(solution)/shard_map/ppermute | solution.py:418
  27.2 3.1 %shard_map.155 = (bf16[896,512]{1,0:T(8,128)(2,1)S(1)}, bf16[1536,512]{1,0:T(8,128)(2,1)S(1)}, bf16[1280,512]{1,0:T(8,128)(2,1)S(1)}, f32[128,512]{1,0:T(8,128)S(1)}, f32[128,512]{1,0:T(8,128)S(1)}) custom-call(s32[1,512]{1,0:T(1,128)S(1)} %copy-done.12, f32[49,29,512]{2,1,0:T(8,128)S(1)} %get-tuple-element.75.wide, f32[128,512]{1,0:T(8,128)S(1)} %get-tuple-element.76.scale, ...), custom_call_target="tpu_custom_call" | custom-call | flops 2055208960 | bytes 7602176 | tf_op jit(solution)/shard_map/pallas_call | solution.py:398
  30.3 5.6 %shard_map.156 = (bf16[896,512]{1,0:T(8,128)(2,1)S(1)}, bf16[1536,512]{1,0:T(8,128)(2,1)S(1)}, bf16[1280,512]{1,0:T(8,128)(2,1)S(1)}, bf16[7,128,2560]{2,1,0:T(8,128)(2,1)S(1)}) custom-call(bf16[896,512]{1,0:T(8,128)(2,1)S(1)} %get-tuple-element.84.x_zero, bf16[1536,512]{1,0:T(8,128)(2,1)S(1)} %get-tuple-element.85.x_one, ...), custom_call_target="tpu_custom_call" | custom-call | flops 4915724288 | bytes 11403264 | tf_op jit(solution)/shard_map/pallas_call | solution.py:398
  35.9 3.5 %shard_map.157 = (bf16[896,512]{1,0:T(8,128)(2,1)S(1)}, bf16[1536,512]{1,0:T(8,128)(2,1)S(1)}, bf16[1280,512]{1,0:T(8,128)(2,1)S(1)}, bf16[128,512]{1,0:T(8,128)(2,1)S(1)}) custom-call(s32[1]{0:T(128)} %bitcast.11.live, s32[1,512]{1,0:T(1,128)S(1)} %copy-done.10, f32[49,29,512]{2,1,0:T(8,128)S(1)} %get-tuple-element.75.wide, ...), custom_call_target="tpu_custom_call" | custom-call | flops 2055208960 | bytes 7602176 | tf_op jit(solution)/shard_map/pallas_call | solution.py:398
  39.5 4.0 %shard_map.158 = (bf16[5632,128]{1,0:T(8,128)(2,1)S(1)}, bf16[5632,128]{1,0:T(8,128)(2,1)S(1)}) custom-call(bf16[1280,512]{1,0:T(8,128)(2,1)S(1)} %get-tuple-element.79.x_two, bf16[1280,512]{1,0:T(8,128)(2,1)S(1)} %get-tuple-element.93.g_two, bf16[1536,512]{1,0:T(8,128)(2,1)S(1)} %get-tuple-element.85.x_one, bf16[1536,512]{1,0:T(8,128)(2,1)S(1)} %get-tuple-element.94.g_one), custom_call_target="tpu_custom_call" | custom-call | flops 2457862144 | bytes 5767168 | tf_op jit(solution)/shard_map/pallas_call | solution.py:398
  43.5 2.7 %shard_map.159 = (bf16[5632,128]{1,0:T(8,128)(2,1)S(1)}, bf16[5632,128]{1,0:T(8,128)(2,1)S(1)}) custom-call(bf16[1536,512]{1,0:T(8,128)(2,1)S(1)} %get-tuple-element.85.x_one, bf16[1536,512]{1,0:T(8,128)(2,1)S(1)} %get-tuple-element.94.g_one, bf16[896,512]{1,0:T(8,128)(2,1)S(1)} %get-tuple-element.84.x_zero, bf16[896,512]{1,0:T(8,128)(2,1)S(1)} %get-tuple-element.97.g_zero, ...), custom_call_target="tpu_custom_call" | custom-call | flops 2457862144 | bytes 5767168 | tf_op jit(solution)/shard_map/pallas_call | solution.py:398
  47.2 2.5 %collective-permute-done.7 = bf16[5632,128]{1,0:T(8,128)(2,1)S(1)} collective-permute-done((bf16[5632,128]{1,0:T(8,128)(2,1)S(1)}, bf16[5632,128]{1,0:T(8,128)(2,1)S(1)}, u32[]{:S(2)}, u32[]{:S(2)}) %collective-permute-start.7) | collective-permute-done | bytes 1441824 | tf_op jit(solution)/shard_map/ppermute | solution.py:418
  53.8 15.2 %shard_map.160 = (bf16[32,6272]{1,0:T(8,128)(2,1)S(1)}, bf16[32,6272]{1,0:T(8,128)(2,1)S(1)}, bf16[32,6272]{1,0:T(8,128)(2,1)S(1)}, bf16[32,6272]{1,0:T(8,128)(2,1)S(1)}) custom-call(s32[1]{0:T(128)} %bitcast.12.live, bf16[896,896]{1,0:T(8,128)(2,1)S(1)} %copy-done.6, bf16[2,768,768]{2,1,0:T(8,128)(2,1)S(1)} %copy-done.1, ...), custom_call_target="tpu_custom_call" | custom-call | flops 9026142208 | bytes 15204352 | tf_op jit(solution)/shard_map/pallas_call | solution.py:398
  73.0 8.1 %collective-permute-done.12 = bf16[32,6272]{1,0:T(8,128)(2,1)S(1)} collective-permute-done((bf16[32,6272]{1,0:T(8,128)(2,1)S(1)}, bf16[32,6272]{1,0:T(8,128)(2,1)S(1)}, u32[]{:S(2)}, u32[]{:S(2)}) %collective-permute-start.12) | collective-permute-done | bytes 401440 | tf_op jit(solution)/shard_map/ppermute | solution.py:418
  84.2 5.2 %collective-permute-done.13 = bf16[704,128]{1,0:T(8,128)(2,1)S(1)} collective-permute-done((bf16[704,128]{1,0:T(8,128)(2,1)S(1)}, bf16[704,128]{1,0:T(8,128)(2,1)S(1)}, u32[]{:S(2)}, u32[]{:S(2)}) %collective-permute-start.13) | collective-permute-done | bytes 180256 | tf_op jit(solution)/shard_map/ppermute | solution.py:418
  89.4 2.7 %collective-permute-start.14 = (bf16[352,128]{1,0:T(8,128)(2,1)S(1)}, bf16[352,128]{1,0:T(8,128)(2,1)S(1)}, u32[]{:S(2)}, u32[]{:S(2)}) collective-permute-start(bf16[352,128]{1,0:T(8,128)(2,1)S(1)} %slice.98), channel_id=1, source_target_pairs={{0,2},{1,3},{2,0},{3,1},{4,6},{5,7},{6,4},{7,5},{8,10},{9,11},{10,... | collective-permute-start | bytes 270344 | tf_op jit(solution)/shard_map/ppermute | solution.py:418
  92.2 2.8 %collective-permute-start.17 = (bf16[352,128]{1,0:T(8,128)(2,1)S(1)}, bf16[352,128]{1,0:T(8,128)(2,1)S(1)}, u32[]{:S(2)}, u32[]{:S(2)}) collective-permute-start(bf16[352,128]{1,0:T(8,128)(2,1)S(1)} %slice.103), channel_id=1, source_target_pairs={{0,2},{1,3},{2,0},{3,1},{4,6},{5,7},{6,4},{7,5},{8,10},{9,11},{10,... | collective-permute-start | bytes 270344 | tf_op jit(solution)/shard_map/ppermute | solution.py:418
  95.0 4.7 %collective-permute-done.14 = bf16[352,128]{1,0:T(8,128)(2,1)S(1)} collective-permute-done((bf16[352,128]{1,0:T(8,128)(2,1)S(1)}, bf16[352,128]{1,0:T(8,128)(2,1)S(1)}, u32[]{:S(2)}, u32[]{:S(2)}) %collective-permute-start.14) | collective-permute-done | bytes 90144 | tf_op jit(solution)/shard_map/ppermute | solution.py:418
  102.8 2.9 %collective-permute-done.15 = bf16[352,128]{1,0:T(8,128)(2,1)S(1)} collective-permute-done((bf16[352,128]{1,0:T(8,128)(2,1)S(1)}, bf16[352,128]{1,0:T(8,128)(2,1)S(1)}, u32[]{:S(2)}, u32[]{:S(2)}) %collective-permute-start.15) | collective-permute-done | bytes 90144 | tf_op jit(solution)/shard_map/ppermute | solution.py:418
  106.9 2.2 %collective-permute-start.21 = (bf16[704,128]{1,0:T(8,128)(2,1)S(1)}, bf16[704,128]{1,0:T(8,128)(2,1)S(1)}, u32[]{:S(2)}, u32[]{:S(2)}) collective-permute-start(bf16[704,128]{1,0:T(8,128)(2,1)S(1)} %pad_maximum_fusion.6), channel_id=1, source_target_pairs={{0,1},{1,0},{2,3},{3,2},{4,5},{5,4},{6,7},{7,6},{8,9},{9,8},{10,11... | collective-permute-start | bytes 540680 | tf_op jit(solution)/shard_map/ppermute | solution.py:418
  111.3 3.3 %collective-permute-done.21 = bf16[704,128]{1,0:T(8,128)(2,1)S(1)} collective-permute-done((bf16[704,128]{1,0:T(8,128)(2,1)S(1)}, bf16[704,128]{1,0:T(8,128)(2,1)S(1)}, u32[]{:S(2)}, u32[]{:S(2)}) %collective-permute-start.21) | collective-permute-done | bytes 180256 | tf_op jit(solution)/shard_map/ppermute | solution.py:418
  118.5 4.5 %collective-permute-done.23 = bf16[32,6272]{1,0:T(8,128)(2,1)S(1)} collective-permute-done((bf16[32,6272]{1,0:T(8,128)(2,1)S(1)}, bf16[32,6272]{1,0:T(8,128)(2,1)S(1)}, u32[]{:S(2)}, u32[]{:S(2)}) %collective-permute-start.23) | collective-permute-done | bytes 401440 | tf_op jit(solution)/shard_map/ppermute | solution.py:418
  124.5 4.5 %collective-permute-done.20 = bf16[1408,128]{1,0:T(8,128)(2,1)S(1)} collective-permute-done((bf16[1408,128]{1,0:T(8,128)(2,1)S(1)}, bf16[1408,128]{1,0:T(8,128)(2,1)S(1)}, u32[]{:S(2)}, u32[]{:S(2)}) %collective-permute-start.20) | collective-permute-done | bytes 360480 | tf_op jit(solution)/shard_map/ppermute | solution.py:418
  131.0 9.6 %collective-permute-done.25 = bf16[2816,128]{1,0:T(8,128)(2,1)S(1)} collective-permute-done((bf16[2816,128]{1,0:T(8,128)(2,1)S(1)}, bf16[2816,128]{1,0:T(8,128)(2,1)S(1)}, u32[]{:S(2)}, u32[]{:S(2)}) %collective-permute-start.25) | collective-permute-done | bytes 720928 | tf_op jit(solution)/shard_map/ppermute | solution.py:418
  142.6 2.8 %shard_map.161 = (f32[2,640,640]{2,1,0:T(8,128)}, f32[2,768,768]{2,1,0:T(8,128)}, f32[896,896]{1,0:T(8,128)}, f32[128,128]{1,0:T(8,128)}) custom-call(bf16[5632,128]{1,0:T(8,128)(2,1)S(1)} %constant_dynamic-update-slice_fusion.refs_0_, bf16[5632,128]{1,0:T(8,128)(2,1)S(1)} %constant_dynamic-update-slice_fusion.5.refs_1_), custom_call_target="tpu_custom_call" | custom-call | bytes 8650752 | tf_op jit(solution)/shard_map/pallas_call | solution.py:398
  146.0 2.7 %shard_map.162 = (f32[2,640,640]{2,1,0:T(8,128)}, f32[2,768,768]{2,1,0:T(8,128)}, f32[896,896]{1,0:T(8,128)}, f32[128,128]{1,0:T(8,128)}) custom-call(f32[2,640,640]{2,1,0:T(8,128)} %get-tuple-element.126.refs_0_, f32[2,768,768]{2,1,0:T(8,128)} %get-tuple-element.127.refs_1_, ...), custom_call_target="tpu_custom_call", output_to_operand_aliasing={{0}: (0, {}), {1}: (1, {}), {2}: (2, {}), {3}: (3, {})} | custom-call | bytes 8650752 | tf_op jit(solution)/shard_map/pallas_call | solution.py:398
  (107 shorter events, 40.3 us)
Async XLA Ops:
  0.6 15.4 %collective-permute-start = (bf16[16,6272]{1,0:T(8,128)(2,1)}, bf16[16,6272]{1,0:T(8,128)(2,1)S(1)}, u32[]{:S(2)}, u32[]{:S(2)}) collective-permute-start(bf16[16,6272]{1,0:T(8,128)(2,1)} %bitcast.18), channel_id=1, source_target_pairs={{0,2},{1,3},{2,0},{3,1},{4,6},{5,7},{6,4},{7,5},{8,10},{9,11},{10,... | collective-permute-start | bytes 602120 | tf_op jit(solution)/shard_map/ppermute | solution.py:418
  4.7 19.0 %collective-permute-start.1 = (bf16[16,6272]{1,0:T(8,128)(2,1)}, bf16[16,6272]{1,0:T(8,128)(2,1)S(1)}, u32[]{:S(2)}, u32[]{:S(2)}) collective-permute-start(bf16[16,6272]{1,0:T(8,128)(2,1)} %bitcast.19), channel_id=1, source_target_pairs={{0,1},{1,0},{2,3},{3,2},{4,5},{5,4},{6,7},{7,6},{8,9},{9,8},{10,11... | collective-permute-start | bytes 602120 | tf_op jit(solution)/shard_map/ppermute | solution.py:418
  6.3 16.7 %collective-permute-start.3 = (bf16[16,6272]{1,0:T(8,128)(2,1)}, bf16[16,6272]{1,0:T(8,128)(2,1)S(1)}, u32[]{:S(2)}, u32[]{:S(2)}) collective-permute-start(bf16[16,6272]{1,0:T(8,128)(2,1)} %bitcast.14), channel_id=1, source_target_pairs={{0,2},{1,3},{2,0},{3,1},{4,6},{5,7},{6,4},{7,5},{8,10},{9,11},{10,... | collective-permute-start | bytes 602120 | tf_op jit(solution)/shard_map/ppermute | solution.py:418
  16.0 11.1 %collective-permute-start.2 = (bf16[16,6272]{1,0:T(8,128)(2,1)S(1)}, bf16[16,6272]{1,0:T(8,128)(2,1)S(1)}, u32[]{:S(2)}, u32[]{:S(2)}) collective-permute-start(bf16[16,6272]{1,0:T(8,128)(2,1)S(1)} %collective-permute-done.refs_1_), channel_id=1, source_target_pairs={{0,1},{1,0},{2,3},{3,2},{4,5},{5,4},{6,7},{7,6},{8,9},{9,8},{10,11... | collective-permute-start | bytes 602120 | tf_op jit(solution)/shard_map/ppermute | solution.py:418
  16.9 19.0 %collective-permute-start.4 = (bf16[16,6272]{1,0:T(8,128)(2,1)S(1)}, bf16[16,6272]{1,0:T(8,128)(2,1)S(1)}, u32[]{:S(2)}, u32[]{:S(2)}) collective-permute-start(bf16[16,6272]{1,0:T(8,128)(2,1)S(1)} %bitcast.15), channel_id=1, source_target_pairs={{0,1},{1,0},{2,3},{3,2},{4,5},{5,4},{6,7},{7,6},{8,9},{9,8},{10,11... | collective-permute-start | bytes 602120 | tf_op jit(solution)/shard_map/ppermute | solution.py:418
  23.0 12.9 %collective-permute-start.5 = (bf16[16,6272]{1,0:T(8,128)(2,1)S(1)}, bf16[16,6272]{1,0:T(8,128)(2,1)S(1)}, u32[]{:S(2)}, u32[]{:S(2)}) collective-permute-start(bf16[16,6272]{1,0:T(8,128)(2,1)S(1)} %collective-permute-done.3.refs_1_), channel_id=1, source_target_pairs={{0,1},{1,0},{2,3},{3,2},{4,5},{5,4},{6,7},{7,6},{8,9},{9,8},{10,11... | collective-permute-start | bytes 602120 | tf_op jit(solution)/shard_map/ppermute | solution.py:418
  50.2 18.9 %collective-permute-start.9 = (bf16[2816,128]{1,0:T(8,128)(2,1)S(1)}, bf16[2816,128]{1,0:T(8,128)(2,1)S(1)}, u32[]{:S(2)}, u32[]{:S(2)}) collective-permute-start(bf16[2816,128]{1,0:T(8,128)(2,1)S(1)} %slice.72), channel_id=1, source_target_pairs={{0,16},{4,20},{8,24},{12,28},{16,0},{20,4},{24,8},{28,12},{1,17},{... | collective-permute-start | bytes 2162696 | tf_op jit(solution)/shard_map/ppermute | solution.py:418
  52.3 18.1 %collective-permute-start.8 = (bf16[2816,128]{1,0:T(8,128)(2,1)S(1)}, bf16[2816,128]{1,0:T(8,128)(2,1)S(1)}, u32[]{:S(2)}, u32[]{:S(2)}) collective-permute-start(bf16[2816,128]{1,0:T(8,128)(2,1)S(1)} %slice.71), channel_id=1, source_target_pairs={{0,8},{4,12},{8,0},{12,4},{16,24},{20,28},{24,16},{28,20},{1,9},{5... | collective-permute-start | bytes 2162696 | tf_op jit(solution)/shard_map/ppermute | solution.py:418
  70.6 10.5 %collective-permute-start.12 = (bf16[32,6272]{1,0:T(8,128)(2,1)S(1)}, bf16[32,6272]{1,0:T(8,128)(2,1)S(1)}, u32[]{:S(2)}, u32[]{:S(2)}) collective-permute-start(bf16[32,6272]{1,0:T(8,128)(2,1)S(1)} %get-tuple-element.112), channel_id=1, source_target_pairs={{0,1},{1,0},{2,3},{3,2},{4,5},{5,4},{6,7},{7,6},{8,9},{9,8},{10,11... | collective-permute-start | bytes 1204232 | tf_op jit(solution)/shard_map/ppermute | solution.py:418
  70.9 10.3 %collective-permute-start.11 = (bf16[1408,128]{1,0:T(8,128)(2,1)S(1)}, bf16[1408,128]{1,0:T(8,128)(2,1)S(1)}, u32[]{:S(2)}, u32[]{:S(2)}) collective-permute-start(bf16[1408,128]{1,0:T(8,128)(2,1)S(1)} %slice.94), channel_id=1, source_target_pairs={{0,8},{4,12},{8,0},{12,4},{16,24},{20,28},{24,16},{28,20},{1,9},{5... | collective-permute-start | bytes 1081352 | tf_op jit(solution)/shard_map/ppermute | solution.py:418
  72.5 9.3 %collective-permute-start.10 = (bf16[1408,128]{1,0:T(8,128)(2,1)S(1)}, bf16[1408,128]{1,0:T(8,128)(2,1)S(1)}, u32[]{:S(2)}, u32[]{:S(2)}) collective-permute-start(bf16[1408,128]{1,0:T(8,128)(2,1)S(1)} %slice.93), channel_id=1, source_target_pairs={{0,16},{4,20},{8,24},{12,28},{16,0},{20,4},{24,8},{28,12},{1,17},{... | collective-permute-start | bytes 1081352 | tf_op jit(solution)/shard_map/ppermute | solution.py:418
  81.9 7.5 %collective-permute-start.13 = (bf16[704,128]{1,0:T(8,128)(2,1)S(1)}, bf16[704,128]{1,0:T(8,128)(2,1)S(1)}, u32[]{:S(2)}, u32[]{:S(2)}) collective-permute-start(bf16[704,128]{1,0:T(8,128)(2,1)S(1)} %slice.96), channel_id=1, source_target_pairs={{0,1},{1,0},{2,3},{3,2},{4,5},{5,4},{6,7},{7,6},{8,9},{9,8},{10,11... | collective-permute-start | bytes 540680 | tf_op jit(solution)/shard_map/ppermute | solution.py:418
  83.8 8.4 %collective-permute-start.16 = (bf16[704,128]{1,0:T(8,128)(2,1)S(1)}, bf16[704,128]{1,0:T(8,128)(2,1)S(1)}, u32[]{:S(2)}, u32[]{:S(2)}) collective-permute-start(bf16[704,128]{1,0:T(8,128)(2,1)S(1)} %slice.101), channel_id=1, source_target_pairs={{0,1},{1,0},{2,3},{3,2},{4,5},{5,4},{6,7},{7,6},{8,9},{9,8},{10,11... | collective-permute-start | bytes 540680 | tf_op jit(solution)/shard_map/ppermute | solution.py:418
  89.4 10.3 %collective-permute-start.14 = (bf16[352,128]{1,0:T(8,128)(2,1)S(1)}, bf16[352,128]{1,0:T(8,128)(2,1)S(1)}, u32[]{:S(2)}, u32[]{:S(2)}) collective-permute-start(bf16[352,128]{1,0:T(8,128)(2,1)S(1)} %slice.98), channel_id=1, source_target_pairs={{0,2},{1,3},{2,0},{3,1},{4,6},{5,7},{6,4},{7,5},{8,10},{9,11},{10,... | collective-permute-start | bytes 270344 | tf_op jit(solution)/shard_map/ppermute | solution.py:418
  92.2 9.0 %collective-permute-start.17 = (bf16[352,128]{1,0:T(8,128)(2,1)S(1)}, bf16[352,128]{1,0:T(8,128)(2,1)S(1)}, u32[]{:S(2)}, u32[]{:S(2)}) collective-permute-start(bf16[352,128]{1,0:T(8,128)(2,1)S(1)} %slice.103), channel_id=1, source_target_pairs={{0,2},{1,3},{2,0},{3,1},{4,6},{5,7},{6,4},{7,5},{8,10},{9,11},{10,... | collective-permute-start | bytes 270344 | tf_op jit(solution)/shard_map/ppermute | solution.py:418
  99.7 6.0 %collective-permute-start.15 = (bf16[352,128]{1,0:T(8,128)(2,1)S(1)}, bf16[352,128]{1,0:T(8,128)(2,1)S(1)}, u32[]{:S(2)}, u32[]{:S(2)}) collective-permute-start(bf16[352,128]{1,0:T(8,128)(2,1)S(1)} %get-tuple-element.137), channel_id=1, source_target_pairs={{0,2},{1,3},{2,0},{3,1},{4,6},{5,7},{6,4},{7,5},{8,10},{9,11},{10,... | collective-permute-start | bytes 270344 | tf_op jit(solution)/shard_map/ppermute | solution.py:418
  106.9 7.7 %collective-permute-start.21 = (bf16[704,128]{1,0:T(8,128)(2,1)S(1)}, bf16[704,128]{1,0:T(8,128)(2,1)S(1)}, u32[]{:S(2)}, u32[]{:S(2)}) collective-permute-start(bf16[704,128]{1,0:T(8,128)(2,1)S(1)} %pad_maximum_fusion.6), channel_id=1, source_target_pairs={{0,1},{1,0},{2,3},{3,2},{4,5},{5,4},{6,7},{7,6},{8,9},{9,8},{10,11... | collective-permute-start | bytes 540680 | tf_op jit(solution)/shard_map/ppermute | solution.py:418
  109.2 8.4 %collective-permute-start.19 = (bf16[704,128]{1,0:T(8,128)(2,1)S(1)}, bf16[704,128]{1,0:T(8,128)(2,1)S(1)}, u32[]{:S(2)}, u32[]{:S(2)}) collective-permute-start(bf16[704,128]{1,0:T(8,128)(2,1)S(1)} %pad_maximum_fusion.5), channel_id=1, source_target_pairs={{0,1},{1,0},{2,3},{3,2},{4,5},{5,4},{6,7},{7,6},{8,9},{9,8},{10,11... | collective-permute-start | bytes 540680 | tf_op jit(solution)/shard_map/ppermute | solution.py:418
  109.3 13.7 %collective-permute-start.23 = (bf16[32,6272]{1,0:T(8,128)(2,1)S(1)}, bf16[32,6272]{1,0:T(8,128)(2,1)S(1)}, u32[]{:S(2)}, u32[]{:S(2)}) collective-permute-start(bf16[32,6272]{1,0:T(8,128)(2,1)S(1)} %get-tuple-element.121), channel_id=1, source_target_pairs={{0,1},{1,0},{2,3},{3,2},{4,5},{5,4},{6,7},{7,6},{8,9},{9,8},{10,11... | collective-permute-start | bytes 1204232 | tf_op jit(solution)/shard_map/ppermute | solution.py:418
  114.7 9.8 %collective-permute-start.22 = (bf16[1408,128]{1,0:T(8,128)(2,1)S(1)}, bf16[1408,128]{1,0:T(8,128)(2,1)S(1)}, u32[]{:S(2)}, u32[]{:S(2)}) collective-permute-start(bf16[1408,128]{1,0:T(8,128)(2,1)S(1)} %pad_maximum_fusion.4), channel_id=1, source_target_pairs={{0,8},{4,12},{8,0},{12,4},{16,24},{20,28},{24,16},{28,20},{1,9},{5... | collective-permute-start | bytes 1081352 | tf_op jit(solution)/shard_map/ppermute | solution.py:418
  117.6 11.3 %collective-permute-start.20 = (bf16[1408,128]{1,0:T(8,128)(2,1)S(1)}, bf16[1408,128]{1,0:T(8,128)(2,1)S(1)}, u32[]{:S(2)}, u32[]{:S(2)}) collective-permute-start(bf16[1408,128]{1,0:T(8,128)(2,1)S(1)} %pad_maximum_fusion.3), channel_id=1, source_target_pairs={{0,16},{4,20},{8,24},{12,28},{16,0},{20,4},{24,8},{28,12},{1,17},{... | collective-permute-start | bytes 1081352 | tf_op jit(solution)/shard_map/ppermute | solution.py:418
  129.1 12.6 %collective-permute-start.24 = (bf16[32,6272]{1,0:T(8,128)(2,1)S(1)}, bf16[32,6272]{1,0:T(8,128)(2,1)S(1)}, u32[]{:S(2)}, u32[]{:S(2)}) collective-permute-start(bf16[32,6272]{1,0:T(8,128)(2,1)S(1)} %pad_maximum_fusion.2), channel_id=1, source_target_pairs={{0,2},{1,3},{2,0},{3,1},{4,6},{5,7},{6,4},{7,5},{8,10},{9,11},{10,... | collective-permute-start | bytes 1204232 | tf_op jit(solution)/shard_map/ppermute | solution.py:418
  129.2 11.4 %collective-permute-start.25 = (bf16[2816,128]{1,0:T(8,128)(2,1)S(1)}, bf16[2816,128]{1,0:T(8,128)(2,1)S(1)}, u32[]{:S(2)}, u32[]{:S(2)}) collective-permute-start(bf16[2816,128]{1,0:T(8,128)(2,1)S(1)} %pad_maximum_fusion), channel_id=1, source_target_pairs={{0,8},{4,12},{8,0},{12,4},{16,24},{20,28},{24,16},{28,20},{1,9},{5... | collective-permute-start | bytes 2162696 | tf_op jit(solution)/shard_map/ppermute | solution.py:418
  130.2 11.4 %collective-permute-start.26 = (bf16[2816,128]{1,0:T(8,128)(2,1)S(1)}, bf16[2816,128]{1,0:T(8,128)(2,1)S(1)}, u32[]{:S(2)}, u32[]{:S(2)}) collective-permute-start(bf16[2816,128]{1,0:T(8,128)(2,1)S(1)} %pad_maximum_fusion.1), channel_id=1, source_target_pairs={{0,16},{4,20},{8,24},{12,28},{16,0},{20,4},{24,8},{28,12},{1,17},{... | collective-permute-start | bytes 2162696 | tf_op jit(solution)/shard_map/ppermute | solution.py:418
  (18 other events, 90.4 us)

commit v4 on v3

--- a/solution.py
+++ b/solution.py
@@ -530,7 +530,7 @@
 
     dp_bits = bits_of("dp")
     stages_a = dp_bits + bits_of("graph")
-    stages_b = dp_bits[:1] + dp_bits[1:][::-1] + bits_of("graph")
+    stages_b = dp_bits[:1] + dp_bits[1:][::-1] + bits_of("graph")[::-1]
     blocks = lax.axis_size("dp") * lax.axis_size("graph")
     rows_two = 2 * two * two * width
     rows_one = one * one * width
@@ -567,7 +567,7 @@
         other_a, other_b = exchange(sent_a, *stage_a), exchange(sent_b, *stage_b)
         if place == 0:
             a, b = add_low(a, other_a), add_low(b, other_b)
-            a, b, messages = tied(a, b, messages)
+            b, messages = tied(b, messages)
             sum_kept, sum_sent, grad_kept, grad_sent = call(
                 functools.partial(back_kernel, sizes, order),
                 (partial_shape,) * 4,
@@ -596,12 +596,12 @@
         half_b = (b, exchange(b, *stages_b[place]))
         if place == last + 2:
             (low_a, high_a), (low_b, high_b) = half_a, half_b
-            high_a, high_b, grad_kept, grad_sent = tied(high_a, high_b, grad_kept, grad_sent)
+            high_b, grad_kept, grad_sent = tied(high_b, grad_kept, grad_sent)
             half_a, half_b = (low_a, high_a), (low_b, high_b)
             grad_half = add_low(grad_kept, exchange(grad_sent, *graph_bits[0]))
         if place == last:
             (low_a, high_a), (low_b, high_b) = half_a, half_b
-            high_a, high_b, sum_half, grad_half = tied(high_a, high_b, sum_half, grad_half)
+            high_a, sum_half, grad_half = tied(high_a, sum_half, grad_half)
             half_a, half_b = (low_a, high_a), (low_b, high_b)
             summed, grad_rows = relative_sum([sum_half, grad_half], graph_bits[1:])
         if place > 0:

time: 149 us -> 145 us (0.973)
  waiting for transfers between devices: 61.4 us -> 55.6 us
  starting transfers between devices: 33 us -> 34.8 us
    ppermute x29, waiting for transfers between devices: 61.4 us -> 55.6 us  [exchange(): return lax.ppermute(value, axis, [(i, i ^ bit) for i in range(count)])]
    ppermute x29, starting transfers between devices: 33 us -> 34.8 us  [exchange(): return lax.ppermute(value, axis, [(i, i ^ bit) for i in range(count)])]
    unnamed x31 -> x32, local copies, waits for them, and re-layouts: 7.04 us -> 7.1 us
  transfers between devices with their start and end apart: 29 -> 29, of which waited for: 19 -> 17; matrix products, arithmetic and copies ran while one was open for 2% -> 2% of each run, Pallas kernels for 21% -> 22%
where the time goes in v4:
time: 145 us
  waiting for transfers between devices  55.6 us (38%)
  Pallas kernels  42.1 us (29%)
  starting transfers between devices  34.8 us (24%)
  local copies, waits for them, and re-layouts  7.53 us (5%)
  other arithmetic  2.95 us (2%)
  between operations  1.95 us (1%)
    ppermute x29, waiting for transfers between devices, exchange(): return lax.ppermute(value, axis, [(i, i ^ bit) for i in range(count)])  55.6 us
    pallas_call x9, Pallas kernels, call(): pl.pallas_call(kernel, out_shape=out_shape, in_specs=[SMEM] * smem + [ANY...  42.1 us
    ppermute x29, starting transfers between devices, exchange(): return lax.ppermute(value, axis, [(i, i ^ bit) for i in range(count)])  34.8 us
    unnamed x32, local copies, waits for them, and re-layouts  7.1 us
  transfers between devices with their start and end apart: 29, of which 17 were waited for; matrix products, arithmetic and copies ran while one was open for 2% of the time, Pallas kernels for 22%

profile of v4, /device:TPU:0, one launch (start us, length us, event | category | flops | bytes accessed | tf_op | source)
XLA Modules:
  0.0 144.9 jit_solution(4621786058458566700)
XLA Ops:
  0.6 4.1 %collective-permute-start = (bf16[16,6272]{1,0:T(8,128)(2,1)}, bf16[16,6272]{1,0:T(8,128)(2,1)S(1)}, u32[]{:S(2)}, u32[]{:S(2)}) collective-permute-start(bf16[16,6272]{1,0:T(8,128)(2,1)} %bitcast.18), channel_id=1, source_target_pairs={{0,2},{1,3},{2,0},{3,1},{4,6},{5,7},{6,4},{7,5},{8,10},{9,11},{10,... | collective-permute-start | bytes 602120 | tf_op jit(solution)/shard_map/ppermute | solution.py:418
  13.5 2.5 %shard_map.154 = (f32[49,29,512]{2,1,0:T(8,128)S(1)}, f32[128,512]{1,0:T(8,128)S(1)}, bf16[896,896]{1,0:T(8,128)(2,1)S(1)}, bf16[2,768,768]{2,1,0:T(8,128)(2,1)S(1)}, bf16[2,640,640]{2,1,0:T(8,128)(2,1)S(1)}) custom-call(bf16[49,29,512]{2,1,0:T(8,128)(2,1)S(1)} %bitcast.13, bf16[896,896]{1,0:T(8,128)(2,1)S(1)} %copy-done.5, ...), custom_call_target="tpu_custom_call" | custom-call | bytes 15421440 | tf_op jit(solution)/shard_map/pallas_call | solution.py:398
  18.9 4.1 %collective-permute-done.3.refs_1_ = bf16[16,6272]{1,0:T(8,128)(2,1)S(1)} collective-permute-done((bf16[16,6272]{1,0:T(8,128)(2,1)}, bf16[16,6272]{1,0:T(8,128)(2,1)S(1)}, u32[]{:S(2)}, u32[]{:S(2)}) %collective-permute-start.3) | collective-permute-done | bytes 200736 | tf_op jit(solution)/shard_map/ppermute | solution.py:418
  23.7 3.4 %collective-permute-done.2.refs_3_ = bf16[16,6272]{1,0:T(8,128)(2,1)S(1)} collective-permute-done((bf16[16,6272]{1,0:T(8,128)(2,1)S(1)}, bf16[16,6272]{1,0:T(8,128)(2,1)S(1)}, u32[]{:S(2)}, u32[]{:S(2)}) %collective-permute-start.2) | collective-permute-done | bytes 200736 | tf_op jit(solution)/shard_map/ppermute | solution.py:418
  27.2 3.1 %shard_map.155 = (bf16[896,512]{1,0:T(8,128)(2,1)S(1)}, bf16[1536,512]{1,0:T(8,128)(2,1)S(1)}, bf16[1280,512]{1,0:T(8,128)(2,1)S(1)}, f32[128,512]{1,0:T(8,128)S(1)}, f32[128,512]{1,0:T(8,128)S(1)}) custom-call(s32[1,512]{1,0:T(1,128)S(1)} %copy-done.12, f32[49,29,512]{2,1,0:T(8,128)S(1)} %get-tuple-element.72.wide, f32[128,512]{1,0:T(8,128)S(1)} %get-tuple-element.73.scale, ...), custom_call_target="tpu_custom_call" | custom-call | flops 2055208960 | bytes 7602176 | tf_op jit(solution)/shard_map/pallas_call | solution.py:398
  30.3 5.6 %shard_map.156 = (bf16[896,512]{1,0:T(8,128)(2,1)S(1)}, bf16[1536,512]{1,0:T(8,128)(2,1)S(1)}, bf16[1280,512]{1,0:T(8,128)(2,1)S(1)}, bf16[7,128,2560]{2,1,0:T(8,128)(2,1)S(1)}) custom-call(bf16[896,512]{1,0:T(8,128)(2,1)S(1)} %get-tuple-element.81.x_zero, bf16[1536,512]{1,0:T(8,128)(2,1)S(1)} %get-tuple-element.82.x_one, ...), custom_call_target="tpu_custom_call" | custom-call | flops 4915724288 | bytes 11403264 | tf_op jit(solution)/shard_map/pallas_call | solution.py:398
  35.9 3.5 %shard_map.157 = (bf16[896,512]{1,0:T(8,128)(2,1)S(1)}, bf16[1536,512]{1,0:T(8,128)(2,1)S(1)}, bf16[1280,512]{1,0:T(8,128)(2,1)S(1)}, bf16[128,512]{1,0:T(8,128)(2,1)S(1)}) custom-call(s32[1]{0:T(128)} %bitcast.11.live, s32[1,512]{1,0:T(1,128)S(1)} %copy-done.10, f32[49,29,512]{2,1,0:T(8,128)S(1)} %get-tuple-element.72.wide, ...), custom_call_target="tpu_custom_call" | custom-call | flops 2055208960 | bytes 7602176 | tf_op jit(solution)/shard_map/pallas_call | solution.py:398
  39.5 4.0 %shard_map.158 = (bf16[5632,128]{1,0:T(8,128)(2,1)S(1)}, bf16[5632,128]{1,0:T(8,128)(2,1)S(1)}) custom-call(bf16[1280,512]{1,0:T(8,128)(2,1)S(1)} %get-tuple-element.76.x_two, bf16[1280,512]{1,0:T(8,128)(2,1)S(1)} %get-tuple-element.90.g_two, bf16[1536,512]{1,0:T(8,128)(2,1)S(1)} %get-tuple-element.82.x_one, bf16[1536,512]{1,0:T(8,128)(2,1)S(1)} %get-tuple-element.91.g_one), custom_call_target="tpu_custom_call" | custom-call | flops 2457862144 | bytes 5767168 | tf_op jit(solution)/shard_map/pallas_call | solution.py:398
  43.5 2.7 %shard_map.159 = (bf16[5632,128]{1,0:T(8,128)(2,1)S(1)}, bf16[5632,128]{1,0:T(8,128)(2,1)S(1)}) custom-call(bf16[1536,512]{1,0:T(8,128)(2,1)S(1)} %get-tuple-element.82.x_one, bf16[1536,512]{1,0:T(8,128)(2,1)S(1)} %get-tuple-element.91.g_one, bf16[896,512]{1,0:T(8,128)(2,1)S(1)} %get-tuple-element.81.x_zero, bf16[896,512]{1,0:T(8,128)(2,1)S(1)} %get-tuple-element.94.g_zero, ...), custom_call_target="tpu_custom_call" | custom-call | flops 2457862144 | bytes 5767168 | tf_op jit(solution)/shard_map/pallas_call | solution.py:398
  52.3 15.2 %shard_map.160 = (bf16[32,6272]{1,0:T(8,128)(2,1)S(1)}, bf16[32,6272]{1,0:T(8,128)(2,1)S(1)}, bf16[32,6272]{1,0:T(8,128)(2,1)S(1)}, bf16[32,6272]{1,0:T(8,128)(2,1)S(1)}) custom-call(s32[1]{0:T(128)} %bitcast.12.live, bf16[896,896]{1,0:T(8,128)(2,1)S(1)} %copy-done.6, bf16[2,768,768]{2,1,0:T(8,128)(2,1)S(1)} %copy-done.1, ...), custom_call_target="tpu_custom_call" | custom-call | flops 9026142208 | bytes 15204352 | tf_op jit(solution)/shard_map/pallas_call | solution.py:398
  72.7 7.5 %collective-permute-done.12 = bf16[32,6272]{1,0:T(8,128)(2,1)S(1)} collective-permute-done((bf16[32,6272]{1,0:T(8,128)(2,1)S(1)}, bf16[32,6272]{1,0:T(8,128)(2,1)S(1)}, u32[]{:S(2)}, u32[]{:S(2)}) %collective-permute-start.12) | collective-permute-done | bytes 401440 | tf_op jit(solution)/shard_map/ppermute | solution.py:418
  84.4 4.3 %collective-permute-done.13 = bf16[704,128]{1,0:T(8,128)(2,1)S(1)} collective-permute-done((bf16[704,128]{1,0:T(8,128)(2,1)S(1)}, bf16[704,128]{1,0:T(8,128)(2,1)S(1)}, u32[]{:S(2)}, u32[]{:S(2)}) %collective-permute-start.13) | collective-permute-done | bytes 180256 | tf_op jit(solution)/shard_map/ppermute | solution.py:418
  88.8 2.7 %collective-permute-start.14 = (bf16[352,128]{1,0:T(8,128)(2,1)S(1)}, bf16[352,128]{1,0:T(8,128)(2,1)S(1)}, u32[]{:S(2)}, u32[]{:S(2)}) collective-permute-start(bf16[352,128]{1,0:T(8,128)(2,1)S(1)} %slice.100), channel_id=1, source_target_pairs={{0,2},{1,3},{2,0},{3,1},{4,6},{5,7},{6,4},{7,5},{8,10},{9,11},{10,... | collective-permute-start | bytes 270344 | tf_op jit(solution)/shard_map/ppermute | solution.py:418
  91.5 3.3 %collective-permute-done.18 = bf16[704,128]{1,0:T(8,128)(2,1)S(1)} collective-permute-done((bf16[704,128]{1,0:T(8,128)(2,1)S(1)}, bf16[704,128]{1,0:T(8,128)(2,1)S(1)}, u32[]{:S(2)}, u32[]{:S(2)}) %collective-permute-start.18) | collective-permute-done | bytes 180256 | tf_op jit(solution)/shard_map/ppermute | solution.py:418
  97.3 2.5 %collective-permute-done.19 = bf16[352,128]{1,0:T(8,128)(2,1)S(1)} collective-permute-done((bf16[352,128]{1,0:T(8,128)(2,1)S(1)}, bf16[352,128]{1,0:T(8,128)(2,1)S(1)}, u32[]{:S(2)}, u32[]{:S(2)}) %collective-permute-start.19) | collective-permute-done | bytes 90144 | tf_op jit(solution)/shard_map/ppermute | solution.py:418
  99.9 2.5 %collective-permute-done.15 = bf16[352,128]{1,0:T(8,128)(2,1)S(1)} collective-permute-done((bf16[352,128]{1,0:T(8,128)(2,1)S(1)}, bf16[352,128]{1,0:T(8,128)(2,1)S(1)}, u32[]{:S(2)}, u32[]{:S(2)}) %collective-permute-start.15) | collective-permute-done | bytes 90144 | tf_op jit(solution)/shard_map/ppermute | solution.py:418
  102.7 4.0 %collective-permute-done.20 = bf16[352,128]{1,0:T(8,128)(2,1)S(1)} collective-permute-done((bf16[352,128]{1,0:T(8,128)(2,1)S(1)}, bf16[352,128]{1,0:T(8,128)(2,1)S(1)}, u32[]{:S(2)}, u32[]{:S(2)}) %collective-permute-start.20) | collective-permute-done | bytes 90144 | tf_op jit(solution)/shard_map/ppermute | solution.py:418
  107.2 3.9 %collective-permute-start.21 = (bf16[32,6272]{1,0:T(8,128)(2,1)S(1)}, bf16[32,6272]{1,0:T(8,128)(2,1)S(1)}, u32[]{:S(2)}, u32[]{:S(2)}) collective-permute-start(bf16[32,6272]{1,0:T(8,128)(2,1)S(1)} %get-tuple-element.115), channel_id=1, source_target_pairs={{0,1},{1,0},{2,3},{3,2},{4,5},{5,4},{6,7},{7,6},{8,9},{9,8},{10,11... | collective-permute-start | bytes 1204232 | tf_op jit(solution)/shard_map/ppermute | solution.py:418
  112.8 2.4 %collective-permute-done.24 = bf16[704,128]{1,0:T(8,128)(2,1)S(1)} collective-permute-done((bf16[704,128]{1,0:T(8,128)(2,1)S(1)}, bf16[704,128]{1,0:T(8,128)(2,1)S(1)}, u32[]{:S(2)}, u32[]{:S(2)}) %collective-permute-start.24) | collective-permute-done | bytes 180256 | tf_op jit(solution)/shard_map/ppermute | solution.py:418
  115.4 3.3 %collective-permute-done.21 = bf16[32,6272]{1,0:T(8,128)(2,1)S(1)} collective-permute-done((bf16[32,6272]{1,0:T(8,128)(2,1)S(1)}, bf16[32,6272]{1,0:T(8,128)(2,1)S(1)}, u32[]{:S(2)}, u32[]{:S(2)}) %collective-permute-start.21) | collective-permute-done | bytes 401440 | tf_op jit(solution)/shard_map/ppermute | solution.py:418
  120.4 3.8 %collective-permute-done.25 = bf16[1408,128]{1,0:T(8,128)(2,1)S(1)} collective-permute-done((bf16[1408,128]{1,0:T(8,128)(2,1)S(1)}, bf16[1408,128]{1,0:T(8,128)(2,1)S(1)}, u32[]{:S(2)}, u32[]{:S(2)}) %collective-permute-start.25) | collective-permute-done | bytes 360480 | tf_op jit(solution)/shard_map/ppermute | solution.py:418
  126.7 9.0 %collective-permute-done.26 = bf16[2816,128]{1,0:T(8,128)(2,1)S(1)} collective-permute-done((bf16[2816,128]{1,0:T(8,128)(2,1)S(1)}, bf16[2816,128]{1,0:T(8,128)(2,1)S(1)}, u32[]{:S(2)}, u32[]{:S(2)}) %collective-permute-start.26) | collective-permute-done | bytes 720928 | tf_op jit(solution)/shard_map/ppermute | solution.py:418
  139.2 2.8 %shard_map.161 = (f32[2,640,640]{2,1,0:T(8,128)}, f32[2,768,768]{2,1,0:T(8,128)}, f32[896,896]{1,0:T(8,128)}, f32[128,128]{1,0:T(8,128)}) custom-call(bf16[5632,128]{1,0:T(8,128)(2,1)S(1)} %constant_dynamic-update-slice_fusion.refs_0_, bf16[5632,128]{1,0:T(8,128)(2,1)S(1)} %constant_dynamic-update-slice_fusion.5.refs_1_), custom_call_target="tpu_custom_call" | custom-call | bytes 8650752 | tf_op jit(solution)/shard_map/pallas_call | solution.py:398
  142.0 2.7 %shard_map.162 = (f32[2,640,640]{2,1,0:T(8,128)}, f32[2,768,768]{2,1,0:T(8,128)}, f32[896,896]{1,0:T(8,128)}, f32[128,128]{1,0:T(8,128)}) custom-call(f32[2,640,640]{2,1,0:T(8,128)} %get-tuple-element.120.refs_0_, f32[2,768,768]{2,1,0:T(8,128)} %get-tuple-element.121.refs_1_, ...), custom_call_target="tpu_custom_call", output_to_operand_aliasing={{0}: (0, {}), {1}: (1, {}), {2}: (2, {}), {3}: (3, {})} | custom-call | bytes 8650752 | tf_op jit(solution)/shard_map/pallas_call | solution.py:398
  (108 shorter events, 39.9 us)
Async XLA Ops:
  0.6 15.4 %collective-permute-start = (bf16[16,6272]{1,0:T(8,128)(2,1)}, bf16[16,6272]{1,0:T(8,128)(2,1)S(1)}, u32[]{:S(2)}, u32[]{:S(2)}) collective-permute-start(bf16[16,6272]{1,0:T(8,128)(2,1)} %bitcast.18), channel_id=1, source_target_pairs={{0,2},{1,3},{2,0},{3,1},{4,6},{5,7},{6,4},{7,5},{8,10},{9,11},{10,... | collective-permute-start | bytes 602120 | tf_op jit(solution)/shard_map/ppermute | solution.py:418
  4.7 19.0 %collective-permute-start.1 = (bf16[16,6272]{1,0:T(8,128)(2,1)}, bf16[16,6272]{1,0:T(8,128)(2,1)S(1)}, u32[]{:S(2)}, u32[]{:S(2)}) collective-permute-start(bf16[16,6272]{1,0:T(8,128)(2,1)} %bitcast.19), channel_id=1, source_target_pairs={{0,1},{1,0},{2,3},{3,2},{4,5},{5,4},{6,7},{7,6},{8,9},{9,8},{10,11... | collective-permute-start | bytes 602120 | tf_op jit(solution)/shard_map/ppermute | solution.py:418
  6.3 16.7 %collective-permute-start.3 = (bf16[16,6272]{1,0:T(8,128)(2,1)}, bf16[16,6272]{1,0:T(8,128)(2,1)S(1)}, u32[]{:S(2)}, u32[]{:S(2)}) collective-permute-start(bf16[16,6272]{1,0:T(8,128)(2,1)} %bitcast.14), channel_id=1, source_target_pairs={{0,2},{1,3},{2,0},{3,1},{4,6},{5,7},{6,4},{7,5},{8,10},{9,11},{10,... | collective-permute-start | bytes 602120 | tf_op jit(solution)/shard_map/ppermute | solution.py:418
  16.0 11.1 %collective-permute-start.2 = (bf16[16,6272]{1,0:T(8,128)(2,1)S(1)}, bf16[16,6272]{1,0:T(8,128)(2,1)S(1)}, u32[]{:S(2)}, u32[]{:S(2)}) collective-permute-start(bf16[16,6272]{1,0:T(8,128)(2,1)S(1)} %collective-permute-done.refs_1_), channel_id=1, source_target_pairs={{0,1},{1,0},{2,3},{3,2},{4,5},{5,4},{6,7},{7,6},{8,9},{9,8},{10,11... | collective-permute-start | bytes 602120 | tf_op jit(solution)/shard_map/ppermute | solution.py:418
  16.9 19.0 %collective-permute-start.4 = (bf16[16,6272]{1,0:T(8,128)(2,1)S(1)}, bf16[16,6272]{1,0:T(8,128)(2,1)S(1)}, u32[]{:S(2)}, u32[]{:S(2)}) collective-permute-start(bf16[16,6272]{1,0:T(8,128)(2,1)S(1)} %bitcast.15), channel_id=1, source_target_pairs={{0,1},{1,0},{2,3},{3,2},{4,5},{5,4},{6,7},{7,6},{8,9},{9,8},{10,11... | collective-permute-start | bytes 602120 | tf_op jit(solution)/shard_map/ppermute | solution.py:418
  23.0 12.9 %collective-permute-start.5 = (bf16[16,6272]{1,0:T(8,128)(2,1)S(1)}, bf16[16,6272]{1,0:T(8,128)(2,1)S(1)}, u32[]{:S(2)}, u32[]{:S(2)}) collective-permute-start(bf16[16,6272]{1,0:T(8,128)(2,1)S(1)} %collective-permute-done.3.refs_1_), channel_id=1, source_target_pairs={{0,1},{1,0},{2,3},{3,2},{4,5},{5,4},{6,7},{7,6},{8,9},{9,8},{10,11... | collective-permute-start | bytes 602120 | tf_op jit(solution)/shard_map/ppermute | solution.py:418
  47.2 20.3 %collective-permute-start.7 = (bf16[2816,128]{1,0:T(8,128)(2,1)S(1)}, bf16[2816,128]{1,0:T(8,128)(2,1)S(1)}, u32[]{:S(2)}, u32[]{:S(2)}) collective-permute-start(bf16[2816,128]{1,0:T(8,128)(2,1)S(1)} %slice.93), channel_id=1, source_target_pairs={{0,8},{4,12},{8,0},{12,4},{16,24},{20,28},{24,16},{28,20},{1,9},{5... | collective-permute-start | bytes 2162696 | tf_op jit(solution)/shard_map/ppermute | solution.py:418
  50.1 18.8 %collective-permute-start.9 = (bf16[2816,128]{1,0:T(8,128)(2,1)S(1)}, bf16[2816,128]{1,0:T(8,128)(2,1)S(1)}, u32[]{:S(2)}, u32[]{:S(2)}) collective-permute-start(bf16[2816,128]{1,0:T(8,128)(2,1)S(1)} %slice.72), channel_id=1, source_target_pairs={{0,16},{4,20},{8,24},{12,28},{16,0},{20,4},{24,8},{28,12},{1,17},{... | collective-permute-start | bytes 2162696 | tf_op jit(solution)/shard_map/ppermute | solution.py:418
  69.1 11.1 %collective-permute-start.12 = (bf16[32,6272]{1,0:T(8,128)(2,1)S(1)}, bf16[32,6272]{1,0:T(8,128)(2,1)S(1)}, u32[]{:S(2)}, u32[]{:S(2)}) collective-permute-start(bf16[32,6272]{1,0:T(8,128)(2,1)S(1)} %get-tuple-element.108), channel_id=1, source_target_pairs={{0,1},{1,0},{2,3},{3,2},{4,5},{5,4},{6,7},{7,6},{8,9},{9,8},{10,11... | collective-permute-start | bytes 1204232 | tf_op jit(solution)/shard_map/ppermute | solution.py:418
  69.4 10.8 %collective-permute-start.11 = (bf16[1408,128]{1,0:T(8,128)(2,1)S(1)}, bf16[1408,128]{1,0:T(8,128)(2,1)S(1)}, u32[]{:S(2)}, u32[]{:S(2)}) collective-permute-start(bf16[1408,128]{1,0:T(8,128)(2,1)S(1)} %slice.96), channel_id=1, source_target_pairs={{0,8},{4,12},{8,0},{12,4},{16,24},{20,28},{24,16},{28,20},{1,9},{5... | collective-permute-start | bytes 1081352 | tf_op jit(solution)/shard_map/ppermute | solution.py:418
  71.2 9.6 %collective-permute-start.10 = (bf16[1408,128]{1,0:T(8,128)(2,1)S(1)}, bf16[1408,128]{1,0:T(8,128)(2,1)S(1)}, u32[]{:S(2)}, u32[]{:S(2)}) collective-permute-start(bf16[1408,128]{1,0:T(8,128)(2,1)S(1)} %slice.95), channel_id=1, source_target_pairs={{0,16},{4,20},{8,24},{12,28},{16,0},{20,4},{24,8},{28,12},{1,17},{... | collective-permute-start | bytes 1081352 | tf_op jit(solution)/shard_map/ppermute | solution.py:418
  80.9 7.8 %collective-permute-start.13 = (bf16[704,128]{1,0:T(8,128)(2,1)S(1)}, bf16[704,128]{1,0:T(8,128)(2,1)S(1)}, u32[]{:S(2)}, u32[]{:S(2)}) collective-permute-start(bf16[704,128]{1,0:T(8,128)(2,1)S(1)} %slice.98), channel_id=1, source_target_pairs={{0,1},{1,0},{2,3},{3,2},{4,5},{5,4},{6,7},{7,6},{8,9},{9,8},{10,11... | collective-permute-start | bytes 540680 | tf_op jit(solution)/shard_map/ppermute | solution.py:418
  82.8 12.0 %collective-permute-start.18 = (bf16[704,128]{1,0:T(8,128)(2,1)S(1)}, bf16[704,128]{1,0:T(8,128)(2,1)S(1)}, u32[]{:S(2)}, u32[]{:S(2)}) collective-permute-start(bf16[704,128]{1,0:T(8,128)(2,1)S(1)} %slice.103), channel_id=1, source_target_pairs={{0,2},{1,3},{2,0},{3,1},{4,6},{5,7},{6,4},{7,5},{8,10},{9,11},{10,... | collective-permute-start | bytes 540680 | tf_op jit(solution)/shard_map/ppermute | solution.py:418
  88.8 7.0 %collective-permute-start.14 = (bf16[352,128]{1,0:T(8,128)(2,1)S(1)}, bf16[352,128]{1,0:T(8,128)(2,1)S(1)}, u32[]{:S(2)}, u32[]{:S(2)}) collective-permute-start(bf16[352,128]{1,0:T(8,128)(2,1)S(1)} %slice.100), channel_id=1, source_target_pairs={{0,2},{1,3},{2,0},{3,1},{4,6},{5,7},{6,4},{7,5},{8,10},{9,11},{10,... | collective-permute-start | bytes 270344 | tf_op jit(solution)/shard_map/ppermute | solution.py:418
  95.8 6.6 %collective-permute-start.15 = (bf16[352,128]{1,0:T(8,128)(2,1)S(1)}, bf16[352,128]{1,0:T(8,128)(2,1)S(1)}, u32[]{:S(2)}, u32[]{:S(2)}) collective-permute-start(bf16[352,128]{1,0:T(8,128)(2,1)S(1)} %get-tuple-element.131), channel_id=1, source_target_pairs={{0,2},{1,3},{2,0},{3,1},{4,6},{5,7},{6,4},{7,5},{8,10},{9,11},{10,... | collective-permute-start | bytes 270344 | tf_op jit(solution)/shard_map/ppermute | solution.py:418
  99.8 6.9 %collective-permute-start.20 = (bf16[352,128]{1,0:T(8,128)(2,1)S(1)}, bf16[352,128]{1,0:T(8,128)(2,1)S(1)}, u32[]{:S(2)}, u32[]{:S(2)}) collective-permute-start(bf16[352,128]{1,0:T(8,128)(2,1)S(1)} %get-tuple-element.129), channel_id=1, source_target_pairs={{0,1},{1,0},{2,3},{3,2},{4,5},{5,4},{6,7},{7,6},{8,9},{9,8},{10,11... | collective-permute-start | bytes 270344 | tf_op jit(solution)/shard_map/ppermute | solution.py:418
  102.4 8.7 %collective-permute-start.16 = (bf16[704,128]{1,0:T(8,128)(2,1)S(1)}, bf16[704,128]{1,0:T(8,128)(2,1)S(1)}, u32[]{:S(2)}, u32[]{:S(2)}) collective-permute-start(bf16[704,128]{1,0:T(8,128)(2,1)S(1)} %pad_maximum_fusion.5), channel_id=1, source_target_pairs={{0,1},{1,0},{2,3},{3,2},{4,5},{5,4},{6,7},{7,6},{8,9},{9,8},{10,11... | collective-permute-start | bytes 540680 | tf_op jit(solution)/shard_map/ppermute | solution.py:418
  106.7 8.5 %collective-permute-start.24 = (bf16[704,128]{1,0:T(8,128)(2,1)S(1)}, bf16[704,128]{1,0:T(8,128)(2,1)S(1)}, u32[]{:S(2)}, u32[]{:S(2)}) collective-permute-start(bf16[704,128]{1,0:T(8,128)(2,1)S(1)} %pad_maximum_fusion.6), channel_id=1, source_target_pairs={{0,2},{1,3},{2,0},{3,1},{4,6},{5,7},{6,4},{7,5},{8,10},{9,11},{10,... | collective-permute-start | bytes 540680 | tf_op jit(solution)/shard_map/ppermute | solution.py:418
  107.2 11.5 %collective-permute-start.21 = (bf16[32,6272]{1,0:T(8,128)(2,1)S(1)}, bf16[32,6272]{1,0:T(8,128)(2,1)S(1)}, u32[]{:S(2)}, u32[]{:S(2)}) collective-permute-start(bf16[32,6272]{1,0:T(8,128)(2,1)S(1)} %get-tuple-element.115), channel_id=1, source_target_pairs={{0,1},{1,0},{2,3},{3,2},{4,5},{5,4},{6,7},{7,6},{8,9},{9,8},{10,11... | collective-permute-start | bytes 1204232 | tf_op jit(solution)/shard_map/ppermute | solution.py:418
  111.2 7.8 %collective-permute-start.17 = (bf16[1408,128]{1,0:T(8,128)(2,1)S(1)}, bf16[1408,128]{1,0:T(8,128)(2,1)S(1)}, u32[]{:S(2)}, u32[]{:S(2)}) collective-permute-start(bf16[1408,128]{1,0:T(8,128)(2,1)S(1)} %pad_maximum_fusion.3), channel_id=1, source_target_pairs={{0,16},{4,20},{8,24},{12,28},{16,0},{20,4},{24,8},{28,12},{1,17},{... | collective-permute-start | bytes 1081352 | tf_op jit(solution)/shard_map/ppermute | solution.py:418
  115.2 8.9 %collective-permute-start.25 = (bf16[1408,128]{1,0:T(8,128)(2,1)S(1)}, bf16[1408,128]{1,0:T(8,128)(2,1)S(1)}, u32[]{:S(2)}, u32[]{:S(2)}) collective-permute-start(bf16[1408,128]{1,0:T(8,128)(2,1)S(1)} %pad_maximum_fusion.4), channel_id=1, source_target_pairs={{0,8},{4,12},{8,0},{12,4},{16,24},{20,28},{24,16},{28,20},{1,9},{5... | collective-permute-start | bytes 1081352 | tf_op jit(solution)/shard_map/ppermute | solution.py:418
  119.1 19.3 %collective-permute-start.22 = (bf16[32,6272]{1,0:T(8,128)(2,1)S(1)}, bf16[32,6272]{1,0:T(8,128)(2,1)S(1)}, u32[]{:S(2)}, u32[]{:S(2)}) collective-permute-start(bf16[32,6272]{1,0:T(8,128)(2,1)S(1)} %pad_maximum_fusion.2), channel_id=1, source_target_pairs={{0,2},{1,3},{2,0},{3,1},{4,6},{5,7},{6,4},{7,5},{8,10},{9,11},{10,... | collective-permute-start | bytes 1204232 | tf_op jit(solution)/shard_map/ppermute | solution.py:418
  124.2 11.5 %collective-permute-start.26 = (bf16[2816,128]{1,0:T(8,128)(2,1)S(1)}, bf16[2816,128]{1,0:T(8,128)(2,1)S(1)}, u32[]{:S(2)}, u32[]{:S(2)}) collective-permute-start(bf16[2816,128]{1,0:T(8,128)(2,1)S(1)} %pad_maximum_fusion.1), channel_id=1, source_target_pairs={{0,16},{4,20},{8,24},{12,28},{16,0},{20,4},{24,8},{28,12},{1,17},{... | collective-permute-start | bytes 2162696 | tf_op jit(solution)/shard_map/ppermute | solution.py:418
  126.5 11.7 %collective-permute-start.23 = (bf16[2816,128]{1,0:T(8,128)(2,1)S(1)}, bf16[2816,128]{1,0:T(8,128)(2,1)S(1)}, u32[]{:S(2)}, u32[]{:S(2)}) collective-permute-start(bf16[2816,128]{1,0:T(8,128)(2,1)S(1)} %pad_maximum_fusion), channel_id=1, source_target_pairs={{0,8},{4,12},{8,0},{12,4},{16,24},{20,28},{24,16},{28,20},{1,9},{5... | collective-permute-start | bytes 2162696 | tf_op jit(solution)/shard_map/ppermute | solution.py:418
  (18 other events, 86.3 us)

commit v5 on v4

--- a/solution.py
+++ b/solution.py
@@ -529,8 +529,8 @@
     )
 
     dp_bits = bits_of("dp")
-    stages_a = dp_bits + bits_of("graph")
-    stages_b = dp_bits[:1] + dp_bits[1:][::-1] + bits_of("graph")[::-1]
+    stages_a = dp_bits + bits_of("graph")[::-1]
+    stages_b = dp_bits[:1] + dp_bits[1:][::-1] + bits_of("graph")
     blocks = lax.axis_size("dp") * lax.axis_size("graph")
     rows_two = 2 * two * two * width
     rows_one = one * one * width

time: 145 us -> 146 us (level)
  waiting for transfers between devices: 55.6 us -> 47.8 us
  starting transfers between devices: 34.8 us -> 42.3 us
    ppermute x29, waiting for transfers between devices: 55.6 us -> 47.8 us  [exchange(): return lax.ppermute(value, axis, [(i, i ^ bit) for i in range(count)])]
    ppermute x29, starting transfers between devices: 34.8 us -> 42.3 us  [exchange(): return lax.ppermute(value, axis, [(i, i ^ bit) for i in range(count)])]
  transfers between devices with their start and end apart: 29 -> 29, of which waited for: 17 -> 19; matrix products, arithmetic and copies ran while one was open for 2% -> 2% of each run, Pallas kernels for 22% -> 22%
where the time goes in v5:
time: 146 us; the launch traced here: 145 us
  waiting for transfers between devices  47.8 us (33%)
  starting transfers between devices  42.3 us (29%)
  Pallas kernels  42.1 us (29%)
  local copies, waits for them, and re-layouts  7.52 us (5%)
  other arithmetic  2.94 us (2%)
  between operations  1.9 us (1%)
    ppermute x29, waiting for transfers between devices, exchange(): return lax.ppermute(value, axis, [(i, i ^ bit) for i in range(count)])  47.8 us
    ppermute x29, starting transfers between devices, exchange(): return lax.ppermute(value, axis, [(i, i ^ bit) for i in range(count)])  42.3 us
    pallas_call x9, Pallas kernels, call(): pl.pallas_call(kernel, out_shape=out_shape, in_specs=[SMEM] * smem + [ANY...  42.1 us
    unnamed x32, local copies, waits for them, and re-layouts  7.1 us
  transfers between devices with their start and end apart: 29, of which 19 were waited for; matrix products, arithmetic and copies ran while one was open for 2% of the time, Pallas kernels for 22%

profile of v5, /device:TPU:0, one launch (start us, length us, event | category | flops | bytes accessed | tf_op | source)
XLA Modules:
  0.0 144.6 jit_solution(1199329052815624500)
XLA Ops:
  0.6 4.1 %collective-permute-start = (bf16[16,6272]{1,0:T(8,128)(2,1)}, bf16[16,6272]{1,0:T(8,128)(2,1)S(1)}, u32[]{:S(2)}, u32[]{:S(2)}) collective-permute-start(bf16[16,6272]{1,0:T(8,128)(2,1)} %bitcast.18), channel_id=1, source_target_pairs={{0,2},{1,3},{2,0},{3,1},{4,6},{5,7},{6,4},{7,5},{8,10},{9,11},{10,... | collective-permute-start | bytes 602120 | tf_op jit(solution)/shard_map/ppermute | solution.py:418
  13.5 2.5 %shard_map.154 = (f32[49,29,512]{2,1,0:T(8,128)S(1)}, f32[128,512]{1,0:T(8,128)S(1)}, bf16[896,896]{1,0:T(8,128)(2,1)S(1)}, bf16[2,768,768]{2,1,0:T(8,128)(2,1)S(1)}, bf16[2,640,640]{2,1,0:T(8,128)(2,1)S(1)}) custom-call(bf16[49,29,512]{2,1,0:T(8,128)(2,1)S(1)} %bitcast.13, bf16[896,896]{1,0:T(8,128)(2,1)S(1)} %copy-done.5, ...), custom_call_target="tpu_custom_call" | custom-call | bytes 15421440 | tf_op jit(solution)/shard_map/pallas_call | solution.py:398
  18.9 4.1 %collective-permute-done.3.refs_1_ = bf16[16,6272]{1,0:T(8,128)(2,1)S(1)} collective-permute-done((bf16[16,6272]{1,0:T(8,128)(2,1)}, bf16[16,6272]{1,0:T(8,128)(2,1)S(1)}, u32[]{:S(2)}, u32[]{:S(2)}) %collective-permute-start.3) | collective-permute-done | bytes 200736 | tf_op jit(solution)/shard_map/ppermute | solution.py:418
  23.7 3.4 %collective-permute-done.2.refs_3_ = bf16[16,6272]{1,0:T(8,128)(2,1)S(1)} collective-permute-done((bf16[16,6272]{1,0:T(8,128)(2,1)S(1)}, bf16[16,6272]{1,0:T(8,128)(2,1)S(1)}, u32[]{:S(2)}, u32[]{:S(2)}) %collective-permute-start.2) | collective-permute-done | bytes 200736 | tf_op jit(solution)/shard_map/ppermute | solution.py:418
  27.2 3.1 %shard_map.155 = (bf16[896,512]{1,0:T(8,128)(2,1)S(1)}, bf16[1536,512]{1,0:T(8,128)(2,1)S(1)}, bf16[1280,512]{1,0:T(8,128)(2,1)S(1)}, f32[128,512]{1,0:T(8,128)S(1)}, f32[128,512]{1,0:T(8,128)S(1)}) custom-call(s32[1,512]{1,0:T(1,128)S(1)} %copy-done.12, f32[49,29,512]{2,1,0:T(8,128)S(1)} %get-tuple-element.72.wide, f32[128,512]{1,0:T(8,128)S(1)} %get-tuple-element.73.scale, ...), custom_call_target="tpu_custom_call" | custom-call | flops 2055208960 | bytes 7602176 | tf_op jit(solution)/shard_map/pallas_call | solution.py:398
  30.3 5.6 %shard_map.156 = (bf16[896,512]{1,0:T(8,128)(2,1)S(1)}, bf16[1536,512]{1,0:T(8,128)(2,1)S(1)}, bf16[1280,512]{1,0:T(8,128)(2,1)S(1)}, bf16[7,128,2560]{2,1,0:T(8,128)(2,1)S(1)}) custom-call(bf16[896,512]{1,0:T(8,128)(2,1)S(1)} %get-tuple-element.81.x_zero, bf16[1536,512]{1,0:T(8,128)(2,1)S(1)} %get-tuple-element.82.x_one, ...), custom_call_target="tpu_custom_call" | custom-call | flops 4915724288 | bytes 11403264 | tf_op jit(solution)/shard_map/pallas_call | solution.py:398
  35.9 3.5 %shard_map.157 = (bf16[896,512]{1,0:T(8,128)(2,1)S(1)}, bf16[1536,512]{1,0:T(8,128)(2,1)S(1)}, bf16[1280,512]{1,0:T(8,128)(2,1)S(1)}, bf16[128,512]{1,0:T(8,128)(2,1)S(1)}) custom-call(s32[1]{0:T(128)} %bitcast.11.live, s32[1,512]{1,0:T(1,128)S(1)} %copy-done.10, f32[49,29,512]{2,1,0:T(8,128)S(1)} %get-tuple-element.72.wide, ...), custom_call_target="tpu_custom_call" | custom-call | flops 2055208960 | bytes 7602176 | tf_op jit(solution)/shard_map/pallas_call | solution.py:398
  39.5 4.0 %shard_map.158 = (bf16[5632,128]{1,0:T(8,128)(2,1)S(1)}, bf16[5632,128]{1,0:T(8,128)(2,1)S(1)}) custom-call(bf16[1280,512]{1,0:T(8,128)(2,1)S(1)} %get-tuple-element.76.x_two, bf16[1280,512]{1,0:T(8,128)(2,1)S(1)} %get-tuple-element.90.g_two, bf16[1536,512]{1,0:T(8,128)(2,1)S(1)} %get-tuple-element.82.x_one, bf16[1536,512]{1,0:T(8,128)(2,1)S(1)} %get-tuple-element.91.g_one), custom_call_target="tpu_custom_call" | custom-call | flops 2457862144 | bytes 5767168 | tf_op jit(solution)/shard_map/pallas_call | solution.py:398
  43.5 2.7 %shard_map.159 = (bf16[5632,128]{1,0:T(8,128)(2,1)S(1)}, bf16[5632,128]{1,0:T(8,128)(2,1)S(1)}) custom-call(bf16[1536,512]{1,0:T(8,128)(2,1)S(1)} %get-tuple-element.82.x_one, bf16[1536,512]{1,0:T(8,128)(2,1)S(1)} %get-tuple-element.91.g_one, bf16[896,512]{1,0:T(8,128)(2,1)S(1)} %get-tuple-element.81.x_zero, bf16[896,512]{1,0:T(8,128)(2,1)S(1)} %get-tuple-element.94.g_zero, ...), custom_call_target="tpu_custom_call" | custom-call | flops 2457862144 | bytes 5767168 | tf_op jit(solution)/shard_map/pallas_call | solution.py:398
  52.3 15.2 %shard_map.160 = (bf16[32,6272]{1,0:T(8,128)(2,1)S(1)}, bf16[32,6272]{1,0:T(8,128)(2,1)S(1)}, bf16[32,6272]{1,0:T(8,128)(2,1)S(1)}, bf16[32,6272]{1,0:T(8,128)(2,1)S(1)}) custom-call(s32[1]{0:T(128)} %bitcast.12.live, bf16[896,896]{1,0:T(8,128)(2,1)S(1)} %copy-done.6, bf16[2,768,768]{2,1,0:T(8,128)(2,1)S(1)} %copy-done.1, ...), custom_call_target="tpu_custom_call" | custom-call | flops 9026142208 | bytes 15204352 | tf_op jit(solution)/shard_map/pallas_call | solution.py:398
  72.7 7.5 %collective-permute-done.12 = bf16[32,6272]{1,0:T(8,128)(2,1)S(1)} collective-permute-done((bf16[32,6272]{1,0:T(8,128)(2,1)S(1)}, bf16[32,6272]{1,0:T(8,128)(2,1)S(1)}, u32[]{:S(2)}, u32[]{:S(2)}) %collective-permute-start.12) | collective-permute-done | bytes 401440 | tf_op jit(solution)/shard_map/ppermute | solution.py:418
  80.9 3.0 %collective-permute-start.13 = (bf16[704,128]{1,0:T(8,128)(2,1)S(1)}, bf16[704,128]{1,0:T(8,128)(2,1)S(1)}, u32[]{:S(2)}, u32[]{:S(2)}) collective-permute-start(bf16[704,128]{1,0:T(8,128)(2,1)S(1)} %slice.98), channel_id=1, source_target_pairs={{0,2},{1,3},{2,0},{3,1},{4,6},{5,7},{6,4},{7,5},{8,10},{9,11},{10,... | collective-permute-start | bytes 540680 | tf_op jit(solution)/shard_map/ppermute | solution.py:418
  84.4 6.3 %collective-permute-done.13 = bf16[704,128]{1,0:T(8,128)(2,1)S(1)} collective-permute-done((bf16[704,128]{1,0:T(8,128)(2,1)S(1)}, bf16[704,128]{1,0:T(8,128)(2,1)S(1)}, u32[]{:S(2)}, u32[]{:S(2)}) %collective-permute-start.13) | collective-permute-done | bytes 180256 | tf_op jit(solution)/shard_map/ppermute | solution.py:418
  91.3 2.7 %collective-permute-start.19 = (bf16[352,128]{1,0:T(8,128)(2,1)S(1)}, bf16[352,128]{1,0:T(8,128)(2,1)S(1)}, u32[]{:S(2)}, u32[]{:S(2)}) collective-permute-start(bf16[352,128]{1,0:T(8,128)(2,1)S(1)} %slice.105), channel_id=1, source_target_pairs={{0,2},{1,3},{2,0},{3,1},{4,6},{5,7},{6,4},{7,5},{8,10},{9,11},{10,... | collective-permute-start | bytes 270344 | tf_op jit(solution)/shard_map/ppermute | solution.py:418
  97.3 2.8 %collective-permute-start.20 = (bf16[352,128]{1,0:T(8,128)(2,1)S(1)}, bf16[352,128]{1,0:T(8,128)(2,1)S(1)}, u32[]{:S(2)}, u32[]{:S(2)}) collective-permute-start(bf16[352,128]{1,0:T(8,128)(2,1)S(1)} %get-tuple-element.129), channel_id=1, source_target_pairs={{0,2},{1,3},{2,0},{3,1},{4,6},{5,7},{6,4},{7,5},{8,10},{9,11},{10,... | collective-permute-start | bytes 270344 | tf_op jit(solution)/shard_map/ppermute | solution.py:418
  100.4 3.2 %collective-permute-start.16 = (bf16[704,128]{1,0:T(8,128)(2,1)S(1)}, bf16[704,128]{1,0:T(8,128)(2,1)S(1)}, u32[]{:S(2)}, u32[]{:S(2)}) collective-permute-start(bf16[704,128]{1,0:T(8,128)(2,1)S(1)} %pad_maximum_fusion.5), channel_id=1, source_target_pairs={{0,2},{1,3},{2,0},{3,1},{4,6},{5,7},{6,4},{7,5},{8,10},{9,11},{10,... | collective-permute-start | bytes 540680 | tf_op jit(solution)/shard_map/ppermute | solution.py:418
  103.6 2.7 %collective-permute-done.20 = bf16[352,128]{1,0:T(8,128)(2,1)S(1)} collective-permute-done((bf16[352,128]{1,0:T(8,128)(2,1)S(1)}, bf16[352,128]{1,0:T(8,128)(2,1)S(1)}, u32[]{:S(2)}, u32[]{:S(2)}) %collective-permute-start.20) | collective-permute-done | bytes 90144 | tf_op jit(solution)/shard_map/ppermute | solution.py:418
  112.1 2.5 %collective-permute-done.24 = bf16[704,128]{1,0:T(8,128)(2,1)S(1)} collective-permute-done((bf16[704,128]{1,0:T(8,128)(2,1)S(1)}, bf16[704,128]{1,0:T(8,128)(2,1)S(1)}, u32[]{:S(2)}, u32[]{:S(2)}) %collective-permute-start.24) | collective-permute-done | bytes 180256 | tf_op jit(solution)/shard_map/ppermute | solution.py:418
  114.6 2.4 %collective-permute-start.25 = (bf16[1408,128]{1,0:T(8,128)(2,1)S(1)}, bf16[1408,128]{1,0:T(8,128)(2,1)S(1)}, u32[]{:S(2)}, u32[]{:S(2)}) collective-permute-start(bf16[1408,128]{1,0:T(8,128)(2,1)S(1)} %pad_maximum_fusion.4), channel_id=1, source_target_pairs={{0,8},{4,12},{8,0},{12,4},{16,24},{20,28},{24,16},{28,20},{1,9},{5... | collective-permute-start | bytes 1081352 | tf_op jit(solution)/shard_map/ppermute | solution.py:418
  120.2 2.5 %collective-permute-done.25 = bf16[1408,128]{1,0:T(8,128)(2,1)S(1)} collective-permute-done((bf16[1408,128]{1,0:T(8,128)(2,1)S(1)}, bf16[1408,128]{1,0:T(8,128)(2,1)S(1)}, u32[]{:S(2)}, u32[]{:S(2)}) %collective-permute-start.25) | collective-permute-done | bytes 360480 | tf_op jit(solution)/shard_map/ppermute | solution.py:418
  122.7 3.1 %collective-permute-start.26 = (bf16[2816,128]{1,0:T(8,128)(2,1)S(1)}, bf16[2816,128]{1,0:T(8,128)(2,1)S(1)}, u32[]{:S(2)}, u32[]{:S(2)}) collective-permute-start(bf16[2816,128]{1,0:T(8,128)(2,1)S(1)} %pad_maximum_fusion.1), channel_id=1, source_target_pairs={{0,16},{4,20},{8,24},{12,28},{16,0},{20,4},{24,8},{28,12},{1,17},{... | collective-permute-start | bytes 2162696 | tf_op jit(solution)/shard_map/ppermute | solution.py:418
  128.4 7.5 %collective-permute-done.26 = bf16[2816,128]{1,0:T(8,128)(2,1)S(1)} collective-permute-done((bf16[2816,128]{1,0:T(8,128)(2,1)S(1)}, bf16[2816,128]{1,0:T(8,128)(2,1)S(1)}, u32[]{:S(2)}, u32[]{:S(2)}) %collective-permute-start.26) | collective-permute-done | bytes 720928 | tf_op jit(solution)/shard_map/ppermute | solution.py:418
  138.9 2.8 %shard_map.161 = (f32[2,640,640]{2,1,0:T(8,128)}, f32[2,768,768]{2,1,0:T(8,128)}, f32[896,896]{1,0:T(8,128)}, f32[128,128]{1,0:T(8,128)}) custom-call(bf16[5632,128]{1,0:T(8,128)(2,1)S(1)} %constant_dynamic-update-slice_fusion.refs_0_, bf16[5632,128]{1,0:T(8,128)(2,1)S(1)} %constant_dynamic-update-slice_fusion.5.refs_1_), custom_call_target="tpu_custom_call" | custom-call | bytes 8650752 | tf_op jit(solution)/shard_map/pallas_call | solution.py:398
  141.7 2.7 %shard_map.162 = (f32[2,640,640]{2,1,0:T(8,128)}, f32[2,768,768]{2,1,0:T(8,128)}, f32[896,896]{1,0:T(8,128)}, f32[128,128]{1,0:T(8,128)}) custom-call(f32[2,640,640]{2,1,0:T(8,128)} %get-tuple-element.120.refs_0_, f32[2,768,768]{2,1,0:T(8,128)} %get-tuple-element.121.refs_1_, ...), custom_call_target="tpu_custom_call", output_to_operand_aliasing={{0}: (0, {}), {1}: (1, {}), {2}: (2, {}), {3}: (3, {})} | custom-call | bytes 8650752 | tf_op jit(solution)/shard_map/pallas_call | solution.py:398
  (108 shorter events, 42.7 us)
Async XLA Ops:
  0.6 15.4 %collective-permute-start = (bf16[16,6272]{1,0:T(8,128)(2,1)}, bf16[16,6272]{1,0:T(8,128)(2,1)S(1)}, u32[]{:S(2)}, u32[]{:S(2)}) collective-permute-start(bf16[16,6272]{1,0:T(8,128)(2,1)} %bitcast.18), channel_id=1, source_target_pairs={{0,2},{1,3},{2,0},{3,1},{4,6},{5,7},{6,4},{7,5},{8,10},{9,11},{10,... | collective-permute-start | bytes 602120 | tf_op jit(solution)/shard_map/ppermute | solution.py:418
  4.7 19.0 %collective-permute-start.1 = (bf16[16,6272]{1,0:T(8,128)(2,1)}, bf16[16,6272]{1,0:T(8,128)(2,1)S(1)}, u32[]{:S(2)}, u32[]{:S(2)}) collective-permute-start(bf16[16,6272]{1,0:T(8,128)(2,1)} %bitcast.19), channel_id=1, source_target_pairs={{0,1},{1,0},{2,3},{3,2},{4,5},{5,4},{6,7},{7,6},{8,9},{9,8},{10,11... | collective-permute-start | bytes 602120 | tf_op jit(solution)/shard_map/ppermute | solution.py:418
  6.3 16.7 %collective-permute-start.3 = (bf16[16,6272]{1,0:T(8,128)(2,1)}, bf16[16,6272]{1,0:T(8,128)(2,1)S(1)}, u32[]{:S(2)}, u32[]{:S(2)}) collective-permute-start(bf16[16,6272]{1,0:T(8,128)(2,1)} %bitcast.14), channel_id=1, source_target_pairs={{0,2},{1,3},{2,0},{3,1},{4,6},{5,7},{6,4},{7,5},{8,10},{9,11},{10,... | collective-permute-start | bytes 602120 | tf_op jit(solution)/shard_map/ppermute | solution.py:418
  16.0 11.1 %collective-permute-start.2 = (bf16[16,6272]{1,0:T(8,128)(2,1)S(1)}, bf16[16,6272]{1,0:T(8,128)(2,1)S(1)}, u32[]{:S(2)}, u32[]{:S(2)}) collective-permute-start(bf16[16,6272]{1,0:T(8,128)(2,1)S(1)} %collective-permute-done.refs_1_), channel_id=1, source_target_pairs={{0,1},{1,0},{2,3},{3,2},{4,5},{5,4},{6,7},{7,6},{8,9},{9,8},{10,11... | collective-permute-start | bytes 602120 | tf_op jit(solution)/shard_map/ppermute | solution.py:418
  16.9 19.0 %collective-permute-start.4 = (bf16[16,6272]{1,0:T(8,128)(2,1)S(1)}, bf16[16,6272]{1,0:T(8,128)(2,1)S(1)}, u32[]{:S(2)}, u32[]{:S(2)}) collective-permute-start(bf16[16,6272]{1,0:T(8,128)(2,1)S(1)} %bitcast.15), channel_id=1, source_target_pairs={{0,1},{1,0},{2,3},{3,2},{4,5},{5,4},{6,7},{7,6},{8,9},{9,8},{10,11... | collective-permute-start | bytes 602120 | tf_op jit(solution)/shard_map/ppermute | solution.py:418
  23.0 12.9 %collective-permute-start.5 = (bf16[16,6272]{1,0:T(8,128)(2,1)S(1)}, bf16[16,6272]{1,0:T(8,128)(2,1)S(1)}, u32[]{:S(2)}, u32[]{:S(2)}) collective-permute-start(bf16[16,6272]{1,0:T(8,128)(2,1)S(1)} %collective-permute-done.3.refs_1_), channel_id=1, source_target_pairs={{0,1},{1,0},{2,3},{3,2},{4,5},{5,4},{6,7},{7,6},{8,9},{9,8},{10,11... | collective-permute-start | bytes 602120 | tf_op jit(solution)/shard_map/ppermute | solution.py:418
  47.2 20.3 %collective-permute-start.7 = (bf16[2816,128]{1,0:T(8,128)(2,1)S(1)}, bf16[2816,128]{1,0:T(8,128)(2,1)S(1)}, u32[]{:S(2)}, u32[]{:S(2)}) collective-permute-start(bf16[2816,128]{1,0:T(8,128)(2,1)S(1)} %slice.93), channel_id=1, source_target_pairs={{0,8},{4,12},{8,0},{12,4},{16,24},{20,28},{24,16},{28,20},{1,9},{5... | collective-permute-start | bytes 2162696 | tf_op jit(solution)/shard_map/ppermute | solution.py:418
  50.1 18.8 %collective-permute-start.9 = (bf16[2816,128]{1,0:T(8,128)(2,1)S(1)}, bf16[2816,128]{1,0:T(8,128)(2,1)S(1)}, u32[]{:S(2)}, u32[]{:S(2)}) collective-permute-start(bf16[2816,128]{1,0:T(8,128)(2,1)S(1)} %slice.72), channel_id=1, source_target_pairs={{0,16},{4,20},{8,24},{12,28},{16,0},{20,4},{24,8},{28,12},{1,17},{... | collective-permute-start | bytes 2162696 | tf_op jit(solution)/shard_map/ppermute | solution.py:418
  69.1 11.1 %collective-permute-start.12 = (bf16[32,6272]{1,0:T(8,128)(2,1)S(1)}, bf16[32,6272]{1,0:T(8,128)(2,1)S(1)}, u32[]{:S(2)}, u32[]{:S(2)}) collective-permute-start(bf16[32,6272]{1,0:T(8,128)(2,1)S(1)} %get-tuple-element.108), channel_id=1, source_target_pairs={{0,1},{1,0},{2,3},{3,2},{4,5},{5,4},{6,7},{7,6},{8,9},{9,8},{10,11... | collective-permute-start | bytes 1204232 | tf_op jit(solution)/shard_map/ppermute | solution.py:418
  69.4 10.8 %collective-permute-start.11 = (bf16[1408,128]{1,0:T(8,128)(2,1)S(1)}, bf16[1408,128]{1,0:T(8,128)(2,1)S(1)}, u32[]{:S(2)}, u32[]{:S(2)}) collective-permute-start(bf16[1408,128]{1,0:T(8,128)(2,1)S(1)} %slice.96), channel_id=1, source_target_pairs={{0,8},{4,12},{8,0},{12,4},{16,24},{20,28},{24,16},{28,20},{1,9},{5... | collective-permute-start | bytes 1081352 | tf_op jit(solution)/shard_map/ppermute | solution.py:418
  71.2 9.6 %collective-permute-start.10 = (bf16[1408,128]{1,0:T(8,128)(2,1)S(1)}, bf16[1408,128]{1,0:T(8,128)(2,1)S(1)}, u32[]{:S(2)}, u32[]{:S(2)}) collective-permute-start(bf16[1408,128]{1,0:T(8,128)(2,1)S(1)} %slice.95), channel_id=1, source_target_pairs={{0,16},{4,20},{8,24},{12,28},{16,0},{20,4},{24,8},{28,12},{1,17},{... | collective-permute-start | bytes 1081352 | tf_op jit(solution)/shard_map/ppermute | solution.py:418
  80.9 9.8 %collective-permute-start.13 = (bf16[704,128]{1,0:T(8,128)(2,1)S(1)}, bf16[704,128]{1,0:T(8,128)(2,1)S(1)}, u32[]{:S(2)}, u32[]{:S(2)}) collective-permute-start(bf16[704,128]{1,0:T(8,128)(2,1)S(1)} %slice.98), channel_id=1, source_target_pairs={{0,2},{1,3},{2,0},{3,1},{4,6},{5,7},{6,4},{7,5},{8,10},{9,11},{10,... | collective-permute-start | bytes 540680 | tf_op jit(solution)/shard_map/ppermute | solution.py:418
  84.0 7.3 %collective-permute-start.18 = (bf16[704,128]{1,0:T(8,128)(2,1)S(1)}, bf16[704,128]{1,0:T(8,128)(2,1)S(1)}, u32[]{:S(2)}, u32[]{:S(2)}) collective-permute-start(bf16[704,128]{1,0:T(8,128)(2,1)S(1)} %slice.103), channel_id=1, source_target_pairs={{0,1},{1,0},{2,3},{3,2},{4,5},{5,4},{6,7},{7,6},{8,9},{9,8},{10,11... | collective-permute-start | bytes 540680 | tf_op jit(solution)/shard_map/ppermute | solution.py:418
  91.3 5.9 %collective-permute-start.19 = (bf16[352,128]{1,0:T(8,128)(2,1)S(1)}, bf16[352,128]{1,0:T(8,128)(2,1)S(1)}, u32[]{:S(2)}, u32[]{:S(2)}) collective-permute-start(bf16[352,128]{1,0:T(8,128)(2,1)S(1)} %slice.105), channel_id=1, source_target_pairs={{0,2},{1,3},{2,0},{3,1},{4,6},{5,7},{6,4},{7,5},{8,10},{9,11},{10,... | collective-permute-start | bytes 270344 | tf_op jit(solution)/shard_map/ppermute | solution.py:418
  97.3 8.9 %collective-permute-start.20 = (bf16[352,128]{1,0:T(8,128)(2,1)S(1)}, bf16[352,128]{1,0:T(8,128)(2,1)S(1)}, u32[]{:S(2)}, u32[]{:S(2)}) collective-permute-start(bf16[352,128]{1,0:T(8,128)(2,1)S(1)} %get-tuple-element.129), channel_id=1, source_target_pairs={{0,2},{1,3},{2,0},{3,1},{4,6},{5,7},{6,4},{7,5},{8,10},{9,11},{10,... | collective-permute-start | bytes 270344 | tf_op jit(solution)/shard_map/ppermute | solution.py:418
  100.4 10.3 %collective-permute-start.16 = (bf16[704,128]{1,0:T(8,128)(2,1)S(1)}, bf16[704,128]{1,0:T(8,128)(2,1)S(1)}, u32[]{:S(2)}, u32[]{:S(2)}) collective-permute-start(bf16[704,128]{1,0:T(8,128)(2,1)S(1)} %pad_maximum_fusion.5), channel_id=1, source_target_pairs={{0,2},{1,3},{2,0},{3,1},{4,6},{5,7},{6,4},{7,5},{8,10},{9,11},{10,... | collective-permute-start | bytes 540680 | tf_op jit(solution)/shard_map/ppermute | solution.py:418
  106.3 8.3 %collective-permute-start.24 = (bf16[704,128]{1,0:T(8,128)(2,1)S(1)}, bf16[704,128]{1,0:T(8,128)(2,1)S(1)}, u32[]{:S(2)}, u32[]{:S(2)}) collective-permute-start(bf16[704,128]{1,0:T(8,128)(2,1)S(1)} %pad_maximum_fusion.6), channel_id=1, source_target_pairs={{0,1},{1,0},{2,3},{3,2},{4,5},{5,4},{6,7},{7,6},{8,9},{9,8},{10,11... | collective-permute-start | bytes 540680 | tf_op jit(solution)/shard_map/ppermute | solution.py:418
  106.3 12.7 %collective-permute-start.21 = (bf16[32,6272]{1,0:T(8,128)(2,1)S(1)}, bf16[32,6272]{1,0:T(8,128)(2,1)S(1)}, u32[]{:S(2)}, u32[]{:S(2)}) collective-permute-start(bf16[32,6272]{1,0:T(8,128)(2,1)S(1)} %get-tuple-element.115), channel_id=1, source_target_pairs={{0,1},{1,0},{2,3},{3,2},{4,5},{5,4},{6,7},{7,6},{8,9},{9,8},{10,11... | collective-permute-start | bytes 1204232 | tf_op jit(solution)/shard_map/ppermute | solution.py:418
  110.7 8.7 %collective-permute-start.17 = (bf16[1408,128]{1,0:T(8,128)(2,1)S(1)}, bf16[1408,128]{1,0:T(8,128)(2,1)S(1)}, u32[]{:S(2)}, u32[]{:S(2)}) collective-permute-start(bf16[1408,128]{1,0:T(8,128)(2,1)S(1)} %pad_maximum_fusion.3), channel_id=1, source_target_pairs={{0,16},{4,20},{8,24},{12,28},{16,0},{20,4},{24,8},{28,12},{1,17},{... | collective-permute-start | bytes 1081352 | tf_op jit(solution)/shard_map/ppermute | solution.py:418
  114.6 8.1 %collective-permute-start.25 = (bf16[1408,128]{1,0:T(8,128)(2,1)S(1)}, bf16[1408,128]{1,0:T(8,128)(2,1)S(1)}, u32[]{:S(2)}, u32[]{:S(2)}) collective-permute-start(bf16[1408,128]{1,0:T(8,128)(2,1)S(1)} %pad_maximum_fusion.4), channel_id=1, source_target_pairs={{0,8},{4,12},{8,0},{12,4},{16,24},{20,28},{24,16},{28,20},{1,9},{5... | collective-permute-start | bytes 1081352 | tf_op jit(solution)/shard_map/ppermute | solution.py:418
  119.5 18.6 %collective-permute-start.22 = (bf16[32,6272]{1,0:T(8,128)(2,1)S(1)}, bf16[32,6272]{1,0:T(8,128)(2,1)S(1)}, u32[]{:S(2)}, u32[]{:S(2)}) collective-permute-start(bf16[32,6272]{1,0:T(8,128)(2,1)S(1)} %pad_maximum_fusion.2), channel_id=1, source_target_pairs={{0,2},{1,3},{2,0},{3,1},{4,6},{5,7},{6,4},{7,5},{8,10},{9,11},{10,... | collective-permute-start | bytes 1204232 | tf_op jit(solution)/shard_map/ppermute | solution.py:418
  122.7 13.2 %collective-permute-start.26 = (bf16[2816,128]{1,0:T(8,128)(2,1)S(1)}, bf16[2816,128]{1,0:T(8,128)(2,1)S(1)}, u32[]{:S(2)}, u32[]{:S(2)}) collective-permute-start(bf16[2816,128]{1,0:T(8,128)(2,1)S(1)} %pad_maximum_fusion.1), channel_id=1, source_target_pairs={{0,16},{4,20},{8,24},{12,28},{16,0},{20,4},{24,8},{28,12},{1,17},{... | collective-permute-start | bytes 2162696 | tf_op jit(solution)/shard_map/ppermute | solution.py:418
  125.9 12.0 %collective-permute-start.23 = (bf16[2816,128]{1,0:T(8,128)(2,1)S(1)}, bf16[2816,128]{1,0:T(8,128)(2,1)S(1)}, u32[]{:S(2)}, u32[]{:S(2)}) collective-permute-start(bf16[2816,128]{1,0:T(8,128)(2,1)S(1)} %pad_maximum_fusion), channel_id=1, source_target_pairs={{0,8},{4,12},{8,0},{12,4},{16,24},{20,28},{24,16},{28,20},{1,9},{5... | collective-permute-start | bytes 2162696 | tf_op jit(solution)/shard_map/ppermute | solution.py:418
  136.0 5.7 %collective-permute-start.28 = (bf16[5632,128]{1,0:T(8,128)(2,1)S(1)}, bf16[5632,128]{1,0:T(8,128)(2,1)S(1)}, u32[]{:S(2)}, u32[]{:S(2)}) collective-permute-start(bf16[5632,128]{1,0:T(8,128)(2,1)S(1)} %constant_dynamic-update-slice_fusion.5.refs_1_), channel_id=1, source_target_pairs={{0,4},{4,0},{8,12},{12,8},{16,20},{20,16},{24,28},{28,24},{1,5},{5... | collective-permute-start | bytes 4325384 | tf_op jit(solution)/shard_map/ppermute | solution.py:418
  (18 other events, 84.7 us)
